TPU v7x, 32 devices: a whole 2x2x4 slice. The times are simulated.
32 devices in a mesh: dp: 4 (over y, x), expert: 2 (over core), shard: 4 (over z).
Axes of the slice: x: 2, y: 2, z: 4, core: 2. Of those that a mesh axis runs over, the one named last changes fastest.
Arguments:
- output_gradient: bfloat16 [4096, 3072], P(('dp', 'expert', 'shard')), may hold values from -6 to 6
- saved_router_scores: float32 [4096, 8], P(('dp', 'expert', 'shard')), may hold values from -8 to 8
- expert_choice_index: int32 [4096, 2], P(('dp', 'expert', 'shard')), may hold values from 0 to 7, as said below
- router_matrix: bfloat16 [8, 3072], replicated, may hold values from -0.109375 to 0.109375
- weight_normalized_entries: bfloat16 [3072, 8192], P('shard', 'expert'), may hold values from -1 to 1
- scales: bfloat16 [48, 8192], P('shard', 'expert'), may hold values from 0.0099487305 to 0.099609375
- stored_hidden_state: bfloat16 [4, 4, 64, 8192], P('dp', 'shard', None, 'expert'), may hold values from -6 to 6
- context: bfloat16 [4096, 3072], P(('dp', 'expert', 'shard')), may hold values from -6 to 6
- adapter_down_factor: bfloat16 [64, 3072], replicated, may hold values from -0.109375 to 0.109375
- adapter_up_factor: bfloat16 [64, 3072], replicated, may hold values from -0.109375 to 0.109375
Outputs:
- hidden_grad: bfloat16 [4, 4, 64, 8192], P('dp', 'shard', None, 'expert')
- token_grad: bfloat16 [4096, 3072], P(('dp', 'expert', 'shard'))
- grad_down: float32 [64, 3072], P(None, 'shard')
- up_factor_gradient: float32 [64, 3072], P(None, 'shard')
Inputs may be any that keep to these rules, and one draw needn't show every extreme that they name: `expert_choice_index`: each token names two different experts and expert 0 at most once. The 128 tokens of one device block name expert 0 at most 32 times, and in every draw all device blocks of some pair of dp and shard indices name it exactly 32 times.
All inputs are finite; a program needn't handle non-finite values.
Results may differ from a plain program's by a relative error of at most 0.015.
Values may be sent and summed in bfloat16 or wider, within the bound.
No kernel may reach another device: no remote copies, remote signals or barrier semaphores. Data moves between devices by JAX's collectives and lax.ppermute only.
A program may use at most 128 MiB of HBM per device.

v0:
```python
import jax
import jax.numpy as jnp
from jax import lax
from jax.sharding import PartitionSpec as P

ADAPTER_SCALE = 0.25


def per_device(
    output_gradient,
    saved_router_scores,
    expert_choice_index,
    router_matrix,
    weight_normalized_entries,
    scales,
    stored_hidden_state,
    context,
    adapter_down_factor,
    adapter_up_factor,
):
    expert_count = lax.axis_size("expert")
    shard_count = lax.axis_size("shard")
    tokens, feature_width = output_gradient.shape
    experts = saved_router_scores.shape[1]
    row_count = stored_hidden_state.shape[2]
    capacity = row_count // expert_count
    ff_share = stored_hidden_state.shape[3]
    block_size = weight_normalized_entries.shape[0] // scales.shape[0]
    labels = jnp.arange(experts, dtype=jnp.int32)
    choose = expert_choice_index[:, :, None] == labels[None, None, :]
    chosen = jnp.sum(jnp.where(choose, saved_router_scores[:, None, :], 0.0), axis=2)
    first_prob = 1.0 / (1.0 + jnp.exp(chosen[:, 1] - chosen[:, 0]))
    second_prob = 1.0 - first_prob
    in_window = expert_choice_index == 0
    window_flag = jnp.any(in_window, axis=1)
    flag_int = window_flag.astype(jnp.int32)
    slot_index = jnp.cumsum(flag_int) - flag_int
    route_probs = jnp.stack([first_prob, second_prob], axis=1).astype(jnp.bfloat16)
    window_prob = jnp.where(in_window[:, 0], route_probs[:, 0], route_probs[:, 1])
    slot_labels = jnp.arange(capacity, dtype=jnp.int32)
    placement = (window_flag[None, :] & (slot_index[None, :] == slot_labels[:, None])).astype(
        jnp.bfloat16
    )
    send_rows = jnp.dot(placement, output_gradient, preferred_element_type=jnp.float32).astype(
        jnp.bfloat16
    )
    send_probs = jnp.dot(placement, window_prob, preferred_element_type=jnp.float32).astype(
        jnp.bfloat16
    )
    all_rows, all_probs = (
        lax.all_gather(send_rows, "expert", axis=0, tiled=True),
        lax.all_gather(send_probs, "expert", axis=0, tiled=True),
    )
    code_blocks = weight_normalized_entries.reshape(scales.shape[0], block_size, ff_share)
    own_weight = (
        (code_blocks.astype(jnp.float32) * scales.astype(jnp.float32)[:, None, :])
        .astype(jnp.bfloat16)
        .reshape(weight_normalized_entries.shape[0], ff_share)
    )
    product = jnp.dot(
        all_rows,
        lax.all_gather(own_weight, "shard", axis=0, tiled=True),
        preferred_element_type=jnp.float32,
    )
    hidden_grad = (all_probs.astype(jnp.float32)[:, None] * product).astype(jnp.bfloat16)
    partial_value = jnp.sum(stored_hidden_state[0, 0].astype(jnp.float32) * product, axis=1)
    returned = lax.psum_scatter(partial_value, "expert", scatter_dimension=0, tiled=True)
    window_grad = jnp.where(window_flag, returned[jnp.minimum(slot_index, capacity - 1)], 0.0)
    pair_grad = jnp.where(in_window, window_grad[:, None], 0.0)
    spread = first_prob * second_prob * (pair_grad[:, 0] - pair_grad[:, 1])
    sign_table = choose[:, 0, :].astype(jnp.float32) - choose[:, 1, :].astype(jnp.float32)
    logit_grad = (spread[:, None] * sign_table).astype(jnp.bfloat16)
    token_grad = jnp.dot(logit_grad, router_matrix, preferred_element_type=jnp.float32).astype(
        jnp.bfloat16
    )
    token_kept = lax.optimization_barrier(token_grad)
    residual_gradient = (
        output_gradient.astype(jnp.float32) + token_kept.astype(jnp.float32)
    ).astype(jnp.bfloat16)
    narrow_input = lax.dot_general(
        context, adapter_down_factor, (((1,), (1,)), ((), ())), preferred_element_type=jnp.float32
    ).astype(jnp.bfloat16)
    narrow_gradient = (
        ADAPTER_SCALE
        * lax.dot_general(
            residual_gradient,
            adapter_up_factor,
            (((1,), (1,)), ((), ())),
            preferred_element_type=jnp.float32,
        )
    ).astype(jnp.bfloat16)
    partial_up_gradient = ADAPTER_SCALE * lax.dot_general(
        narrow_input,
        residual_gradient,
        (((0,), (0,)), ((), ())),
        preferred_element_type=jnp.float32,
    )
    part_down = lax.dot_general(
        narrow_gradient, context, (((0,), (0,)), ((), ())), preferred_element_type=jnp.float32
    )
    summed_up, summed_down = lax.psum((partial_up_gradient, part_down), ("dp", "expert", "shard"))
    share_width = feature_width // shard_count
    first_col = lax.axis_index("shard") * share_width
    up_factor_gradient = lax.dynamic_slice_in_dim(summed_up, first_col, share_width, 1)
    grad_down = lax.dynamic_slice_in_dim(summed_down, first_col, share_width, 1)
    return (
        hidden_grad.reshape(stored_hidden_state.shape),
        token_grad,
        grad_down,
        up_factor_gradient,
    )


def solution(mesh):
    in_specs = (
        P(("dp", "expert", "shard"), None),
        P(("dp", "expert", "shard"), None),
        P(("dp", "expert", "shard"), None),
        P(),
        P("shard", "expert"),
        P("shard", "expert"),
        P("dp", "shard", None, "expert"),
        P(("dp", "expert", "shard"), None),
        P(),
        P(),
    )
    out_specs = (
        P("dp", "shard", None, "expert"),
        P(("dp", "expert", "shard"), None),
        P(None, "shard"),
        P(None, "shard"),
    )
    return jax.shard_map(
        per_device, mesh=mesh, in_specs=in_specs, out_specs=out_specs, check_vma=False
    )
```

profile of v0, /device:TPU:0, one launch (start us, length us, event | category | flops | bytes accessed | tf_op | source)
XLA Modules:
  0.0 608.2 jit_solution(15648484556468143896)
XLA Ops:
  7.2 0.0 copy-start
  7.2 0.0 all-gather.2.cloned.1.call-start
  7.2 1.0 convert_element_type.90
  8.2 7.4 %fusion = bf16[768,4096]{1,0:T(8,128)(2,1)} fusion(bf16[768,4096]{1,0:T(8,128)(2,1)} %param.14, f32[12,4096]{1,0:T(8,128)S(1)} %convert_element_type.90), kind=kLoop, calls=%fused_computation.2 | loop fusion | flops 9437184 | bytes 12779520 | tf_op jit(solution)/shard_map/convert_element_type | solution.py:57
  15.6 0.0 copy-start.4
  15.6 0.0 copy-start.6
  15.6 0.0 copy-start.1
  15.6 0.0 copy-start.5
  15.6 0.0 copy-start.3
  15.6 0.0 all-gather.2.cloned.1.call-update
  15.6 0.0 all-reduce.5.cloned.1.call-start
  15.7 0.6 copy-done.4
  16.3 0.5 fusion.24
  16.8 0.1 copy.26
  16.9 0.0 copy-done.6
  16.9 0.6 fusion.25
  18.2 0.2 reduce-window.4
  19.0 0.1 fusion.6
  19.1 0.0 copy-done.1
  19.1 0.0 copy-start.8
  19.1 0.2 convolution_convert_fusion.1
  19.4 2.2 all_gather.10
  21.6 0.0 copy-done.8
  21.6 0.0 copy-done.5
  21.6 422.1 %all-gather.2.cloned.1.call-done = bf16[3072,4096]{1,0:T(8,128)(2,1)} async-done(((bf16[768,4096]{1,0:T(8,128)(2,1)}), bf16[3072,4096]{1,0:T(8,128)(2,1)}) %all-gather.2.cloned.1.call-update) | async-done | bytes 25165840 | tf_op jit(solution)/shard_map/all_gather | solution.py:62
  443.7 0.0 copy-done.3
  443.7 11.1 %fusion.4 = (f32[64]{0:T(128)}, f32[64,4096]{1,0:T(8,128)S(1)}) fusion(bf16[1,1,64,4096]{3,2,1,0:T(8,128)(2,1)S(1)} %copy-done.3, bf16[64,3072]{1,0:T(8,128)(2,1)S(1)} %all_gather.10, bf16[3072,4096]{1,0:T(8,128)(2,1)} %all-gather.2.cloned.1.call-done), kind=kOutput, calls=%fused_computation.14 | convolution fusion | flops 1611399168 | bytes 27132160 | tf_op jit(solution)/shard_map/dot_general | solution.py:60
  454.8 0.0 copy-start.7
  454.8 0.0 copy-start.9
  454.8 2.6 all-reduce.1
  457.3 0.1 dynamic-slice.2
  457.4 1.2 gather_fusion
  458.7 0.7 broadcast_select_fusion
  459.3 1.2 convolution_convert_fusion
  460.6 0.0 copy-done
  460.6 0.0 copy-start.2
  460.6 3.0 convolution_multiply_fusion
  463.5 2.6 fusion.2
  466.2 0.0 copy-done.7
  466.2 0.0 copy-done.9
  466.2 0.1 fusion.3
  466.3 0.2 dynamic-update-slice
  466.5 2.5 all-reduce
  469.0 0.0 all-reduce.5.cloned.1.call-update
  469.0 0.9 fusion.5
  469.9 129.6 %all-reduce.5.cloned.1.call-done = (f32[64,3072]{1,0:T(8,128)}, f32[64,3072]{1,0:T(8,128)}) async-done(((f32[64,3072]{1,0:T(8,128)}, f32[64,3072]{1,0:T(8,128)}), (f32[64,3072]{1,0:T(8,128)}, f32[64,3072]{1,0:T(8,128)})) %all-reduce.5.cloned.1.call-update) | async-done | bytes 1572880 | tf_op jit(solution)/shard_map/psum | solution.py:101
  599.5 1.8 constant_dynamic-slice_fusion
  601.3 0.0 copy-done.2
  (9 shorter events, 0.1 us)
Async XLA Ops:
  7.2 453.4 %copy-start = (bf16[128,3072]{1,0:T(8,128)(2,1)S(1)}, bf16[128,3072]{1,0:T(8,128)(2,1)}, u32[]{:S(2)}) copy-start(bf16[128,3072]{1,0:T(8,128)(2,1)} %param.17) | copy-start | bytes 2359300
  7.2 436.5 %all-gather.2.cloned.1.call-start = ((), (), s32[]{:S(2)}) async-start(), calls=%async_computation | async-start | bytes 31457280 | tf_op jit(solution)/shard_map/all_gather | solution.py:62
  15.6 0.7 copy-start.4
  15.6 1.3 copy-start.6
  15.6 3.5 copy-start.1
  15.6 6.0 copy-start.5
  15.6 428.1 %copy-start.3 = (bf16[1,1,64,4096]{3,2,1,0:T(8,128)(2,1)S(1)}, bf16[1,1,64,4096]{3,2,1,0:T(8,128)(2,1)}, u32[]{:S(2)}) copy-start(bf16[1,1,64,4096]{3,2,1,0:T(8,128)(2,1)} %param.16) | copy-start | bytes 1572868
  15.6 583.9 %all-reduce.5.cloned.1.call-start = ((), (), s32[]{:S(2)}) async-start(), calls=%async_computation.1 | async-start | bytes 3145728 | tf_op jit(solution)/shard_map/psum | solution.py:101
  19.1 2.4 copy-start.8
  454.8 11.4 %copy-start.7 = (pred[128,2]{0,1:T(4,128)(4,1)S(1)}, pred[128,2]{0,1:T(4,128)(4,1)}, u32[]{:S(2)}) copy-start(pred[128,2]{0,1:T(4,128)(4,1)} %get-tuple-element.11) | copy-start | bytes 772
  454.8 11.4 %copy-start.9 = (s32[128]{0:T(128)S(1)}, s32[128]{0:T(128)}, u32[]{:S(2)}) copy-start(s32[128]{0:T(128)} %copy-done.8) | copy-start | bytes 1540
  460.6 140.8 %copy-start.2 = (bf16[128,3072]{1,0:T(8,128)(2,1)}, bf16[128,3072]{1,0:T(8,128)(2,1)S(1)}, u32[]{:S(2)}) copy-start(bf16[128,3072]{1,0:T(8,128)(2,1)S(1)} %convolution_convert_fusion) | copy-start | bytes 2359300
Sparse Core Ops, SparseCore 0:
  15.8 427.8 all-gather.1
  469.1 130.3 all-reduce.4
where the time goes:
time: 609 us; the launch traced here: 608 us
  waiting for transfers between devices  552 us (91%)
  matrix products  18.3 us (3%)
  between operations  15.5 us (3%)
  other arithmetic  10.8 us (2%)
  blocking collectives  7.19 us (1%)
    all_gather x1, waiting for transfers between devices, per_device(): lax.all_gather(own_weight, 'shard', axis=0, tiled=True)  422 us
    psum x1, waiting for transfers between devices, per_device(): lax.psum((partial_up_gradient, part_down), ('dp', 'expert', 'shard'))  130 us
  transfers between devices with their start and end apart: 2, of which 2 were waited for; matrix products, arithmetic and copies ran while one was open for 0% of the time, Pallas kernels for 0%

commit v1 on v0

v1 whole, which is shorter than its diff:
```python
import jax
import jax.numpy as jnp
from jax import lax
from jax.sharding import PartitionSpec as P

ADAPTER_SCALE = 0.25


def xor_pairs(count, bits):
    return [(i, i ^ bits) for i in range(count)]


def route(saved_router_scores, expert_choice_index, capacity):
    experts = saved_router_scores.shape[1]
    labels = jnp.arange(experts, dtype=jnp.int32)
    choose = expert_choice_index[:, :, None] == labels[None, None, :]
    chosen = jnp.sum(jnp.where(choose, saved_router_scores[:, None, :], 0.0), axis=2)
    first_prob = 1.0 / (1.0 + jnp.exp(chosen[:, 1] - chosen[:, 0]))
    second_prob = 1.0 - first_prob
    in_window = expert_choice_index == 0
    window_flag = jnp.any(in_window, axis=1)
    flag_int = window_flag.astype(jnp.int32)
    slot_index = jnp.cumsum(flag_int) - flag_int
    route_probs = jnp.stack([first_prob, second_prob], axis=1).astype(jnp.bfloat16)
    window_prob = jnp.where(in_window[:, 0], route_probs[:, 0], route_probs[:, 1])
    slot_labels = jnp.arange(capacity, dtype=jnp.int32)
    placement = window_flag[None, :] & (slot_index[None, :] == slot_labels[:, None])
    window_sign = in_window[:, 0].astype(jnp.float32) - in_window[:, 1].astype(jnp.float32)
    sign_table = choose[:, 0, :].astype(jnp.float32) - choose[:, 1, :].astype(jnp.float32)
    factors = (first_prob * second_prob * window_sign)[:, None] * sign_table
    return placement, window_prob, factors


def exchange_rows(send_rows, shard, shard_count):
    capacity, width = send_rows.shape
    blocks = send_rows.reshape(capacity, shard_count, width // shard_count).transpose(1, 0, 2)
    got = []
    for k in range(shard_count):
        block = lax.dynamic_index_in_dim(blocks, shard ^ k, 0, keepdims=False)
        if k:
            block = lax.ppermute(block, "shard", xor_pairs(shard_count, k))
        got.append(block)
    return jnp.stack(got)


def combine_products(parts, is_end):
    swap = xor_pairs(4, 1)
    first = jnp.where(is_end, parts[3], parts[1])
    last = jnp.where(is_end, parts[1], parts[3])
    near = lax.ppermute(first, "shard", swap)
    middle = lax.ppermute(last, "shard", [(1, 2), (2, 1)])
    near_wide = near.astype(jnp.float32)
    forward = parts[2].astype(jnp.float32) + jnp.where(is_end, 0.0, near_wide)
    far = lax.ppermute(forward.astype(jnp.bfloat16), "shard", xor_pairs(4, 2))
    outer = lax.ppermute(last, "shard", [(0, 1), (3, 2)])
    return (
        jnp.where(is_end, near_wide, 0.0)
        + middle.astype(jnp.float32)
        + far.astype(jnp.float32)
        + outer.astype(jnp.float32)
    )


def halve(value, axis, index, bit, count):
    half = value.shape[0] // 2
    side = (index >> bit) & 1
    keep = lax.dynamic_slice_in_dim(value, side * half, half, 0)
    send = lax.dynamic_slice_in_dim(value, (1 - side) * half, half, 0)
    got = lax.ppermute(send.astype(jnp.bfloat16), axis, xor_pairs(count, 1 << bit))
    return keep + got.astype(jnp.float32)


def widen(value, axis, index, bit, count):
    side = (index >> bit) & 1
    got = lax.ppermute(value, axis, xor_pairs(count, 1 << bit))
    return jnp.where(
        side == 0, jnp.concatenate([value, got], 0), jnp.concatenate([got, value], 0)
    )


def per_device(
    output_gradient,
    saved_router_scores,
    expert_choice_index,
    router_matrix,
    weight_normalized_entries,
    scales,
    stored_hidden_state,
    context,
    adapter_down_factor,
    adapter_up_factor,
):
    dp_count = lax.axis_size("dp")
    expert_count = lax.axis_size("expert")
    shard_count = lax.axis_size("shard")
    dp = lax.axis_index("dp")
    expert = lax.axis_index("expert")
    shard = lax.axis_index("shard")
    direct = (dp_count, expert_count, shard_count) == (4, 2, 4)
    tokens, feature_width = output_gradient.shape
    row_count = stored_hidden_state.shape[2]
    capacity = row_count // expert_count
    ff_share = stored_hidden_state.shape[3]
    share_width = feature_width // shard_count
    block_size = weight_normalized_entries.shape[0] // scales.shape[0]
    rank = adapter_up_factor.shape[0]

    placement, window_prob, factors = route(saved_router_scores, expert_choice_index, capacity)
    placed = placement.astype(jnp.bfloat16)
    send_rows = jnp.dot(placed, output_gradient, preferred_element_type=jnp.float32).astype(
        jnp.bfloat16
    )
    send_probs = jnp.dot(placed, window_prob, preferred_element_type=jnp.float32).astype(
        jnp.bfloat16
    )
    if direct:
        blocks = exchange_rows(send_rows, shard, shard_count)
    else:
        blocks = lax.all_to_all(
            send_rows.reshape(capacity, shard_count, share_width).transpose(1, 0, 2), "shard", 0, 0
        )
    gathered = lax.all_gather(blocks, "expert", axis=1)
    all_probs = lax.all_gather(send_probs, "expert", axis=0, tiled=True)

    code_blocks = weight_normalized_entries.reshape(scales.shape[0], block_size, ff_share)
    own_weight = (code_blocks * scales[:, None, :]).reshape(
        weight_normalized_entries.shape[0], ff_share
    )
    product = jnp.dot(
        gathered.reshape(shard_count * row_count, share_width),
        own_weight,
        preferred_element_type=jnp.float32,
    ).reshape(shard_count, row_count, ff_share)

    narrow_input = lax.dot_general(
        context, adapter_down_factor, (((1,), (1,)), ((), ())), preferred_element_type=jnp.float32
    ).astype(jnp.bfloat16)
    narrow_gradient = (
        ADAPTER_SCALE
        * lax.dot_general(
            output_gradient,
            adapter_up_factor,
            (((1,), (1,)), ((), ())),
            preferred_element_type=jnp.float32,
        )
    ).astype(jnp.bfloat16)
    early_up = ADAPTER_SCALE * lax.dot_general(
        narrow_input, output_gradient, (((0,), (0,)), ((), ())), preferred_element_type=jnp.float32
    )
    early_down = lax.dot_general(
        narrow_gradient, context, (((0,), (0,)), ((), ())), preferred_element_type=jnp.float32
    )
    early = jnp.concatenate([early_up, early_down], 0)

    if direct:
        is_end = (shard == 0) | (shard == 3)
        parts = [product[k].astype(jnp.bfloat16) for k in range(1, 4)]
        total = product[0] + combine_products([None] + parts, is_end)
        early = halve(early, "expert", expert, 0, 2)
        early = halve(early, "dp", dp, 0, 4)
        early = halve(early, "dp", dp, 1, 4)
        early_blocks = early.astype(jnp.bfloat16)
        early = jnp.sum(exchange_rows(early_blocks, shard, shard_count).astype(jnp.float32), 0)
        early = widen(early, "dp", dp, 1, 4)
        early = widen(early, "dp", dp, 0, 4)
        early = widen(early, "expert", expert, 0, 2)
    else:
        total = lax.psum_scatter(product.astype(jnp.bfloat16), "shard", scatter_dimension=0)
        total = total.astype(jnp.float32)
        early = lax.psum(early, ("dp", "expert"))
        early = lax.psum_scatter(early, "shard", scatter_dimension=1, tiled=True)

    hidden_grad = (all_probs.astype(jnp.float32)[:, None] * total).astype(jnp.bfloat16)
    partial_value = jnp.sum(stored_hidden_state[0, 0].astype(jnp.float32) * total, axis=1)
    slot_grad = lax.psum(partial_value, "expert")
    own_grad = lax.dynamic_slice_in_dim(slot_grad, expert * capacity, capacity, 0)
    window_grad = jnp.sum(jnp.where(placement, own_grad[:, None], 0.0), axis=0)
    logit_grad = (factors * window_grad[:, None]).astype(jnp.bfloat16)
    token_grad = jnp.dot(logit_grad, router_matrix, preferred_element_type=jnp.float32).astype(
        jnp.bfloat16
    )
    late_input = lax.dot_general(
        logit_grad, narrow_input, (((0,), (0,)), ((), ())), preferred_element_type=jnp.float32
    )
    late_context = lax.dot_general(
        logit_grad, context, (((0,), (0,)), ((), ())), preferred_element_type=jnp.float32
    )
    if direct:
        for bit in (1, 0):
            half = late_context.shape[1] // 2
            side = (shard >> bit) & 1
            keep = lax.dynamic_slice_in_dim(late_context, side * half, half, 1)
            send = lax.dynamic_slice_in_dim(late_context, (1 - side) * half, half, 1)
            got = lax.ppermute(
                jnp.concatenate([send, late_input], 1), "shard", xor_pairs(4, 1 << bit)
            )
            late_context = keep + got[:, :half]
            late_input = late_input + got[:, half:]
        late = jnp.concatenate([late_context, late_input], 1)
        for bit in (0, 1):
            late = late + lax.ppermute(late, "dp", xor_pairs(4, 1 << bit))
        late = late + lax.ppermute(late, "expert", [(0, 1), (1, 0)])
        late_context, late_input = late[:, :share_width], late[:, share_width:]
    else:
        late_input = lax.psum(late_input, ("dp", "expert", "shard"))
        late_context = lax.psum(late_context, ("dp", "expert"))
        late_context = lax.psum_scatter(late_context, "shard", scatter_dimension=1, tiled=True)
    own_router = lax.dynamic_slice_in_dim(router_matrix, shard * share_width, share_width, 1)
    factor_router = ADAPTER_SCALE * lax.dot_general(
        adapter_up_factor, router_matrix, (((1,), (1,)), ((), ())), preferred_element_type=jnp.float32
    )
    up_factor_gradient = early[:rank] + ADAPTER_SCALE * lax.dot_general(
        late_input,
        own_router.astype(jnp.float32),
        (((0,), (0,)), ((), ())),
        precision=lax.Precision.HIGHEST,
        preferred_element_type=jnp.float32,
    )
    grad_down = early[rank:] + jnp.dot(
        factor_router,
        late_context,
        precision=lax.Precision.HIGHEST,
        preferred_element_type=jnp.float32,
    )
    return (
        hidden_grad.reshape(stored_hidden_state.shape),
        token_grad,
        grad_down,
        up_factor_gradient,
    )


def solution(mesh):
    tokens_spec = P(("dp", "expert", "shard"), None)
    in_specs = (
        tokens_spec,
        tokens_spec,
        tokens_spec,
        P(),
        P("shard", "expert"),
        P("shard", "expert"),
        P("dp", "shard", None, "expert"),
        tokens_spec,
        P(),
        P(),
    )
    out_specs = (
        P("dp", "shard", None, "expert"),
        tokens_spec,
        P(None, "shard"),
        P(None, "shard"),
    )
    return jax.shard_map(
        per_device, mesh=mesh, in_specs=in_specs, out_specs=out_specs, check_vma=False
    )
```

time: 609 us -> 127 us (0.21)
  waiting for transfers between devices: 552 us -> 46.3 us
  starting transfers between devices: 0.08 us -> 28.8 us
  between operations: 15.5 us -> 1.7 us
  other arithmetic: 10.8 us -> 19.1 us
    all_gather x1 -> x0, waiting for transfers between devices: 422 us -> none  [per_device(): lax.all_gather(own_weight, 'shard', axis=0, tiled=True)]
    psum x1 -> x0, waiting for transfers between devices: 130 us -> none  [per_device(): lax.psum((partial_up_gradient, part_down), ('dp', 'expert', 'shard'))]
    ppermute x0 -> x21, waiting for transfers between devices: none -> 46.3 us  [the longest x1 20.8 us: combine_products(): near = lax.ppermute(first, 'shard', swap)]
    ppermute x0 -> x21, starting transfers between devices: none -> 28.8 us  [the longest x6 11.3 us: exchange_rows(): block = lax.ppermute(block, 'shard', xor_pairs(shard_count, k))]
    mul x1 -> x2, other arithmetic: 0.01 us -> 6.65 us  [the longest x1 5.9 us: per_device(): code_blocks * scales[:, None, :]]
    convert_element_type x4 -> x5, other arithmetic: 8.37 us -> 1.85 us  [the longest x1 0.95 us: combine_products(): far = lax.ppermute(forward.astype(jnp.bfloat16), 'shard', xor_pairs(4, 2))]
    dot_general x4 -> x10, matrix products: 14.4 us -> 13.5 us  [the longest x1 6.64 us: per_device(): jnp.dot(gathered.reshape(shard_count * row_count, share_width), own_weigh...]
  transfers between devices with their start and end apart: 2 -> 21, of which waited for: 2 -> 8; matrix products, arithmetic and copies ran while one was open for 0% -> 27% of each run, Pallas kernels for 0% -> 0%
where the time goes in v1:
time: 127 us; the launch traced here: 126 us
  waiting for transfers between devices  46.3 us (36%)
  starting transfers between devices  28.8 us (23%)
  other arithmetic  19.1 us (15%)
  matrix products  15.5 us (12%)
  local copies, waits for them, and re-layouts  7.66 us (6%)
  blocking collectives  7.14 us (6%)
  between operations  1.7 us (1%)
    ppermute x1, waiting for transfers between devices, combine_products(): near = lax.ppermute(first, 'shard', swap)  20.8 us
    ppermute x6, waiting for transfers between devices, exchange_rows(): block = lax.ppermute(block, 'shard', xor_pairs(shard_count, k))  12.3 us
    ppermute x6, starting transfers between devices, exchange_rows(): block = lax.ppermute(block, 'shard', xor_pairs(shard_count, k))  11.3 us
    ppermute x2, waiting for transfers between devices, per_device(): lax.ppermute(jnp.concatenate([send, late_input], 1), 'shard', xor_pairs(4...  7.34 us
    dot_general x1, matrix products, per_device(): jnp.dot(gathered.reshape(shard_count * row_count, share_width), own_weigh...  6.64 us
    unnamed x35, local copies, waits for them, and re-layouts  5.95 us
    mul x1, other arithmetic, per_device(): code_blocks * scales[:, None, :]  5.9 us
    ppermute x1, starting transfers between devices, combine_products(): outer = lax.ppermute(last, 'shard', [(0, 1), (3, 2)])  5.86 us
  transfers between devices with their start and end apart: 21, of which 8 were waited for; matrix products, arithmetic and copies ran while one was open for 27% of the time, Pallas kernels for 0%

profile of v1, /device:TPU:0, one launch (start us, length us, event | category | flops | bytes accessed | tf_op | source)
XLA Modules:
  0.0 126.3 jit_solution(9030179930383845992)
XLA Ops:
  0.7 1.4 %fusion.46 = (pred[128]{0:T(512)(128)(4,1)S(1)}, pred[128,2]{0,1:T(4,128)(4,1)}) fusion(s32[128,2]{0,1:T(2,128)} %param.12), kind=kLoop, calls=%fused_computation.107 | loop fusion | flops 384 | bytes 1408 | tf_op jit(solution)/shard_map/reduce_or | solution.py:21
  2.1 0.1 copy.28
  2.2 0.2 reduce-window.8
  2.3 0.1 reduce
  2.6 0.6 copy-done.10
  3.1 0.2 convolution_convert_fusion.1
  3.4 0.1 reshape.95
  3.5 1.1 constant_dynamic-slice_fusion.9
  4.6 0.6 copy.53
  5.2 5.1 %collective-permute-start.2 = (bf16[32,768]{1,0:T(8,128)(2,1)}, bf16[32,768]{1,0:T(8,128)(2,1)}, u32[]{:S(2)}, u32[]{:S(2)}) collective-permute-start(bf16[32,768]{1,0:T(8,128)(2,1)} %bitcast.65), channel_id=1, source_target_pairs={{0,3},{1,2},{2,1},{3,0},{4,7},{5,6},{6,5},{7,4},{8,11},{9,10},{10,... | collective-permute-start | bytes 147464 | tf_op jit(solution)/shard_map/ppermute | solution.py:41
  10.3 0.6 copy.55
  10.9 0.6 copy.54
  11.5 0.6 collective-permute-start.1
  12.1 1.6 %convolution_convert_fusion.2 = bf16[128,64]{0,1:T(8,128)(2,1)S(1)} fusion(bf16[128,3072]{1,0:T(8,128)(2,1)} %param.17, bf16[64,3072]{1,0:T(8,128)(2,1)} %param.18), kind=kOutput, calls=%fused_computation.13 | convolution fusion | flops 50339840 | bytes 1196032 | tf_op jit(solution)/shard_map/dot_general | solution.py:135
  13.7 0.3 convolution_multiply_fusion
  14.0 0.8 fusion.1
  14.8 0.9 fusion.11
  15.6 1.3 iota_compare_fusion.1
  16.9 1.6 %convolution_multiply_fusion.3 = f32[64,8]{0,1:T(8,128)} fusion(bf16[64,3072]{1,0:T(8,128)(2,1)S(1)} %copy-done.2, bf16[8,3072]{1,0:T(8,128)(2,1)} %param.13), kind=kOutput, calls=%fused_computation.15 | convolution fusion | flops 3146240 | bytes 444416 | tf_op jit(solution)/shard_map/dot_general | solution.py:209
  18.5 1.3 %select_reduce_fusion.1 = f32[128,2]{0,1:T(2,128)} fusion(f32[128,8]{0,1:T(8,128)} %param.11, s32[128,2]{0,1:T(2,128)} %param.12), kind=kLoop, calls=%fused_computation.65 | loop fusion | flops 5888 | bytes 6144 | tf_op jit(solution)/shard_map/reduce_sum | solution.py:17
  19.8 0.9 copy.56
  20.7 5.9 %bitcast_multiply_fusion = bf16[768,4096]{1,0:T(8,128)(2,1)} fusion(bf16[768,4096]{1,0:T(8,128)(2,1)} %param.14, bf16[12,4096]{1,0:T(8,128)(2,1)} %param.15), kind=kLoop, calls=%fused_computation | loop fusion | flops 3145728 | bytes 12681216 | tf_op jit(solution)/shard_map/mul | solution.py:126
  26.6 0.9 pad_maximum_fusion
  27.5 2.2 %all-gather = bf16[4,64,768]{2,1,0:T(8,128)(2,1)S(1)} all-gather(bf16[4,32,768]{2,1,0:T(8,128)(2,1)S(1)} %pad_maximum_fusion), channel_id=2, replica_groups=mesh['dp'=4,'expert'=2,'shard'=4] {'expert'}, dimensions={1}, use_global_device_ids=true | all-gather | bytes 589824 | tf_op jit(solution)/shard_map/all_gather | solution.py:122
  29.7 6.6 %fusion.47 = (bf16[256,4096]{1,0:T(8,128)(2,1)S(1)}, f32[256,4096]{1,0:T(8,128)}) fusion(bf16[256,768]{1,0:T(8,128)(2,1)S(1)} %bitcast.73, bf16[768,4096]{1,0:T(8,128)(2,1)} %bitcast_multiply_fusion), kind=kOutput, calls=%fused_computation.108 | convolution fusion | flops 1611661312 | bytes 12976128 | tf_op jit(solution)/shard_map/dot_general | solution.py:129
  36.3 1.1 fusion.13
  37.5 1.8 %collective-permute-start.8 = (bf16[32,3072]{1,0:T(8,128)(2,1)S(1)}, bf16[32,3072]{1,0:T(8,128)(2,1)S(1)}, u32[]{:S(2)}, u32[]{:S(2)}) collective-permute-start(bf16[32,3072]{1,0:T(8,128)(2,1)S(1)} %dynamic-slice_convert_fusion), channel_id=1, source_target_pairs={{0,8},{8,0},{16,24},{24,16},{1,9},{9,1},{17,25},{25,17},{2,10},{10... | collective-permute-start | bytes 589832 | tf_op jit(solution)/shard_map/ppermute | solution.py:69
  39.3 0.9 broadcast_select_fusion.1
  40.2 0.7 collective-permute-start.4
  40.9 5.9 %collective-permute-start.6 = (bf16[64,4096]{1,0:T(8,128)(2,1)}, bf16[64,4096]{1,0:T(8,128)(2,1)S(1)}, u32[]{:S(2)}, u32[]{:S(2)}) collective-permute-start(bf16[64,4096]{1,0:T(8,128)(2,1)} %get-tuple-element.11), channel_id=1, source_target_pairs={{0,1},{3,2},{4,5},{7,6},{8,9},{11,10},{12,13},{15,14},{16,17},{19,... | collective-permute-start | bytes 1572872 | tf_op jit(solution)/shard_map/ppermute | solution.py:55
  46.9 1.6 %collective-permute-start.9 = (bf16[16,3072]{1,0:T(8,128)(2,1)S(1)}, bf16[16,3072]{1,0:T(8,128)(2,1)S(1)}, u32[]{:S(2)}, u32[]{:S(2)}) collective-permute-start(bf16[16,3072]{1,0:T(8,128)(2,1)S(1)} %dynamic-slice_convert_fusion.1), channel_id=1, source_target_pairs={{0,16},{8,24},{16,0},{24,8},{1,17},{9,25},{17,1},{25,9},{2,18},{10... | collective-permute-start | bytes 294920 | tf_op jit(solution)/shard_map/ppermute | solution.py:69
  48.5 20.8 %collective-permute-done.3 = bf16[64,4096]{1,0:T(8,128)(2,1)S(1)} collective-permute-done((bf16[64,4096]{1,0:T(8,128)(2,1)S(1)}, bf16[64,4096]{1,0:T(8,128)(2,1)S(1)}, u32[]{:S(2)}, u32[]{:S(2)}) %collective-permute-start.3) | collective-permute-done | bytes 524320 | tf_op jit(solution)/shard_map/ppermute | solution.py:50
  69.3 0.9 fusion.8
  70.2 2.5 %collective-permute-start.5 = (bf16[64,4096]{1,0:T(8,128)(2,1)}, bf16[64,4096]{1,0:T(8,128)(2,1)}, u32[]{:S(2)}, u32[]{:S(2)}) collective-permute-start(bf16[64,4096]{1,0:T(8,128)(2,1)} %fusion.8), channel_id=1, source_target_pairs={{0,2},{1,3},{2,0},{3,1},{4,6},{5,7},{6,4},{7,5},{8,10},{9,11},{10,... | collective-permute-start | bytes 1572872 | tf_op jit(solution)/shard_map/ppermute | solution.py:54
  72.8 0.2 constant_dynamic-slice_fusion.5
  73.1 0.8 fusion.35
  73.9 3.0 %collective-permute-start.11 = (bf16[16,768]{1,0:T(8,128)(2,1)S(1)}, bf16[16,768]{1,0:T(8,128)(2,1)S(1)}, u32[]{:S(2)}, u32[]{:S(2)}) collective-permute-start(bf16[16,768]{1,0:T(8,128)(2,1)S(1)} %bitcast.79), channel_id=1, source_target_pairs={{0,2},{1,3},{2,0},{3,1},{4,6},{5,7},{6,4},{7,5},{8,10},{9,11},{10,... | collective-permute-start | bytes 73736 | tf_op jit(solution)/shard_map/ppermute | solution.py:41
  76.9 7.2 %collective-permute-done.10 = bf16[16,768]{1,0:T(8,128)(2,1)S(1)} collective-permute-done((bf16[16,768]{1,0:T(8,128)(2,1)S(1)}, bf16[16,768]{1,0:T(8,128)(2,1)S(1)}, u32[]{:S(2)}, u32[]{:S(2)}) %collective-permute-start.10) | collective-permute-done | bytes 24608 | tf_op jit(solution)/shard_map/ppermute | solution.py:41
  84.0 2.6 %collective-permute-start.12 = (bf16[16,768]{1,0:T(8,128)(2,1)S(1)}, bf16[16,768]{1,0:T(8,128)(2,1)S(1)}, u32[]{:S(2)}, u32[]{:S(2)}) collective-permute-start(bf16[16,768]{1,0:T(8,128)(2,1)S(1)} %bitcast.80), channel_id=1, source_target_pairs={{0,3},{1,2},{2,1},{3,0},{4,7},{5,6},{6,5},{7,4},{8,11},{9,10},{10,... | collective-permute-start | bytes 73736 | tf_op jit(solution)/shard_map/ppermute | solution.py:41
  86.7 0.8 fusion.2
  87.5 1.2 dynamic-slice.32
  89.4 0.2 dynamic-update-slice
  89.6 2.4 %all-reduce = bf16[64]{0:T(256)(128)(2,1)S(1)} all-reduce(bf16[64]{0:T(256)(128)(2,1)S(1)} %dynamic-update-slice), channel_id=1, replica_groups=mesh['dp'=4,'expert'=2,'shard'=4] {'expert'}, use_global_device_ids=true, to_apply=%add | all-reduce | flops 64 | bytes 256
  92.1 5.1 %collective-permute-done.11 = bf16[16,768]{1,0:T(8,128)(2,1)S(1)} collective-permute-done((bf16[16,768]{1,0:T(8,128)(2,1)S(1)}, bf16[16,768]{1,0:T(8,128)(2,1)S(1)}, u32[]{:S(2)}, u32[]{:S(2)}) %collective-permute-start.11) | collective-permute-done | bytes 24608 | tf_op jit(solution)/shard_map/ppermute | solution.py:41
  97.2 1.6 %collective-permute-start.13 = (f32[16,768]{1,0:T(8,128)S(1)}, f32[16,768]{1,0:T(8,128)S(1)}, u32[]{:S(2)}, u32[]{:S(2)}) collective-permute-start(f32[16,768]{1,0:T(8,128)S(1)} %convert_reduce_fusion), channel_id=1, source_target_pairs={{0,16},{8,24},{16,0},{24,8},{1,17},{9,25},{17,1},{25,9},{2,18},{10... | collective-permute-start | bytes 147464 | tf_op jit(solution)/shard_map/ppermute | solution.py:75
  98.8 0.8 copy-done.3
  99.6 0.2 copy-done.4
  99.8 2.4 %fusion.9 = (f32[64]{0:T(128)S(1)}, f32[64,4096]{1,0:T(8,128)S(1)}) fusion(bf16[1,1,64,4096]{3,2,1,0:T(8,128)(2,1)} %param.16, bf16[64,4096]{1,0:T(8,128)(2,1)} %copy-done.4, bf16[64,4096]{1,0:T(8,128)(2,1)} %collective-permute-done.5, bf16[64,4096]{1,0:T(8,128)(2,1)} %copy-done.3, bf16[64,4096]{1,0:T(8,128)(2,1)S(1)} %collective-permute-done.3, pred[]{:T(512)S(6)} %or.3, ...), kind=kLoop, calls=%fused_computation.25 | loop fusion | flops 3145664 | bytes 4718849 | tf_op jit(solution)/shard_map/reduce_sum | solution.py:174
  102.1 2.5 %psum.7 = f32[64]{0:T(128)S(1)} all-reduce(f32[64]{0:T(128)S(1)} %get-tuple-element.6), channel_id=1, replica_groups=mesh['dp'=4,'expert'=2,'shard'=4] {'expert'}, use_global_device_ids=true, to_apply=%region_4.5 | all-reduce | flops 64 | bytes 512 | tf_op jit(solution)/shard_map/psum | solution.py:175
  104.8 0.2 fusion.41
  105.0 0.1 fusion.39
  105.1 1.6 %collective-permute-start.16 = (f32[8,1600]{1,0:T(8,128)S(1)}, f32[8,1600]{1,0:T(8,128)S(1)}, u32[]{:S(2)}, u32[]{:S(2)}) collective-permute-start(f32[8,1600]{1,0:T(8,128)S(1)} %pad_maximum_fusion.1), channel_id=1, source_target_pairs={{0,2},{1,3},{2,0},{3,1},{4,6},{5,7},{6,4},{7,5},{8,10},{9,11},{10,... | collective-permute-start | bytes 153608 | tf_op jit(solution)/shard_map/ppermute | solution.py:194
  106.8 0.6 collective-permute-start.14
  107.4 3.8 %collective-permute-done.16 = f32[8,1600]{1,0:T(8,128)S(1)} collective-permute-done((f32[8,1600]{1,0:T(8,128)S(1)}, f32[8,1600]{1,0:T(8,128)S(1)}, u32[]{:S(2)}, u32[]{:S(2)}) %collective-permute-start.16) | collective-permute-done | bytes 51232 | tf_op jit(solution)/shard_map/ppermute | solution.py:194
  111.3 0.2 collective-permute-done.14
  111.6 3.6 %collective-permute-done.17 = f32[8,832]{1,0:T(8,128)S(1)} collective-permute-done((f32[8,832]{1,0:T(8,128)S(1)}, f32[8,832]{1,0:T(8,128)S(1)}, u32[]{:S(2)}, u32[]{:S(2)}) %collective-permute-start.17) | collective-permute-done | bytes 26656 | tf_op jit(solution)/shard_map/ppermute | solution.py:194
  115.2 0.6 collective-permute-start.18
  115.8 3.3 %collective-permute-done.18 = f32[8,832]{1,0:T(8,128)S(1)} collective-permute-done((f32[8,832]{1,0:T(8,128)S(1)}, f32[8,832]{1,0:T(8,128)S(1)}, u32[]{:S(2)}, u32[]{:S(2)}) %collective-permute-start.18) | collective-permute-done | bytes 26656 | tf_op jit(solution)/shard_map/ppermute | solution.py:201
  119.1 0.5 collective-permute-start.19
  119.6 0.9 fusion.14
  120.5 2.4 %collective-permute-done.19 = f32[8,832]{1,0:T(8,128)S(1)} collective-permute-done((f32[8,832]{1,0:T(8,128)S(1)}, f32[8,832]{1,0:T(8,128)S(1)}, u32[]{:S(2)}, u32[]{:S(2)}) %collective-permute-start.19) | collective-permute-done | bytes 26656 | tf_op jit(solution)/shard_map/ppermute | solution.py:201
  123.0 1.3 %convolution_convert_fusion = bf16[128,3072]{1,0:T(8,128)(2,1)} fusion(bf16[8,3072]{1,0:T(8,128)(2,1)S(1)} %copy-done.5, pred[128,2,8]{0,2,1:T(8,128)(4,1)S(1)} %copy-done.7, f32[128]{0:T(128)S(1)} %select_reduce_fusion, f32[128]{0:T(128)S(1)} %get-tuple-element.4), kind=kOutput, calls=%fused_computation.1 | convolution fusion | flops 6690816 | bytes 838656 | tf_op jit(solution)/shard_map/dot_general | solution.py:179
  124.3 1.0 slice_add_fusion
  125.3 1.0 slice_add_fusion.1
  (72 shorter events, 1.0 us)
Async XLA Ops:
  0.6 2.5 %copy-start = (bf16[128,3072]{1,0:T(8,128)(2,1)S(1)}, bf16[128,3072]{1,0:T(8,128)(2,1)}, u32[]{:S(2)}) copy-start(bf16[128,3072]{1,0:T(8,128)(2,1)} %param.10) | copy-start | bytes 2359300
  0.6 13.3 %copy-start.1 = (bf16[128,3072]{1,0:T(8,128)(2,1)S(1)}, bf16[128,3072]{1,0:T(8,128)(2,1)}, u32[]{:S(2)}) copy-start(bf16[128,3072]{1,0:T(8,128)(2,1)} %param.17) | copy-start | bytes 2359300
  0.7 13.3 %copy-start.2 = (bf16[64,3072]{1,0:T(8,128)(2,1)S(1)}, bf16[64,3072]{1,0:T(8,128)(2,1)}, u32[]{:S(2)}) copy-start(bf16[64,3072]{1,0:T(8,128)(2,1)} %param.19) | copy-start | bytes 1179652
  2.0 0.5 copy-start.8
  2.6 0.6 copy-start.10
  5.2 21.4 %collective-permute-start.2 = (bf16[32,768]{1,0:T(8,128)(2,1)}, bf16[32,768]{1,0:T(8,128)(2,1)}, u32[]{:S(2)}, u32[]{:S(2)}) collective-permute-start(bf16[32,768]{1,0:T(8,128)(2,1)} %bitcast.65), channel_id=1, source_target_pairs={{0,3},{1,2},{2,1},{3,0},{4,7},{5,6},{6,5},{7,4},{8,11},{9,10},{10,... | collective-permute-start | bytes 147464 | tf_op jit(solution)/shard_map/ppermute | solution.py:41
  10.9 15.7 %collective-permute-start = (bf16[32,768]{1,0:T(8,128)(2,1)}, bf16[32,768]{1,0:T(8,128)(2,1)}, u32[]{:S(2)}, u32[]{:S(2)}) collective-permute-start(bf16[32,768]{1,0:T(8,128)(2,1)} %bitcast.67), channel_id=1, source_target_pairs={{0,1},{1,0},{2,3},{3,2},{4,5},{5,4},{6,7},{7,6},{8,9},{9,8},{10,11... | collective-permute-start | bytes 147464 | tf_op jit(solution)/shard_map/ppermute | solution.py:41
  11.5 15.1 %collective-permute-start.1 = (bf16[32,768]{1,0:T(8,128)(2,1)}, bf16[32,768]{1,0:T(8,128)(2,1)}, u32[]{:S(2)}, u32[]{:S(2)}) collective-permute-start(bf16[32,768]{1,0:T(8,128)(2,1)} %bitcast.66), channel_id=1, source_target_pairs={{0,2},{1,3},{2,0},{3,1},{4,6},{5,7},{6,4},{7,5},{8,10},{9,11},{10,... | collective-permute-start | bytes 147464 | tf_op jit(solution)/shard_map/ppermute | solution.py:41
  15.6 20.7 %collective-permute-start.7 = (bf16[64,3072]{1,0:T(8,128)(2,1)}, bf16[64,3072]{1,0:T(8,128)(2,1)}, u32[]{:S(2)}, u32[]{:S(2)}) collective-permute-start(bf16[64,3072]{1,0:T(8,128)(2,1)} %fusion.11), channel_id=1, source_target_pairs={{0,4},{4,0},{1,5},{5,1},{2,6},{6,2},{3,7},{7,3},{8,12},{12,8},{9,1... | collective-permute-start | bytes 1179656 | tf_op jit(solution)/shard_map/ppermute | solution.py:69
  37.5 9.3 %collective-permute-start.8 = (bf16[32,3072]{1,0:T(8,128)(2,1)S(1)}, bf16[32,3072]{1,0:T(8,128)(2,1)S(1)}, u32[]{:S(2)}, u32[]{:S(2)}) collective-permute-start(bf16[32,3072]{1,0:T(8,128)(2,1)S(1)} %dynamic-slice_convert_fusion), channel_id=1, source_target_pairs={{0,8},{8,0},{16,24},{24,16},{1,9},{9,1},{17,25},{25,17},{2,10},{10... | collective-permute-start | bytes 589832 | tf_op jit(solution)/shard_map/ppermute | solution.py:69
  40.2 58.6 %collective-permute-start.4 = (bf16[64,4096]{1,0:T(8,128)(2,1)}, bf16[64,4096]{1,0:T(8,128)(2,1)S(1)}, u32[]{:S(2)}, u32[]{:S(2)}) collective-permute-start(bf16[64,4096]{1,0:T(8,128)(2,1)} %get-tuple-element.11), channel_id=1, source_target_pairs={{1,2},{2,1},{5,6},{6,5},{9,10},{10,9},{13,14},{14,13},{17,18},{18,... | collective-permute-start | bytes 1572872 | tf_op jit(solution)/shard_map/ppermute | solution.py:51
  40.9 57.9 %collective-permute-start.6 = (bf16[64,4096]{1,0:T(8,128)(2,1)}, bf16[64,4096]{1,0:T(8,128)(2,1)S(1)}, u32[]{:S(2)}, u32[]{:S(2)}) collective-permute-start(bf16[64,4096]{1,0:T(8,128)(2,1)} %get-tuple-element.11), channel_id=1, source_target_pairs={{0,1},{3,2},{4,5},{7,6},{8,9},{11,10},{12,13},{15,14},{16,17},{19,... | collective-permute-start | bytes 1572872 | tf_op jit(solution)/shard_map/ppermute | solution.py:55
  46.7 22.5 %collective-permute-start.3 = (bf16[64,4096]{1,0:T(8,128)(2,1)S(1)}, bf16[64,4096]{1,0:T(8,128)(2,1)S(1)}, u32[]{:S(2)}, u32[]{:S(2)}) collective-permute-start(bf16[64,4096]{1,0:T(8,128)(2,1)S(1)} %get-tuple-element.10), channel_id=1, source_target_pairs={{0,1},{1,0},{2,3},{3,2},{4,5},{5,4},{6,7},{7,6},{8,9},{9,8},{10,11... | collective-permute-start | bytes 1572872 | tf_op jit(solution)/shard_map/ppermute | solution.py:50
  46.9 57.8 %copy-start.9 = (pred[128]{0:T(512)(128)(4,1)S(1)}, pred[128]{0:T(512)(128)(4,1)}, u32[]{:S(2)}) copy-start(pred[128]{0:T(512)(128)(4,1)} %copy-done.8) | copy-start | bytes 388
  46.9 57.8 %copy-start.11 = (s32[128]{0:T(128)S(1)}, s32[128]{0:T(128)}, u32[]{:S(2)}) copy-start(s32[128]{0:T(128)} %copy-done.10) | copy-start | bytes 1540
  46.9 57.9 %copy-start.7 = (pred[128,2,8]{0,2,1:T(8,128)(4,1)S(1)}, pred[128,2,8]{0,2,1:T(8,128)(4,1)}, u32[]{:S(2)}) copy-start(pred[128,2,8]{0,2,1:T(8,128)(4,1)} %iota_compare_fusion.1) | copy-start | bytes 6148
  46.9 25.8 %collective-permute-start.9 = (bf16[16,3072]{1,0:T(8,128)(2,1)S(1)}, bf16[16,3072]{1,0:T(8,128)(2,1)S(1)}, u32[]{:S(2)}, u32[]{:S(2)}) collective-permute-start(bf16[16,3072]{1,0:T(8,128)(2,1)S(1)} %dynamic-slice_convert_fusion.1), channel_id=1, source_target_pairs={{0,16},{8,24},{16,0},{24,8},{1,17},{9,25},{17,1},{25,9},{2,18},{10... | collective-permute-start | bytes 294920 | tf_op jit(solution)/shard_map/ppermute | solution.py:69
  70.2 28.6 %collective-permute-start.5 = (bf16[64,4096]{1,0:T(8,128)(2,1)}, bf16[64,4096]{1,0:T(8,128)(2,1)}, u32[]{:S(2)}, u32[]{:S(2)}) collective-permute-start(bf16[64,4096]{1,0:T(8,128)(2,1)} %fusion.8), channel_id=1, source_target_pairs={{0,2},{1,3},{2,0},{3,1},{4,6},{5,7},{6,4},{7,5},{8,10},{9,11},{10,... | collective-permute-start | bytes 1572872 | tf_op jit(solution)/shard_map/ppermute | solution.py:54
  73.0 11.0 %collective-permute-start.10 = (bf16[16,768]{1,0:T(8,128)(2,1)S(1)}, bf16[16,768]{1,0:T(8,128)(2,1)S(1)}, u32[]{:S(2)}, u32[]{:S(2)}) collective-permute-start(bf16[16,768]{1,0:T(8,128)(2,1)S(1)} %bitcast.81), channel_id=1, source_target_pairs={{0,1},{1,0},{2,3},{3,2},{4,5},{5,4},{6,7},{7,6},{8,9},{9,8},{10,11... | collective-permute-start | bytes 73736 | tf_op jit(solution)/shard_map/ppermute | solution.py:41
  73.9 23.3 %collective-permute-start.11 = (bf16[16,768]{1,0:T(8,128)(2,1)S(1)}, bf16[16,768]{1,0:T(8,128)(2,1)S(1)}, u32[]{:S(2)}, u32[]{:S(2)}) collective-permute-start(bf16[16,768]{1,0:T(8,128)(2,1)S(1)} %bitcast.79), channel_id=1, source_target_pairs={{0,2},{1,3},{2,0},{3,1},{4,6},{5,7},{6,4},{7,5},{8,10},{9,11},{10,... | collective-permute-start | bytes 73736 | tf_op jit(solution)/shard_map/ppermute | solution.py:41
  84.0 13.1 %collective-permute-start.12 = (bf16[16,768]{1,0:T(8,128)(2,1)S(1)}, bf16[16,768]{1,0:T(8,128)(2,1)S(1)}, u32[]{:S(2)}, u32[]{:S(2)}) collective-permute-start(bf16[16,768]{1,0:T(8,128)(2,1)S(1)} %bitcast.80), channel_id=1, source_target_pairs={{0,3},{1,2},{2,1},{3,0},{4,7},{5,6},{6,5},{7,4},{8,11},{9,10},{10,... | collective-permute-start | bytes 73736 | tf_op jit(solution)/shard_map/ppermute | solution.py:41
  97.2 9.6 %collective-permute-start.13 = (f32[16,768]{1,0:T(8,128)S(1)}, f32[16,768]{1,0:T(8,128)S(1)}, u32[]{:S(2)}, u32[]{:S(2)}) collective-permute-start(f32[16,768]{1,0:T(8,128)S(1)} %convert_reduce_fusion), channel_id=1, source_target_pairs={{0,16},{8,24},{16,0},{24,8},{1,17},{9,25},{17,1},{25,9},{2,18},{10... | collective-permute-start | bytes 147464 | tf_op jit(solution)/shard_map/ppermute | solution.py:75
  98.8 0.8 copy-start.3
  98.8 1.0 copy-start.4
  99.8 23.3 %copy-start.5 = (bf16[8,3072]{1,0:T(8,128)(2,1)S(1)}, bf16[8,3072]{1,0:T(8,128)(2,1)}, u32[]{:S(2)}) copy-start(bf16[8,3072]{1,0:T(8,128)(2,1)} %param.13) | copy-start | bytes 147460
  99.8 25.5 %copy-start.6 = (f32[64,8]{0,1:T(8,128)S(1)}, f32[64,8]{0,1:T(8,128)}, u32[]{:S(2)}) copy-start(f32[64,8]{0,1:T(8,128)} %convolution_multiply_fusion.3) | copy-start | bytes 6148
  105.1 6.0 %collective-permute-start.16 = (f32[8,1600]{1,0:T(8,128)S(1)}, f32[8,1600]{1,0:T(8,128)S(1)}, u32[]{:S(2)}, u32[]{:S(2)}) collective-permute-start(f32[8,1600]{1,0:T(8,128)S(1)} %pad_maximum_fusion.1), channel_id=1, source_target_pairs={{0,2},{1,3},{2,0},{3,1},{4,6},{5,7},{6,4},{7,5},{8,10},{9,11},{10,... | collective-permute-start | bytes 153608 | tf_op jit(solution)/shard_map/ppermute | solution.py:194
  106.8 4.7 %collective-permute-start.14 = (f32[32,768]{1,0:T(8,128)S(1)}, f32[32,768]{1,0:T(8,128)S(1)}, u32[]{:S(2)}, u32[]{:S(2)}) collective-permute-start(f32[32,768]{1,0:T(8,128)S(1)} %maximum_select_fusion.2), channel_id=1, source_target_pairs={{0,8},{8,0},{16,24},{24,16},{1,9},{9,1},{17,25},{25,17},{2,10},{10... | collective-permute-start | bytes 294920 | tf_op jit(solution)/shard_map/ppermute | solution.py:75
  111.2 3.9 %collective-permute-start.17 = (f32[8,832]{1,0:T(8,128)S(1)}, f32[8,832]{1,0:T(8,128)S(1)}, u32[]{:S(2)}, u32[]{:S(2)}) collective-permute-start(f32[8,832]{1,0:T(8,128)S(1)} %pad_maximum_fusion.2), channel_id=1, source_target_pairs={{0,1},{1,0},{2,3},{3,2},{4,5},{5,4},{6,7},{7,6},{8,9},{9,8},{10,11... | collective-permute-start | bytes 79880 | tf_op jit(solution)/shard_map/ppermute | solution.py:194
  111.5 4.3 %collective-permute-start.15 = (f32[64,768]{1,0:T(8,128)S(1)}, f32[64,768]{1,0:T(8,128)S(1)}, u32[]{:S(2)}, u32[]{:S(2)}) collective-permute-start(f32[64,768]{1,0:T(8,128)S(1)} %maximum_select_fusion.1), channel_id=1, source_target_pairs={{0,4},{4,0},{1,5},{5,1},{2,6},{6,2},{3,7},{7,3},{8,12},{12,8},{9,1... | collective-permute-start | bytes 589832 | tf_op jit(solution)/shard_map/ppermute | solution.py:75
  115.2 3.9 %collective-permute-start.18 = (f32[8,832]{1,0:T(8,128)S(1)}, f32[8,832]{1,0:T(8,128)S(1)}, u32[]{:S(2)}, u32[]{:S(2)}) collective-permute-start(f32[8,832]{1,0:T(8,128)S(1)} %pad_maximum_fusion.3), channel_id=1, source_target_pairs={{0,8},{8,0},{16,24},{24,16},{1,9},{9,1},{17,25},{25,17},{2,10},{10... | collective-permute-start | bytes 79880 | tf_op jit(solution)/shard_map/ppermute | solution.py:201
  119.1 3.9 %collective-permute-start.19 = (f32[8,832]{1,0:T(8,128)S(1)}, f32[8,832]{1,0:T(8,128)S(1)}, u32[]{:S(2)}, u32[]{:S(2)}) collective-permute-start(f32[8,832]{1,0:T(8,128)S(1)} %fusion.44), channel_id=1, source_target_pairs={{0,16},{8,24},{16,0},{24,8},{1,17},{9,25},{17,1},{25,9},{2,18},{10... | collective-permute-start | bytes 79880 | tf_op jit(solution)/shard_map/ppermute | solution.py:201
  123.0 1.3 %collective-permute-start.20 = (f32[8,832]{1,0:T(8,128)S(1)}, f32[8,832]{1,0:T(8,128)S(1)}, u32[]{:S(2)}, u32[]{:S(2)}) collective-permute-start(f32[8,832]{1,0:T(8,128)S(1)} %add.142), channel_id=1, source_target_pairs={{0,4},{4,0},{1,5},{5,1},{2,6},{6,2},{3,7},{7,3},{8,12},{12,8},{9,1... | collective-permute-start | bytes 79880 | tf_op jit(solution)/shard_map/ppermute | solution.py:202

commit v2 on v1

v2 whole, which is shorter than its diff:
```python
import functools

import jax
import jax.numpy as jnp
from jax import lax
from jax.experimental import pallas as pl
from jax.experimental.pallas import tpu as pltpu
from jax.sharding import PartitionSpec as P

ADAPTER_SCALE = 0.25
LANES = 128
F32 = jnp.float32
BF16 = jnp.bfloat16
SMEM = pl.BlockSpec(memory_space=pltpu.SMEM)
VMEM = pl.BlockSpec(memory_space=pltpu.VMEM)
HBM = pl.BlockSpec(memory_space=pltpu.HBM)
EXACT = lax.Precision.HIGHEST


def params(mebibytes=16):
    return pltpu.CompilerParams(vmem_limit_bytes=mebibytes * 1024 * 1024)


def cost(flops, bytes_accessed):
    return pl.CostEstimate(flops=flops, bytes_accessed=bytes_accessed, transcendentals=0)


def in_hbm(value):
    return pltpu.with_memory_space_constraint(value, pltpu.HBM)


def whole(shape):
    return pl.BlockSpec(shape, lambda *_: (0,) * len(shape))


def contract(a, b, dim_a, dim_b, precision=None):
    return lax.dot_general(
        a, b, (((dim_a,), (dim_b,)), ((), ())), precision=precision, preferred_element_type=F32
    )


def xor_pairs(count, bits):
    return [(i, i ^ bits) for i in range(count)]


def feature_block(ref, place, k, width):
    start = pl.multiple_of((place[0] ^ k) * width, LANES)
    return ref[:, pl.ds(start, width)]


def route_kernel(
    place, scores_hbm, choice_hbm, grad_hbm, rows_ref, slots_ref, info_ref,
    scores_ref, choice_ref, grad_ref, sems,
):
    load_scores = pltpu.make_async_copy(scores_hbm, scores_ref, sems.at[0])
    load_choice = pltpu.make_async_copy(choice_hbm, choice_ref, sems.at[1])
    load = pltpu.make_async_copy(grad_hbm, grad_ref, sems.at[2])
    load_scores.start()
    load_choice.start()
    load.start()
    load_scores.wait()
    load_choice.wait()
    scores = scores_ref[...]
    experts, tokens = scores.shape
    shards, capacity, width = rows_ref.shape
    first_choice = choice_ref[0:1, :]
    second_choice = choice_ref[1:2, :]
    labels = lax.broadcasted_iota(jnp.int32, (experts, tokens), 0)
    chosen_first = jnp.sum(jnp.where(labels == first_choice, scores, 0.0), axis=0, keepdims=True)
    chosen_second = jnp.sum(jnp.where(labels == second_choice, scores, 0.0), axis=0, keepdims=True)
    first_prob = 1.0 / (1.0 + jnp.exp(chosen_second - chosen_first))
    second_prob = 1.0 - first_prob
    in_first = (first_choice == 0).astype(F32)
    in_second = (second_choice == 0).astype(F32)
    flags = jnp.broadcast_to(in_first + in_second, (capacity, tokens))
    row = lax.broadcasted_iota(jnp.int32, (tokens, tokens), 0)
    column = lax.broadcasted_iota(jnp.int32, (tokens, tokens), 1)
    before = (row < column).astype(F32).astype(BF16)
    slot = jnp.dot(flags.astype(BF16), before, preferred_element_type=F32)
    number = lax.broadcasted_iota(jnp.int32, (capacity, tokens), 0).astype(F32)
    slots = jnp.where((flags > 0.5) & (slot == number), 1.0, 0.0)
    slots_ref[...] = slots
    sign = (labels == first_choice).astype(F32) - (labels == second_choice).astype(F32)
    info_ref[:experts] = first_prob * second_prob * (in_first - in_second) * sign
    window_prob = jnp.where(in_first > 0.5, first_prob, second_prob)
    info_ref[experts:] = jnp.broadcast_to(window_prob, (info_ref.shape[0] - experts, tokens))
    picks = slots.astype(BF16)
    load.wait()
    for k in range(shards):
        block = feature_block(grad_ref, place, k, width)
        rows_ref[k] = jnp.dot(picks, block, preferred_element_type=F32).astype(BF16)


def route(place, scores, choice, grad, capacity, shards):
    tokens, features = grad.shape
    return pl.pallas_call(
        route_kernel,
        out_shape=(
            jax.ShapeDtypeStruct((shards, capacity, features // shards), BF16),
            jax.ShapeDtypeStruct((capacity, tokens), F32),
            jax.ShapeDtypeStruct((2 * scores.shape[1], tokens), F32),
        ),
        in_specs=[SMEM, HBM, HBM, HBM],
        out_specs=(VMEM,) * 3,
        scratch_shapes=[
            pltpu.VMEM(scores.T.shape, F32),
            pltpu.VMEM(choice.T.shape, jnp.int32),
            pltpu.VMEM(grad.shape, BF16),
            pltpu.SemaphoreType.DMA((3,)),
        ],
        compiler_params=params(),
        cost_estimate=cost(2 * tokens * capacity * features, 2 * tokens * features),
        name="route",
    )(place, in_hbm(scores.T), in_hbm(choice.T), in_hbm(grad))


def product_kernel(half, place, rows_ref, weight_ref, *refs):
    outs, lhs = refs[-5:-1], refs[-1]
    shards, capacity, _ = rows_ref.shape
    is_end = place[3]
    order = (1 + 2 * is_end, 2, 3 - 2 * is_end, 0)
    for slot, k in enumerate(order):
        lhs[slot * capacity : (slot + 1) * capacity] = rows_ref[k]
    rows = slice(half * capacity, (half + 1) * capacity)
    tile = 512
    for t in range(weight_ref.shape[1] // tile):
        part = slice(t * tile, (t + 1) * tile)
        result = jnp.dot(lhs[...], weight_ref[:, part], preferred_element_type=F32)
        for slot, ref in enumerate(outs):
            ref[rows, part] = result[slot * capacity : (slot + 1) * capacity].astype(ref.dtype)


def products(place, rows, weight, before=()):
    shards, capacity, width = rows.shape
    hidden = weight.shape[1]
    sent = pltpu.VMEM((2 * capacity, hidden), BF16)
    return pl.pallas_call(
        functools.partial(product_kernel, len(before) // 4),
        out_shape=(sent, sent, sent, pltpu.VMEM((2 * capacity, hidden), F32)),
        in_specs=[SMEM, VMEM, VMEM] + [VMEM] * len(before),
        out_specs=(VMEM,) * 4,
        input_output_aliases={3 + i: i for i in range(len(before))},
        scratch_shapes=[pltpu.VMEM((shards * capacity, width), BF16)],
        compiler_params=params(),
        cost_estimate=cost(2 * shards * capacity * width * hidden, 2 * width * hidden),
        name="products",
    )(place, rows, pltpu.with_memory_space_constraint(weight, pltpu.VMEM), *before)


def forward_kernel(place, far_ref, near_ref, out_ref):
    keep = 1.0 - place[3].astype(F32)
    out_ref[...] = (far_ref[...].astype(F32) + keep * near_ref[...].astype(F32)).astype(BF16)


def add_near(place, far, near):
    return pl.pallas_call(
        forward_kernel,
        out_shape=pltpu.VMEM(far.shape, BF16),
        in_specs=[SMEM, VMEM, VMEM],
        out_specs=VMEM,
        compiler_params=params(),
        cost_estimate=cost(2 * far.size, 6 * far.size),
        name="add_near",
    )(place, far, near)


def weight_kernel(codes_hbm, scales_hbm, weight_ref, codes_ref, scales_ref, scale_sem, sems):
    load_scales = pltpu.make_async_copy(scales_hbm, scales_ref, scale_sem)
    load_scales.start()
    tiles = sems.shape[0]
    tile = codes_ref.shape[1] // tiles
    loads = []
    for t in range(tiles):
        part = pl.ds(t * tile, tile)
        loads.append(
            pltpu.make_async_copy(codes_hbm.at[:, part], codes_ref.at[:, part], sems.at[t])
        )
        loads[t].start()
    blocks = scales_ref.shape[0]
    size = codes_ref.shape[0] // blocks
    load_scales.wait()
    for t in range(tiles):
        loads[t].wait()
        part = slice(t * tile, (t + 1) * tile)
        for b in range(blocks):
            rows = slice(b * size, (b + 1) * size)
            weight_ref[rows, part] = codes_ref[rows, part] * scales_ref[b : b + 1, part]


def dequantize(codes, scales, tiles):
    return pl.pallas_call(
        weight_kernel,
        out_shape=pltpu.VMEM(codes.shape, BF16),
        in_specs=[HBM, HBM],
        out_specs=VMEM,
        scratch_shapes=[
            pltpu.VMEM(codes.shape, BF16),
            pltpu.VMEM(scales.shape, BF16),
            pltpu.SemaphoreType.DMA,
            pltpu.SemaphoreType.DMA((tiles,)),
        ],
        compiler_params=params(),
        cost_estimate=cost(codes.size, 4 * codes.size),
        name="dequantize",
    )(in_hbm(codes), in_hbm(scales))


def adapter_kernel(
    place, grad_hbm, context_hbm, down_hbm, up_hbm, router_hbm, slots_ref, info_ref,
    early_ref, picked_ref, mixed_ref,
    grad_ref, context_ref, down_ref, up_ref, router_ref, sems,
):
    pairs = (
        (context_hbm, context_ref),
        (down_hbm, down_ref),
        (grad_hbm, grad_ref),
        (up_hbm, up_ref),
        (router_hbm, router_ref),
    )
    loads = [
        pltpu.make_async_copy(source, target, sems.at[i])
        for i, (source, target) in enumerate(pairs)
    ]
    for load in loads:
        load.start()
    groups, shards, rows, width = early_ref.shape
    capacity = picked_ref.shape[0]
    features = shards * width
    half = groups // 2
    loads[0].wait()
    loads[1].wait()
    low_in = contract(context_ref[...], down_ref[...], 1, 1).astype(BF16)
    for load in loads[2:]:
        load.wait()
    low_grad = (ADAPTER_SCALE * contract(grad_ref[...], up_ref[...], 1, 1)).astype(BF16)
    mixed_ref[...] = ADAPTER_SCALE * contract(up_ref[...], router_ref[...], 1, 1)
    slots = slots_ref[...].astype(BF16)
    for k in range(shards):
        grad = feature_block(grad_ref, place, k, width)
        context = feature_block(context_ref, place, k, width)
        up = ADAPTER_SCALE * contract(low_in, grad, 0, 0)
        down = contract(low_grad, context, 0, 0)
        for g in range(half):
            early_ref[g ^ place[1], k] = up[g * rows : (g + 1) * rows]
            early_ref[(g + half) ^ place[1], k] = down[g * rows : (g + 1) * rows]
        picked_ref[:, k * width : (k + 1) * width] = jnp.dot(
            slots, context, preferred_element_type=F32
        ).astype(BF16)
    low = jnp.dot(slots, low_in, preferred_element_type=F32).astype(BF16)
    picked_ref[:, features:] = jnp.zeros((capacity, 2 * LANES), BF16)
    picked_ref[:, features : features + low.shape[1]] = low
    info = contract(slots_ref[...], info_ref[...], 1, 1, EXACT)
    picked_ref[:, features + LANES : features + LANES + info.shape[1]] = info.astype(BF16)


def adapter_early(place, grad, context, down, up, router, slots, info, groups, shards):
    tokens, features = grad.shape
    rank = up.shape[0]
    rows = 2 * rank // groups
    arrays = (grad, context, down, up, router)
    return pl.pallas_call(
        adapter_kernel,
        out_shape=(
            jax.ShapeDtypeStruct((groups, shards, rows, features // shards), F32),
            jax.ShapeDtypeStruct((slots.shape[0], features + 2 * LANES), BF16),
            jax.ShapeDtypeStruct((rank, router.shape[0]), F32),
        ),
        in_specs=[SMEM] + [HBM] * 5 + [VMEM] * 2,
        out_specs=(VMEM,) * 3,
        scratch_shapes=[pltpu.VMEM(value.shape, BF16) for value in arrays]
        + [pltpu.SemaphoreType.DMA((5,))],
        compiler_params=params(),
        cost_estimate=cost(0, 0),
        name="adapter_early",
    )(place, *[in_hbm(value) for value in arrays], slots, info)


def finish_kernel(
    experts, place, own_ref, near_ref, middle_ref, far_ref, outer_ref, hidden_ref, picked_ref, other_ref,
    grad_hbm, prob_ref, prob_other_ref, late_ref, grad_ref, sems,
):
    shards, _, late_width = late_ref.shape
    width = late_width - LANES
    features = shards * width
    is_end = place[3].astype(F32)
    tiles = sems.shape[0]
    hidden = far_ref.shape[1]
    tile = hidden // tiles

    def store(t):
        part = pl.ds(t * tile, tile)
        return pltpu.make_async_copy(grad_ref.at[:, part], grad_hbm.at[:, part], sems.at[t])

    capacity = picked_ref.shape[0]
    pickeds = (picked_ref, other_ref)
    infos = [ref[:, features + LANES :].astype(F32) for ref in pickeds]
    totals = [jnp.zeros((capacity, LANES), F32) for _ in pickeds]
    for t in range(tiles):
        part = slice(t * tile, (t + 1) * tile)
        for half, info in enumerate(infos):
            rows = slice(half * capacity, (half + 1) * capacity)
            whole_rows = pl.ds(pl.multiple_of((place[2] ^ half) * capacity, capacity), capacity)
            product = (
                own_ref[rows, part]
                + is_end * near_ref[rows, part].astype(F32)
                + far_ref[rows, part].astype(F32)
                + (1.0 - is_end)
                * (middle_ref[rows, part].astype(F32) + outer_ref[rows, part].astype(F32))
            )
            grad_ref[whole_rows, part] = (info[:, experts : experts + 1] * product).astype(BF16)
            weighted = hidden_ref[whole_rows, part].astype(F32) * product
            for j in range(tile // LANES):
                totals[half] = totals[half] + weighted[:, j * LANES : (j + 1) * LANES]
        store(t).start()
    diagonal = lax.broadcasted_iota(jnp.int32, (capacity, capacity), 0) == lax.broadcasted_iota(
        jnp.int32, (capacity, capacity), 1
    )
    lane = lax.broadcasted_iota(jnp.int32, (capacity, LANES), 1)
    logits = []
    for info, total, out in zip(infos, totals, (prob_ref, prob_other_ref), strict=True):
        prob = jnp.sum(total, axis=1, keepdims=True)
        flat = jnp.sum(jnp.where(diagonal, prob, 0.0), axis=0, keepdims=True)
        out[...] = jnp.broadcast_to(flat, out.shape)
        logits.append(jnp.where(lane < experts, info * prob, 0.0).astype(BF16))

    def late(columns):
        return sum(
            contract(logit, ref[:, columns], 0, 0)[:experts]
            for logit, ref in zip(logits, pickeds, strict=True)
        )

    low = late(slice(features, features + LANES))
    for k in range(shards):
        late_ref[k, :, :width] = late(slice(k * width, (k + 1) * width))
        late_ref[k, :, width:] = low
    for t in range(tiles):
        store(t).wait()


def finish(place, own, near, middle, far, outer, hidden_state, picked, other, experts, shards, tiles):
    rows, hidden = far.shape
    capacity = picked.shape[0]
    width = (picked.shape[1] - 2 * LANES) // shards
    return pl.pallas_call(
        functools.partial(finish_kernel, experts),
        out_shape=(
            jax.ShapeDtypeStruct((rows, hidden), BF16),
            jax.ShapeDtypeStruct((8, capacity), F32),
            jax.ShapeDtypeStruct((8, capacity), F32),
            jax.ShapeDtypeStruct((shards, experts, width + LANES), F32),
        ),
        in_specs=[SMEM] + [VMEM] * 8,
        out_specs=(HBM, VMEM, VMEM, VMEM),
        scratch_shapes=[pltpu.VMEM((rows, hidden), BF16), pltpu.SemaphoreType.DMA((tiles,))],
        compiler_params=params(),
        cost_estimate=cost(8 * rows * hidden, 10 * rows * hidden),
        name="finish",
    )(place, own, near, middle, far, outer, hidden_state, picked, other)


def token_kernel(prob_ref, prob_got_ref, slots_ref, info_ref, router_ref, token_hbm, token_ref, sems):
    experts = router_ref.shape[0]
    own = prob_ref[...] + prob_got_ref[...]
    window = jnp.dot(own, slots_ref[...], precision=EXACT, preferred_element_type=F32)[0:1]
    logits = (info_ref[:experts] * window).astype(BF16)
    tiles = sems.shape[0]
    tile = token_ref.shape[1] // tiles
    stores = []
    for t in range(tiles):
        part = pl.ds(t * tile, tile)
        token_ref[:, part] = contract(logits, router_ref[:, part], 0, 0).astype(BF16)
        store = pltpu.make_async_copy(token_ref.at[:, part], token_hbm.at[:, part], sems.at[t])
        store.start()
        stores.append(store)
    for store in stores:
        store.wait()


def token_gradient(prob, prob_got, slots, info, router, tiles):
    tokens = slots.shape[1]
    features = router.shape[1]
    return pl.pallas_call(
        token_kernel,
        out_shape=jax.ShapeDtypeStruct((tokens, features), BF16),
        in_specs=[VMEM] * 5,
        out_specs=HBM,
        scratch_shapes=[pltpu.VMEM((tokens, features), BF16), pltpu.SemaphoreType.DMA((tiles,))],
        compiler_params=params(),
        cost_estimate=cost(2 * tokens * features * router.shape[0], 2 * tokens * features),
        name="token_gradient",
    )(prob, prob_got, slots, info, router)


def adapter_late_kernel(place, early_ref, late_ref, mixed_ref, router_ref, down_ref, up_ref):
    groups, rows, _ = early_ref.shape
    half = groups // 2
    rank, width = up_ref.shape
    router = feature_block(router_ref, place, 0, width).astype(F32)
    up = ADAPTER_SCALE * contract(late_ref[:, width : width + rank], router, 0, 0, EXACT)
    down = jnp.dot(
        mixed_ref[...], late_ref[:, :width], precision=EXACT, preferred_element_type=F32
    )
    for g in range(half):
        part = slice(g * rows, (g + 1) * rows)
        up_ref[part] = early_ref[g ^ place[1], :, :width].astype(F32) + up[part]
        down_ref[part] = early_ref[(g + half) ^ place[1], :, :width].astype(F32) + down[part]


def adapter_late(place, early, late, mixed, router):
    groups, rows, width = early.shape
    out = jax.ShapeDtypeStruct((groups * rows // 2, width - LANES), F32)
    return pl.pallas_call(
        adapter_late_kernel,
        out_shape=(out, out),
        in_specs=[SMEM] + [VMEM] * 4,
        out_specs=(whole(out.shape),) * 2,
        compiler_params=params(),
        cost_estimate=cost(64 * groups * rows * width, 8 * groups * rows * width),
        name="adapter_late",
    )(place, early, late, mixed, router)


def swap(value, axis, count, bits):
    return lax.ppermute(value, axis, xor_pairs(count, bits))


def after(value, *others):
    return lax.optimization_barrier((value,) + others)[0]


def direct_device(
    output_gradient,
    saved_router_scores,
    expert_choice_index,
    router_matrix,
    weight_normalized_entries,
    scales,
    stored_hidden_state,
    context,
    adapter_down_factor,
    adapter_up_factor,
):
    dp = lax.axis_index("dp")
    expert = lax.axis_index("expert")
    shard = lax.axis_index("shard")
    is_end = ((shard == 0) | (shard == 3)).astype(jnp.int32)
    group = expert * 4 + dp
    place = jnp.stack([shard, group, expert, is_end]).astype(jnp.int32)
    row_count, ff_share = stored_hidden_state.shape[2:]
    capacity = row_count // 2
    experts = saved_router_scores.shape[1]

    send_rows, slots, info = route(
        place, saved_router_scores, expert_choice_index, output_gradient, capacity, 4
    )
    rows = jnp.stack(
        [send_rows[0]] + [swap(send_rows[k], "shard", 4, k) for k in range(1, 4)]
    )
    weight = dequantize(weight_normalized_entries, scales, 4)
    rows, weight = lax.optimization_barrier((rows, weight))
    other_rows = swap(rows, "expert", 2, 1)

    partial = products(place, rows, weight)
    first, far, last, own = products(place, other_rows, weight, partial)
    near = swap(first, "shard", 4, 1)
    middle = lax.ppermute(last, "shard", [(1, 2), (2, 1)])
    early, picked, mixed = adapter_early(
        after(place, last), output_gradient, context, adapter_down_factor, adapter_up_factor,
        router_matrix, slots, info, 8, 4,
    )
    far, near, early, picked = lax.optimization_barrier((far, near, early, picked))
    forward = add_near(place, far, near)
    across = swap(forward, "shard", 4, 2)
    forward, last, middle = lax.optimization_barrier((forward, last, middle))
    outer = swap(last, "shard", 4, 1)
    forward, early, picked = lax.optimization_barrier((forward, early, picked))
    other_picked = swap(picked, "expert", 2, 1)
    early = early[:4] + swap(early[4:].astype(BF16), "expert", 2, 1).astype(F32)
    parts = early.astype(BF16)
    early = early[0] + sum(swap(parts[k], "dp", 4, k).astype(F32) for k in range(1, 4))
    across, early, other_picked = lax.optimization_barrier((across, early, other_picked))
    across, outer = lax.optimization_barrier((across, outer))

    hidden_grad, prob, prob_other, late = finish(
        place, own, near, middle, across, outer, stored_hidden_state[0, 0], picked, other_picked,
        experts, 4, 4,
    )
    early = jnp.pad(early, ((0, 0), (0, 0), (0, LANES)))
    late = jnp.concatenate([late, early], 1)
    late = late[:2] + swap(late[2:].astype(BF16), "shard", 4, 2).astype(F32)
    prob_got = swap(prob_other, "expert", 2, 1)
    late = late[0] + swap(late[1].astype(BF16), "shard", 4, 1).astype(F32)
    late, early = late[:experts], late[experts:].astype(BF16)
    mine = jnp.concatenate([late.astype(BF16), early], 0)
    got = [swap(mine, "dp", 4, k) for k in range(1, 4)]
    token_grad = token_gradient(prob, prob_got, slots, info, router_matrix, 4)
    late = late + sum(other[:experts].astype(F32) for other in got)
    early = jnp.concatenate([early] + [other[experts:] for other in got], 0)
    got = swap(jnp.concatenate([late.astype(BF16), early], 0), "expert", 2, 1)
    late = late + got[:experts].astype(F32)
    early = jnp.concatenate([early, got[experts:]], 0)
    early = early.reshape(8, -1, early.shape[1])
    grad_down, up_factor_gradient = adapter_late(place, early, late, mixed, router_matrix)
    return (
        hidden_grad.reshape(stored_hidden_state.shape),
        token_grad,
        grad_down,
        up_factor_gradient,
    )


def route_general(saved_router_scores, expert_choice_index, capacity):
    experts = saved_router_scores.shape[1]
    labels = jnp.arange(experts, dtype=jnp.int32)
    choose = expert_choice_index[:, :, None] == labels[None, None, :]
    chosen = jnp.sum(jnp.where(choose, saved_router_scores[:, None, :], 0.0), axis=2)
    first_prob = 1.0 / (1.0 + jnp.exp(chosen[:, 1] - chosen[:, 0]))
    second_prob = 1.0 - first_prob
    in_window = expert_choice_index == 0
    window_flag = jnp.any(in_window, axis=1)
    flag_int = window_flag.astype(jnp.int32)
    slot_index = jnp.cumsum(flag_int) - flag_int
    route_probs = jnp.stack([first_prob, second_prob], axis=1).astype(jnp.bfloat16)
    window_prob = jnp.where(in_window[:, 0], route_probs[:, 0], route_probs[:, 1])
    slot_labels = jnp.arange(capacity, dtype=jnp.int32)
    placement = window_flag[None, :] & (slot_index[None, :] == slot_labels[:, None])
    window_sign = in_window[:, 0].astype(jnp.float32) - in_window[:, 1].astype(jnp.float32)
    sign_table = choose[:, 0, :].astype(jnp.float32) - choose[:, 1, :].astype(jnp.float32)
    factors = (first_prob * second_prob * window_sign)[:, None] * sign_table
    return placement, window_prob, factors


def general_device(
    output_gradient,
    saved_router_scores,
    expert_choice_index,
    router_matrix,
    weight_normalized_entries,
    scales,
    stored_hidden_state,
    context,
    adapter_down_factor,
    adapter_up_factor,
):
    expert_count = lax.axis_size("expert")
    shard_count = lax.axis_size("shard")
    expert = lax.axis_index("expert")
    shard = lax.axis_index("shard")
    tokens, feature_width = output_gradient.shape
    row_count = stored_hidden_state.shape[2]
    capacity = row_count // expert_count
    ff_share = stored_hidden_state.shape[3]
    share_width = feature_width // shard_count
    block_size = weight_normalized_entries.shape[0] // scales.shape[0]
    rank = adapter_up_factor.shape[0]

    placement, window_prob, factors = route_general(saved_router_scores, expert_choice_index, capacity)
    placed = placement.astype(jnp.bfloat16)
    send_rows = jnp.dot(placed, output_gradient, preferred_element_type=jnp.float32).astype(
        jnp.bfloat16
    )
    send_probs = jnp.dot(placed, window_prob, preferred_element_type=jnp.float32).astype(
        jnp.bfloat16
    )
    blocks = lax.all_to_all(
        send_rows.reshape(capacity, shard_count, share_width).transpose(1, 0, 2), "shard", 0, 0
    )
    gathered = lax.all_gather(blocks, "expert", axis=1)
    all_probs = lax.all_gather(send_probs, "expert", axis=0, tiled=True)

    code_blocks = weight_normalized_entries.reshape(scales.shape[0], block_size, ff_share)
    own_weight = (code_blocks * scales[:, None, :]).reshape(
        weight_normalized_entries.shape[0], ff_share
    )
    product = jnp.dot(
        gathered.reshape(shard_count * row_count, share_width),
        own_weight,
        preferred_element_type=jnp.float32,
    ).reshape(shard_count, row_count, ff_share)

    narrow_input = lax.dot_general(
        context, adapter_down_factor, (((1,), (1,)), ((), ())), preferred_element_type=jnp.float32
    ).astype(jnp.bfloat16)
    narrow_gradient = (
        ADAPTER_SCALE
        * lax.dot_general(
            output_gradient,
            adapter_up_factor,
            (((1,), (1,)), ((), ())),
            preferred_element_type=jnp.float32,
        )
    ).astype(jnp.bfloat16)
    early_up = ADAPTER_SCALE * lax.dot_general(
        narrow_input, output_gradient, (((0,), (0,)), ((), ())), preferred_element_type=jnp.float32
    )
    early_down = lax.dot_general(
        narrow_gradient, context, (((0,), (0,)), ((), ())), preferred_element_type=jnp.float32
    )
    early = jnp.concatenate([early_up, early_down], 0)

    total = lax.psum_scatter(product.astype(jnp.bfloat16), "shard", scatter_dimension=0)
    total = total.astype(jnp.float32)
    early = lax.psum(early, ("dp", "expert"))
    early = lax.psum_scatter(early, "shard", scatter_dimension=1, tiled=True)

    hidden_grad = (all_probs.astype(jnp.float32)[:, None] * total).astype(jnp.bfloat16)
    partial_value = jnp.sum(stored_hidden_state[0, 0].astype(jnp.float32) * total, axis=1)
    slot_grad = lax.psum(partial_value, "expert")
    own_grad = lax.dynamic_slice_in_dim(slot_grad, expert * capacity, capacity, 0)
    window_grad = jnp.sum(jnp.where(placement, own_grad[:, None], 0.0), axis=0)
    logit_grad = (factors * window_grad[:, None]).astype(jnp.bfloat16)
    token_grad = jnp.dot(logit_grad, router_matrix, preferred_element_type=jnp.float32).astype(
        jnp.bfloat16
    )
    late_input = lax.dot_general(
        logit_grad, narrow_input, (((0,), (0,)), ((), ())), preferred_element_type=jnp.float32
    )
    late_context = lax.dot_general(
        logit_grad, context, (((0,), (0,)), ((), ())), preferred_element_type=jnp.float32
    )
    late_input = lax.psum(late_input, ("dp", "expert", "shard"))
    late_context = lax.psum(late_context, ("dp", "expert"))
    late_context = lax.psum_scatter(late_context, "shard", scatter_dimension=1, tiled=True)
    own_router = lax.dynamic_slice_in_dim(router_matrix, shard * share_width, share_width, 1)
    factor_router = ADAPTER_SCALE * lax.dot_general(
        adapter_up_factor, router_matrix, (((1,), (1,)), ((), ())), preferred_element_type=jnp.float32
    )
    up_factor_gradient = early[:rank] + ADAPTER_SCALE * lax.dot_general(
        late_input,
        own_router.astype(jnp.float32),
        (((0,), (0,)), ((), ())),
        precision=lax.Precision.HIGHEST,
        preferred_element_type=jnp.float32,
    )
    grad_down = early[rank:] + jnp.dot(
        factor_router,
        late_context,
        precision=lax.Precision.HIGHEST,
        preferred_element_type=jnp.float32,
    )
    return (
        hidden_grad.reshape(stored_hidden_state.shape),
        token_grad,
        grad_down,
        up_factor_gradient,
    )


def solution(mesh):
    axes = dict(mesh.shape)
    direct = (axes["dp"], axes["expert"], axes["shard"]) == (4, 2, 4)
    tokens_spec = P(("dp", "expert", "shard"), None)
    in_specs = (
        tokens_spec,
        tokens_spec,
        tokens_spec,
        P(),
        P("shard", "expert"),
        P("shard", "expert"),
        P("dp", "shard", None, "expert"),
        tokens_spec,
        P(),
        P(),
    )
    out_specs = (
        P("dp", "shard", None, "expert"),
        tokens_spec,
        P(None, "shard"),
        P(None, "shard"),
    )
    return jax.shard_map(
        direct_device if direct else general_device, mesh=mesh, in_specs=in_specs, out_specs=out_specs, check_vma=False
    )
```

time: 127 us -> 83.6 us (0.66)
  other arithmetic: 19.1 us -> 0.37 us
  Pallas kernels: 0 us -> 17.8 us
  matrix products: 15.5 us -> 0 us
  starting transfers between devices: 28.8 us -> 18.2 us
  local copies, waits for them, and re-layouts: 7.66 us -> 0.19 us
  blocking collectives: 7.14 us -> 0 us
    pallas_call x0 -> x9, Pallas kernels: none -> 17.8 us  [the longest x1 3.47 us: adapter_early(): pl.pallas_call(adapter_kernel, out_shape=(jax.ShapeDtypeStruct((groups, s...]
    dot_general x12 -> x0, matrix products: 15.5 us -> none  [the longest x1 6.64 us: per_device(): jnp.dot(gathered.reshape(shard_count * row_count, share_width), own_weigh...]
    ppermute x21 -> x20, starting transfers between devices: 28.8 us -> 18.2 us  [the longest x19 17.6 us: swap(): return lax.ppermute(value, axis, xor_pairs(count, bits))]
    mul x2 -> x0, other arithmetic: 6.65 us -> none  [the longest x1 5.9 us: per_device(): code_blocks * scales[:, None, :]]
    unnamed x35 -> x8, local copies, waits for them, and re-layouts: 5.95 us -> 0.06 us
    reduce_sum x4 -> x0, other arithmetic: 3.77 us -> none  [the longest x1 2.38 us: per_device(): jnp.sum(stored_hidden_state[0, 0].astype(jnp.float32) * total, axis=1)]
    psum x1 -> x0, blocking collectives: 2.47 us -> none  [per_device(): slot_grad = lax.psum(partial_value, 'expert')]
    unnamed x1 -> x0, blocking collectives: 2.45 us -> none
  transfers between devices with their start and end apart: 21 -> 20, of which waited for: 8 -> 13; matrix products, arithmetic and copies ran while one was open for 27% -> 0% of each run, Pallas kernels for 0% -> 12%
where the time goes in v2:
time: 83.6 us; the launch traced here: 83.4 us
  waiting for transfers between devices  45.9 us (55%)
  starting transfers between devices  18.2 us (22%)
  Pallas kernels  17.8 us (21%)
  between operations  0.92 us (1%)
    ppermute x19, waiting for transfers between devices, swap(): return lax.ppermute(value, axis, xor_pairs(count, bits))  45.9 us
    ppermute x19, starting transfers between devices, swap(): return lax.ppermute(value, axis, xor_pairs(count, bits))  17.6 us
    pallas_call x1, Pallas kernels, adapter_early(): pl.pallas_call(adapter_kernel, out_shape=(jax.ShapeDtypeStruct((groups, s...  3.47 us
    pallas_call x2, Pallas kernels, products(): pl.pallas_call(functools.partial(product_kernel, len(before) // 4), out_s...  3.07 us
    pallas_call x1, Pallas kernels, dequantize(): pl.pallas_call(weight_kernel, out_shape=pltpu.VMEM(codes.shape, BF16), in...  3.05 us
    pallas_call x1, Pallas kernels, finish(): pl.pallas_call(functools.partial(finish_kernel, experts), out_shape=(jax....  2.46 us
    pallas_call x1, Pallas kernels, route(): pl.pallas_call(route_kernel, out_shape=(jax.ShapeDtypeStruct((shards, cap...  1.99 us
    pallas_call x1, Pallas kernels, adapter_late(): pl.pallas_call(adapter_late_kernel, out_shape=(out, out), in_specs=[SMEM]...  1.74 us
  transfers between devices with their start and end apart: 20, of which 13 were waited for; matrix products, arithmetic and copies ran while one was open for 0% of the time, Pallas kernels for 12%

profile of v2, /device:TPU:0, one launch (start us, length us, event | category | flops | bytes accessed | tf_op | source)
XLA Modules:
  0.0 83.4 jit_solution(7958735086562131722)
XLA Ops:
  0.6 0.1 pad_add_fusion.place
  0.7 2.0 %route.1 = (bf16[4,32,768]{2,1,0:T(8,128)(2,1)S(1)}, f32[32,128]{1,0:T(8,128)S(1)}, f32[16,128]{1,0:T(8,128)S(1)}) custom-call(s32[4]{0:T(128)S(1)} %pad_add_fusion.place, f32[8,128]{1,0:T(8,128)} %bitcast.39, s32[2,128]{1,0:T(2,128)} %bitcast.40, bf16[128,3072]{1,0:T(8,128)(2,1)} %grad_hbm.3), custom_call_target="tpu_custom_call" | custom-call | flops 25165824 | bytes 786432 | tf_op jit(solution)/shard_map/route/pallas_call | solution.py:96
  2.7 5.1 %collective-permute-start.2 = (bf16[32,768]{1,0:T(8,128)(2,1)S(1)}, bf16[32,768]{1,0:T(8,128)(2,1)S(1)}, u32[]{:S(2)}, u32[]{:S(2)}) collective-permute-start(bf16[32,768]{1,0:T(8,128)(2,1)S(1)} %get-tuple-element.84), channel_id=1, source_target_pairs={{0,3},{1,2},{2,1},{3,0},{4,7},{5,6},{6,5},{7,4},{8,11},{9,10},{10,... | collective-permute-start | bytes 147464 | tf_op jit(solution)/shard_map/ppermute | solution.py:424
  7.9 0.0 collective-permute-start.1
  7.9 0.6 collective-permute-start
  8.5 3.1 %dequantize.1.weight_ref = bf16[768,4096]{1,0:T(8,128)(2,1)S(1)} custom-call(bf16[768,4096]{1,0:T(8,128)(2,1)} %codes_hbm.1, bf16[12,4096]{1,0:T(8,128)(2,1)} %scales_hbm.1), custom_call_target="tpu_custom_call" | custom-call | flops 3145728 | bytes 12582912 | tf_op jit(solution)/shard_map/dequantize/pallas_call | solution.py:191
  11.6 0.0 collective-permute-done.2
  11.6 1.3 %collective-permute-done.1 = bf16[32,768]{1,0:T(8,128)(2,1)S(1)} collective-permute-done((bf16[32,768]{1,0:T(8,128)(2,1)S(1)}, bf16[32,768]{1,0:T(8,128)(2,1)S(1)}, u32[]{:S(2)}, u32[]{:S(2)}) %collective-permute-start.1) | collective-permute-done | bytes 49184 | tf_op jit(solution)/shard_map/ppermute | solution.py:424
  12.8 0.0 collective-permute-done
  12.9 0.1 collective-permute-start.3
  13.0 1.5 %products.2 = (bf16[64,4096]{1,0:T(8,128)(2,1)S(1)}, bf16[64,4096]{1,0:T(8,128)(2,1)S(1)}, bf16[64,4096]{1,0:T(8,128)(2,1)S(1)}, f32[64,4096]{1,0:T(8,128)S(1)}) custom-call(s32[4]{0:T(128)S(1)} %pad_add_fusion.place, bf16[4,32,768]{2,1,0:T(8,128)(2,1)S(1)} %pad_maximum_fusion.rows_ref, bf16[768,4096]{1,0:T(8,128)(2,1)S(1)} %dequantize.1.weight_ref), custom_call_target="tpu_custom_call" | custom-call | flops 805306368 | bytes 6291456 | tf_op jit(solution)/shard_map/products/pallas_call | solution.py:137
  14.5 0.0 collective-permute-done.3.rows_ref
  14.5 1.5 %products.3 = (bf16[64,4096]{1,0:T(8,128)(2,1)S(1)}, bf16[64,4096]{1,0:T(8,128)(2,1)S(1)}, bf16[64,4096]{1,0:T(8,128)(2,1)S(1)}, f32[64,4096]{1,0:T(8,128)S(1)}) custom-call(s32[4]{0:T(128)S(1)} %pad_add_fusion.place, ...), custom_call_target="tpu_custom_call", output_to_operand_aliasing={{0}: (3, {}), {1}: (4, {}), {2}: (5, {}), {3}: (6, {})} | custom-call | flops 805306368 | bytes 6291456 | tf_op jit(solution)/shard_map/products/pallas_call | solution.py:137
  16.1 0.0 copy-start
  16.1 0.7 collective-permute-start.4
  16.8 0.7 collective-permute-start.5
  17.5 3.5 %adapter_early.1 = (f32[8,4,16,768]{3,2,1,0:T(8,128)S(1)}, bf16[32,3328]{1,0:T(8,128)(2,1)S(1)}, f32[64,8]{1,0:T(8,128)S(1)}) custom-call(s32[4]{0:T(128)S(1)} %pad_add_fusion.place, bf16[128,3072]{1,0:T(8,128)(2,1)} %grad_hbm.3, bf16[128,3072]{1,0:T(8,128)(2,1)} %context_hbm.1, bf16[64,3072]{1,0:T(8,128)(2,1)} %down_hbm.1, bf16[64,3072]{1,0:T(8,128)(2,1)} %up_hbm.1, ...), custom_call_target="tpu_custom_call" | custom-call | tf_op jit(solution)/shard_map/adapter_early/pallas_call | solution.py:261
  20.9 0.0 copy-start.1
  21.0 9.5 %collective-permute-done.4.near_ref = bf16[64,4096]{1,0:T(8,128)(2,1)S(1)} collective-permute-done((bf16[64,4096]{1,0:T(8,128)(2,1)S(1)}, bf16[64,4096]{1,0:T(8,128)(2,1)S(1)}, u32[]{:S(2)}, u32[]{:S(2)}) %collective-permute-start.4) | collective-permute-done | bytes 524320 | tf_op jit(solution)/shard_map/ppermute | solution.py:424
  30.5 0.1 collective-permute-start.7
  30.6 0.7 add_near.1
  31.3 2.1 %collective-permute-start.6 = (bf16[64,4096]{1,0:T(8,128)(2,1)S(1)}, bf16[64,4096]{1,0:T(8,128)(2,1)S(1)}, u32[]{:S(2)}, u32[]{:S(2)}) collective-permute-start(bf16[64,4096]{1,0:T(8,128)(2,1)S(1)} %add_near.1), channel_id=1, source_target_pairs={{0,2},{1,3},{2,0},{3,1},{4,6},{5,7},{6,4},{7,5},{8,10},{9,11},{10,... | collective-permute-start | bytes 1572872 | tf_op jit(solution)/shard_map/ppermute | solution.py:424
  33.4 0.0 collective-permute-done.5.middle_ref
  33.4 1.0 %collective-permute-start.12 = (bf16[64,4096]{1,0:T(8,128)(2,1)S(1)}, bf16[64,4096]{1,0:T(8,128)(2,1)S(1)}, u32[]{:S(2)}, u32[]{:S(2)}) collective-permute-start(bf16[64,4096]{1,0:T(8,128)(2,1)S(1)} %get-tuple-element.64), channel_id=1, source_target_pairs={{0,1},{1,0},{2,3},{3,2},{4,5},{5,4},{6,7},{7,6},{8,9},{9,8},{10,11... | collective-permute-start | bytes 1572872 | tf_op jit(solution)/shard_map/ppermute | solution.py:424
  34.4 0.0 collective-permute-done.7
  34.4 0.1 fusion.3
  34.6 1.6 %collective-permute-start.8 = (bf16[4,16,768]{2,1,0:T(8,128)(2,1)S(1)}, bf16[4,16,768]{2,1,0:T(8,128)(2,1)S(1)}, u32[]{:S(2)}, u32[]{:S(2)}) collective-permute-start(bf16[4,16,768]{2,1,0:T(8,128)(2,1)S(1)} %get-tuple-element.80), channel_id=1, source_target_pairs={{0,8},{8,0},{16,24},{24,16},{1,9},{9,1},{17,25},{25,17},{2,10},{10... | collective-permute-start | bytes 294920 | tf_op jit(solution)/shard_map/ppermute | solution.py:424
  36.1 1.5 %collective-permute-start.10 = (bf16[4,16,768]{2,1,0:T(8,128)(2,1)S(1)}, bf16[4,16,768]{2,1,0:T(8,128)(2,1)S(1)}, u32[]{:S(2)}, u32[]{:S(2)}) collective-permute-start(bf16[4,16,768]{2,1,0:T(8,128)(2,1)S(1)} %get-tuple-element.81), channel_id=1, source_target_pairs={{0,24},{8,16},{16,8},{24,0},{1,25},{9,17},{17,9},{25,1},{2,26},{10... | collective-permute-start | bytes 294920 | tf_op jit(solution)/shard_map/ppermute | solution.py:424
  37.6 0.5 collective-permute-start.9
  38.1 1.1 %collective-permute-done.8 = bf16[4,16,768]{2,1,0:T(8,128)(2,1)S(1)} collective-permute-done((bf16[4,16,768]{2,1,0:T(8,128)(2,1)S(1)}, bf16[4,16,768]{2,1,0:T(8,128)(2,1)S(1)}, u32[]{:S(2)}, u32[]{:S(2)}) %collective-permute-start.8) | collective-permute-done | bytes 98336 | tf_op jit(solution)/shard_map/ppermute | solution.py:424
  39.3 0.0 collective-permute-start.11
  39.3 3.2 %collective-permute-done.10 = bf16[4,16,768]{2,1,0:T(8,128)(2,1)S(1)} collective-permute-done((bf16[4,16,768]{2,1,0:T(8,128)(2,1)S(1)}, bf16[4,16,768]{2,1,0:T(8,128)(2,1)S(1)}, u32[]{:S(2)}, u32[]{:S(2)}) %collective-permute-start.10) | collective-permute-done | bytes 98336 | tf_op jit(solution)/shard_map/ppermute | solution.py:424
  42.4 1.2 %collective-permute-done.9 = bf16[4,16,768]{2,1,0:T(8,128)(2,1)S(1)} collective-permute-done((bf16[4,16,768]{2,1,0:T(8,128)(2,1)S(1)}, bf16[4,16,768]{2,1,0:T(8,128)(2,1)S(1)}, u32[]{:S(2)}, u32[]{:S(2)}) %collective-permute-start.9) | collective-permute-done | bytes 98336 | tf_op jit(solution)/shard_map/ppermute | solution.py:424
  43.7 0.0 collective-permute-done.11.other_ref
  43.7 14.2 %collective-permute-done.6.far_ref = bf16[64,4096]{1,0:T(8,128)(2,1)S(1)} collective-permute-done((bf16[64,4096]{1,0:T(8,128)(2,1)S(1)}, bf16[64,4096]{1,0:T(8,128)(2,1)S(1)}, u32[]{:S(2)}, u32[]{:S(2)}) %collective-permute-start.6) | collective-permute-done | bytes 524320 | tf_op jit(solution)/shard_map/ppermute | solution.py:424
  57.9 0.6 collective-permute-done.12.outer_ref
  58.5 0.0 copy-done
  58.5 2.5 %finish.1 = (bf16[64,4096]{1,0:T(8,128)(2,1)}, f32[8,32]{1,0:T(8,128)S(1)}, f32[8,32]{1,0:T(8,128)S(1)}, f32[4,8,896]{2,1,0:T(8,128)S(1)}) custom-call(s32[4]{0:T(128)S(1)} %pad_add_fusion.place, f32[64,4096]{1,0:T(8,128)S(1)} %get-tuple-element.47.own_ref, bf16[64,4096]{1,0:T(8,128)(2,1)S(1)} %collective-permute-done.4.near_ref, ...), custom_call_target="tpu_custom_call" | custom-call | flops 2097152 | bytes 2621440 | tf_op jit(solution)/shard_map/finish/pallas_call | solution.py:344
  61.0 0.1 collective-permute-start.14
  61.1 6.5 %collective-permute-done.14 = bf16[2,24,896]{2,1,0:T(8,128)(2,1)S(1)} collective-permute-done((bf16[2,24,896]{2,1,0:T(8,128)(2,1)S(1)}, bf16[2,24,896]{2,1,0:T(8,128)(2,1)S(1)}, u32[]{:S(2)}, u32[]{:S(2)}) %collective-permute-start.14) | collective-permute-done | bytes 86048 | tf_op jit(solution)/shard_map/ppermute | solution.py:424
  67.6 0.1 collective-permute-start.15
  67.7 4.0 %collective-permute-done.15 = bf16[24,896]{1,0:T(8,128)(2,1)S(1)} collective-permute-done((bf16[24,896]{1,0:T(8,128)(2,1)S(1)}, bf16[24,896]{1,0:T(8,128)(2,1)S(1)}, u32[]{:S(2)}, u32[]{:S(2)}) %collective-permute-start.15) | collective-permute-done | bytes 43040 | tf_op jit(solution)/shard_map/ppermute | solution.py:424
  71.7 2.5 %collective-permute-start.18 = (bf16[24,896]{1,0:T(8,128)(2,1)S(1)}, bf16[24,896]{1,0:T(8,128)(2,1)S(1)}, u32[]{:S(2)}, u32[]{:S(2)}) collective-permute-start(bf16[24,896]{1,0:T(8,128)(2,1)S(1)} %pad_maximum_fusion.1), channel_id=1, source_target_pairs={{0,24},{8,16},{16,8},{24,0},{1,25},{9,17},{17,9},{25,1},{2,26},{10... | collective-permute-start | bytes 129032 | tf_op jit(solution)/shard_map/ppermute | solution.py:424
  74.3 0.5 collective-permute-start.17
  74.8 0.5 collective-permute-start.16
  75.3 1.6 %collective-permute-done.18 = bf16[24,896]{1,0:T(8,128)(2,1)S(1)} collective-permute-done((bf16[24,896]{1,0:T(8,128)(2,1)S(1)}, bf16[24,896]{1,0:T(8,128)(2,1)S(1)}, u32[]{:S(2)}, u32[]{:S(2)}) %collective-permute-start.18) | collective-permute-done | bytes 43040 | tf_op jit(solution)/shard_map/ppermute | solution.py:424
  76.9 1.4 %collective-permute-done.17 = bf16[24,896]{1,0:T(8,128)(2,1)S(1)} collective-permute-done((bf16[24,896]{1,0:T(8,128)(2,1)S(1)}, bf16[24,896]{1,0:T(8,128)(2,1)S(1)}, u32[]{:S(2)}, u32[]{:S(2)}) %collective-permute-start.17) | collective-permute-done | bytes 43040 | tf_op jit(solution)/shard_map/ppermute | solution.py:424
  78.3 0.5 collective-permute-done.16
  78.9 0.1 collective-permute-start.19
  79.0 0.5 collective-permute-start.13
  79.5 0.8 %collective-permute-done.13.prob_got_ref = f32[8,32]{1,0:T(8,128)S(1)} collective-permute-done((f32[8,32]{1,0:T(8,128)S(1)}, f32[8,32]{1,0:T(8,128)S(1)}, u32[]{:S(2)}, u32[]{:S(2)}) %collective-permute-start.13) | collective-permute-done | bytes 1056 | tf_op jit(solution)/shard_map/ppermute | solution.py:424
  80.3 0.0 copy-done.1
  80.3 1.3 %token_gradient.1 = bf16[128,3072]{1,0:T(8,128)(2,1)} custom-call(f32[8,32]{1,0:T(8,128)S(1)} %get-tuple-element.69.prob_ref, f32[8,32]{1,0:T(8,128)S(1)} %collective-permute-done.13.prob_got_ref, f32[32,128]{1,0:T(8,128)S(1)} %get-tuple-element.52.slots_ref, f32[16,128]{1,0:T(8,128)S(1)} %get-tuple-element.53.info_ref, bf16[8,3072]{1,0:T(8,128)(2,1)S(1)} %copy-done.1), custom_call_target="tpu_custom_call" | custom-call | flops 6291456 | bytes 786432 | tf_op jit(solution)/shard_map/token_gradient/pallas_call | solution.py:382
  81.6 0.0 collective-permute-done.19
  81.7 1.7 %adapter_late.1 = (f32[64,768]{1,0:T(8,128)}, f32[64,768]{1,0:T(8,128)}) custom-call(s32[4]{0:T(128)S(1)} %pad_add_fusion.place, bf16[8,16,896]{2,1,0:T(8,128)(2,1)S(1)} %bitcast.35, f32[8,896]{1,0:T(8,128)S(1)} %convert_add_fusion.1.late_ref, f32[64,8]{1,0:T(8,128)S(1)} %get-tuple-element.73.mixed_ref, bf16[8,3072]{1,0:T(8,128)(2,1)S(1)} %copy-done.1), custom_call_target="tpu_custom_call" | custom-call | flops 7340032 | bytes 917504 | tf_op jit(solution)/shard_map/adapter_late/pallas_call | solution.py:412
  (20 shorter events, 0.4 us)
Async XLA Ops:
  2.7 8.8 %collective-permute-start.2 = (bf16[32,768]{1,0:T(8,128)(2,1)S(1)}, bf16[32,768]{1,0:T(8,128)(2,1)S(1)}, u32[]{:S(2)}, u32[]{:S(2)}) collective-permute-start(bf16[32,768]{1,0:T(8,128)(2,1)S(1)} %get-tuple-element.84), channel_id=1, source_target_pairs={{0,3},{1,2},{2,1},{3,0},{4,7},{5,6},{6,5},{7,4},{8,11},{9,10},{10,... | collective-permute-start | bytes 147464 | tf_op jit(solution)/shard_map/ppermute | solution.py:424
  7.9 5.0 %collective-permute-start.1 = (bf16[32,768]{1,0:T(8,128)(2,1)S(1)}, bf16[32,768]{1,0:T(8,128)(2,1)S(1)}, u32[]{:S(2)}, u32[]{:S(2)}) collective-permute-start(bf16[32,768]{1,0:T(8,128)(2,1)S(1)} %get-tuple-element.85), channel_id=1, source_target_pairs={{0,2},{1,3},{2,0},{3,1},{4,6},{5,7},{6,4},{7,5},{8,10},{9,11},{10,... | collective-permute-start | bytes 147464 | tf_op jit(solution)/shard_map/ppermute | solution.py:424
  7.9 5.0 %collective-permute-start = (bf16[32,768]{1,0:T(8,128)(2,1)S(1)}, bf16[32,768]{1,0:T(8,128)(2,1)S(1)}, u32[]{:S(2)}, u32[]{:S(2)}) collective-permute-start(bf16[32,768]{1,0:T(8,128)(2,1)S(1)} %get-tuple-element.86), channel_id=1, source_target_pairs={{0,1},{1,0},{2,3},{3,2},{4,5},{5,4},{6,7},{7,6},{8,9},{9,8},{10,11... | collective-permute-start | bytes 147464 | tf_op jit(solution)/shard_map/ppermute | solution.py:424
  12.9 1.6 %collective-permute-start.3 = (bf16[4,32,768]{2,1,0:T(8,128)(2,1)S(1)}, bf16[4,32,768]{2,1,0:T(8,128)(2,1)S(1)}, u32[]{:S(2)}, u32[]{:S(2)}) collective-permute-start(bf16[4,32,768]{2,1,0:T(8,128)(2,1)S(1)} %pad_maximum_fusion.rows_ref), channel_id=1, source_target_pairs={{0,4},{4,0},{1,5},{5,1},{2,6},{6,2},{3,7},{7,3},{8,12},{12,8},{9,1... | collective-permute-start | bytes 589832 | tf_op jit(solution)/shard_map/ppermute | solution.py:424
  16.1 42.4 %copy-start = (bf16[1,1,64,4096]{3,2,1,0:T(8,128)(2,1)S(1)}, bf16[1,1,64,4096]{3,2,1,0:T(8,128)(2,1)}, u32[]{:S(2)}) copy-start(bf16[1,1,64,4096]{3,2,1,0:T(8,128)(2,1)} %param.16) | copy-start | bytes 1572868
  16.1 14.4 %collective-permute-start.4 = (bf16[64,4096]{1,0:T(8,128)(2,1)S(1)}, bf16[64,4096]{1,0:T(8,128)(2,1)S(1)}, u32[]{:S(2)}, u32[]{:S(2)}) collective-permute-start(bf16[64,4096]{1,0:T(8,128)(2,1)S(1)} %get-tuple-element.49), channel_id=1, source_target_pairs={{0,1},{1,0},{2,3},{3,2},{4,5},{5,4},{6,7},{7,6},{8,9},{9,8},{10,11... | collective-permute-start | bytes 1572872 | tf_op jit(solution)/shard_map/ppermute | solution.py:424
  16.8 16.6 %collective-permute-start.5 = (bf16[64,4096]{1,0:T(8,128)(2,1)S(1)}, bf16[64,4096]{1,0:T(8,128)(2,1)S(1)}, u32[]{:S(2)}, u32[]{:S(2)}) collective-permute-start(bf16[64,4096]{1,0:T(8,128)(2,1)S(1)} %get-tuple-element.64), channel_id=1, source_target_pairs={{1,2},{2,1},{5,6},{6,5},{9,10},{10,9},{13,14},{14,13},{17,18},{18,... | collective-permute-start | bytes 1572872 | tf_op jit(solution)/shard_map/ppermute | solution.py:466
  20.9 59.4 %copy-start.1 = (bf16[8,3072]{1,0:T(8,128)(2,1)S(1)}, bf16[8,3072]{1,0:T(8,128)(2,1)}, u32[]{:S(2)}) copy-start(bf16[8,3072]{1,0:T(8,128)(2,1)} %router_ref.3) | copy-start | bytes 147460
  30.5 3.9 %collective-permute-start.7 = (bf16[4,4,16,768]{3,2,1,0:T(8,128)(2,1)S(1)}, bf16[4,4,16,768]{3,2,1,0:T(8,128)(2,1)S(1)}, u32[]{:S(2)}, u32[]{:S(2)}) collective-permute-start(bf16[4,4,16,768]{3,2,1,0:T(8,128)(2,1)S(1)} %slice.168), channel_id=1, source_target_pairs={{0,4},{4,0},{1,5},{5,1},{2,6},{6,2},{3,7},{7,3},{8,12},{12,8},{9,1... | collective-permute-start | bytes 1179656 | tf_op jit(solution)/shard_map/ppermute | solution.py:424
  31.3 26.6 %collective-permute-start.6 = (bf16[64,4096]{1,0:T(8,128)(2,1)S(1)}, bf16[64,4096]{1,0:T(8,128)(2,1)S(1)}, u32[]{:S(2)}, u32[]{:S(2)}) collective-permute-start(bf16[64,4096]{1,0:T(8,128)(2,1)S(1)} %add_near.1), channel_id=1, source_target_pairs={{0,2},{1,3},{2,0},{3,1},{4,6},{5,7},{6,4},{7,5},{8,10},{9,11},{10,... | collective-permute-start | bytes 1572872 | tf_op jit(solution)/shard_map/ppermute | solution.py:424
  33.4 25.1 %collective-permute-start.12 = (bf16[64,4096]{1,0:T(8,128)(2,1)S(1)}, bf16[64,4096]{1,0:T(8,128)(2,1)S(1)}, u32[]{:S(2)}, u32[]{:S(2)}) collective-permute-start(bf16[64,4096]{1,0:T(8,128)(2,1)S(1)} %get-tuple-element.64), channel_id=1, source_target_pairs={{0,1},{1,0},{2,3},{3,2},{4,5},{5,4},{6,7},{7,6},{8,9},{9,8},{10,11... | collective-permute-start | bytes 1572872 | tf_op jit(solution)/shard_map/ppermute | solution.py:424
  34.6 4.7 %collective-permute-start.8 = (bf16[4,16,768]{2,1,0:T(8,128)(2,1)S(1)}, bf16[4,16,768]{2,1,0:T(8,128)(2,1)S(1)}, u32[]{:S(2)}, u32[]{:S(2)}) collective-permute-start(bf16[4,16,768]{2,1,0:T(8,128)(2,1)S(1)} %get-tuple-element.80), channel_id=1, source_target_pairs={{0,8},{8,0},{16,24},{24,16},{1,9},{9,1},{17,25},{25,17},{2,10},{10... | collective-permute-start | bytes 294920 | tf_op jit(solution)/shard_map/ppermute | solution.py:424
  36.1 6.3 %collective-permute-start.10 = (bf16[4,16,768]{2,1,0:T(8,128)(2,1)S(1)}, bf16[4,16,768]{2,1,0:T(8,128)(2,1)S(1)}, u32[]{:S(2)}, u32[]{:S(2)}) collective-permute-start(bf16[4,16,768]{2,1,0:T(8,128)(2,1)S(1)} %get-tuple-element.81), channel_id=1, source_target_pairs={{0,24},{8,16},{16,8},{24,0},{1,25},{9,17},{17,9},{25,1},{2,26},{10... | collective-permute-start | bytes 294920 | tf_op jit(solution)/shard_map/ppermute | solution.py:424
  37.6 6.0 %collective-permute-start.9 = (bf16[4,16,768]{2,1,0:T(8,128)(2,1)S(1)}, bf16[4,16,768]{2,1,0:T(8,128)(2,1)S(1)}, u32[]{:S(2)}, u32[]{:S(2)}) collective-permute-start(bf16[4,16,768]{2,1,0:T(8,128)(2,1)S(1)} %get-tuple-element.82), channel_id=1, source_target_pairs={{0,16},{8,24},{16,0},{24,8},{1,17},{9,25},{17,1},{25,9},{2,18},{10... | collective-permute-start | bytes 294920 | tf_op jit(solution)/shard_map/ppermute | solution.py:424
  39.3 4.4 %collective-permute-start.11 = (bf16[32,3328]{1,0:T(8,128)(2,1)S(1)}, bf16[32,3328]{1,0:T(8,128)(2,1)S(1)}, u32[]{:S(2)}, u32[]{:S(2)}) collective-permute-start(bf16[32,3328]{1,0:T(8,128)(2,1)S(1)} %get-tuple-element.62.picked_ref), channel_id=1, source_target_pairs={{0,4},{4,0},{1,5},{5,1},{2,6},{6,2},{3,7},{7,3},{8,12},{12,8},{9,1... | collective-permute-start | bytes 638984 | tf_op jit(solution)/shard_map/ppermute | solution.py:424
  61.0 6.6 %collective-permute-start.14 = (bf16[2,24,896]{2,1,0:T(8,128)(2,1)S(1)}, bf16[2,24,896]{2,1,0:T(8,128)(2,1)S(1)}, u32[]{:S(2)}, u32[]{:S(2)}) collective-permute-start(bf16[2,24,896]{2,1,0:T(8,128)(2,1)S(1)} %slice.169), channel_id=1, source_target_pairs={{0,2},{1,3},{2,0},{3,1},{4,6},{5,7},{6,4},{7,5},{8,10},{9,11},{10,... | collective-permute-start | bytes 258056 | tf_op jit(solution)/shard_map/ppermute | solution.py:424
  67.6 4.1 %collective-permute-start.15 = (bf16[24,896]{1,0:T(8,128)(2,1)S(1)}, bf16[24,896]{1,0:T(8,128)(2,1)S(1)}, u32[]{:S(2)}, u32[]{:S(2)}) collective-permute-start(bf16[24,896]{1,0:T(8,128)(2,1)S(1)} %fusion.2), channel_id=1, source_target_pairs={{0,1},{1,0},{2,3},{3,2},{4,5},{5,4},{6,7},{7,6},{8,9},{9,8},{10,11... | collective-permute-start | bytes 129032 | tf_op jit(solution)/shard_map/ppermute | solution.py:424
  71.7 5.2 %collective-permute-start.18 = (bf16[24,896]{1,0:T(8,128)(2,1)S(1)}, bf16[24,896]{1,0:T(8,128)(2,1)S(1)}, u32[]{:S(2)}, u32[]{:S(2)}) collective-permute-start(bf16[24,896]{1,0:T(8,128)(2,1)S(1)} %pad_maximum_fusion.1), channel_id=1, source_target_pairs={{0,24},{8,16},{16,8},{24,0},{1,25},{9,17},{17,9},{25,1},{2,26},{10... | collective-permute-start | bytes 129032 | tf_op jit(solution)/shard_map/ppermute | solution.py:424
  74.3 4.0 %collective-permute-start.17 = (bf16[24,896]{1,0:T(8,128)(2,1)S(1)}, bf16[24,896]{1,0:T(8,128)(2,1)S(1)}, u32[]{:S(2)}, u32[]{:S(2)}) collective-permute-start(bf16[24,896]{1,0:T(8,128)(2,1)S(1)} %pad_maximum_fusion.1), channel_id=1, source_target_pairs={{0,16},{8,24},{16,0},{24,8},{1,17},{9,25},{17,1},{25,9},{2,18},{10... | collective-permute-start | bytes 129032 | tf_op jit(solution)/shard_map/ppermute | solution.py:424
  74.8 4.0 %collective-permute-start.16 = (bf16[24,896]{1,0:T(8,128)(2,1)S(1)}, bf16[24,896]{1,0:T(8,128)(2,1)S(1)}, u32[]{:S(2)}, u32[]{:S(2)}) collective-permute-start(bf16[24,896]{1,0:T(8,128)(2,1)S(1)} %pad_maximum_fusion.1), channel_id=1, source_target_pairs={{0,8},{8,0},{16,24},{24,16},{1,9},{9,1},{17,25},{25,17},{2,10},{10... | collective-permute-start | bytes 129032 | tf_op jit(solution)/shard_map/ppermute | solution.py:424
  78.9 2.7 %collective-permute-start.19 = (bf16[72,896]{1,0:T(8,128)(2,1)S(1)}, bf16[72,896]{1,0:T(8,128)(2,1)S(1)}, u32[]{:S(2)}, u32[]{:S(2)}) collective-permute-start(bf16[72,896]{1,0:T(8,128)(2,1)S(1)} %get-tuple-element.87), channel_id=1, source_target_pairs={{0,4},{4,0},{1,5},{5,1},{2,6},{6,2},{3,7},{7,3},{8,12},{12,8},{9,1... | collective-permute-start | bytes 387080 | tf_op jit(solution)/shard_map/ppermute | solution.py:424
  79.0 1.3 %collective-permute-start.13 = (f32[8,32]{1,0:T(8,128)S(1)}, f32[8,32]{1,0:T(8,128)S(1)}, u32[]{:S(2)}, u32[]{:S(2)}) collective-permute-start(f32[8,32]{1,0:T(8,128)S(1)} %get-tuple-element.70), channel_id=1, source_target_pairs={{0,4},{4,0},{1,5},{5,1},{2,6},{6,2},{3,7},{7,3},{8,12},{12,8},{9,1... | collective-permute-start | bytes 3080 | tf_op jit(solution)/shard_map/ppermute | solution.py:424

commit v3 on v2

--- a/solution.py
+++ b/solution.py
@@ -164,6 +164,27 @@
     )(place, far, near)
 
 
+def partial_kernel(place, own_ref, near_ref, middle_ref, out_ref):
+    is_end = place[3].astype(F32)
+    out_ref[...] = (
+        own_ref[...]
+        + is_end * near_ref[...].astype(F32)
+        + (1.0 - is_end) * middle_ref[...].astype(F32)
+    )
+
+
+def add_first(place, own, near, middle):
+    return pl.pallas_call(
+        partial_kernel,
+        out_shape=pltpu.VMEM(own.shape, F32),
+        in_specs=[SMEM] + [VMEM] * 3,
+        out_specs=VMEM,
+        compiler_params=params(),
+        cost_estimate=cost(0, 0),
+        name="add_first",
+    )(place, own, near, middle)
+
+
 def weight_kernel(codes_hbm, scales_hbm, weight_ref, codes_ref, scales_ref, scale_sem, sems):
     load_scales = pltpu.make_async_copy(scales_hbm, scales_ref, scale_sem)
     load_scales.start()
@@ -276,42 +297,33 @@
 
 
 def finish_kernel(
-    experts, place, own_ref, near_ref, middle_ref, far_ref, outer_ref, hidden_ref, picked_ref, other_ref,
-    grad_hbm, prob_ref, prob_other_ref, late_ref, grad_ref, sems,
+    experts, place, partial_ref, far_ref, outer_ref, hidden_ref, picked_ref, other_ref,
+    product_ref, prob_ref, prob_other_ref, late_ref,
 ):
     shards, _, late_width = late_ref.shape
     width = late_width - LANES
     features = shards * width
     is_end = place[3].astype(F32)
-    tiles = sems.shape[0]
     hidden = far_ref.shape[1]
-    tile = hidden // tiles
-
-    def store(t):
-        part = pl.ds(t * tile, tile)
-        return pltpu.make_async_copy(grad_ref.at[:, part], grad_hbm.at[:, part], sems.at[t])
-
+    tile = 512
     capacity = picked_ref.shape[0]
     pickeds = (picked_ref, other_ref)
     infos = [ref[:, features + LANES :].astype(F32) for ref in pickeds]
     totals = [jnp.zeros((capacity, LANES), F32) for _ in pickeds]
-    for t in range(tiles):
+    for t in range(hidden // tile):
         part = slice(t * tile, (t + 1) * tile)
-        for half, info in enumerate(infos):
+        for half in range(2):
             rows = slice(half * capacity, (half + 1) * capacity)
             whole_rows = pl.ds(pl.multiple_of((place[2] ^ half) * capacity, capacity), capacity)
             product = (
-                own_ref[rows, part]
-                + is_end * near_ref[rows, part].astype(F32)
+                partial_ref[rows, part]
                 + far_ref[rows, part].astype(F32)
-                + (1.0 - is_end)
-                * (middle_ref[rows, part].astype(F32) + outer_ref[rows, part].astype(F32))
+                + (1.0 - is_end) * outer_ref[rows, part].astype(F32)
             )
-            grad_ref[whole_rows, part] = (info[:, experts : experts + 1] * product).astype(BF16)
+            product_ref[rows, part] = product
             weighted = hidden_ref[whole_rows, part].astype(F32) * product
             for j in range(tile // LANES):
                 totals[half] = totals[half] + weighted[:, j * LANES : (j + 1) * LANES]
-        store(t).start()
     diagonal = lax.broadcasted_iota(jnp.int32, (capacity, capacity), 0) == lax.broadcasted_iota(
         jnp.int32, (capacity, capacity), 1
     )
@@ -333,29 +345,59 @@
     for k in range(shards):
         late_ref[k, :, :width] = late(slice(k * width, (k + 1) * width))
         late_ref[k, :, width:] = low
+
+
+def hidden_kernel(experts, place, product_ref, picked_ref, other_ref, grad_hbm, grad_ref, sems):
+    capacity = picked_ref.shape[0]
+    column = picked_ref.shape[1] - LANES + experts
+    tiles = sems.shape[0]
+    tile = product_ref.shape[1] // tiles
+    stores = []
     for t in range(tiles):
-        store(t).wait()
-
-
-def finish(place, own, near, middle, far, outer, hidden_state, picked, other, experts, shards, tiles):
+        part = pl.ds(t * tile, tile)
+        for half, ref in enumerate((picked_ref, other_ref)):
+            rows = slice(half * capacity, (half + 1) * capacity)
+            whole_rows = pl.ds(pl.multiple_of((place[2] ^ half) * capacity, capacity), capacity)
+            window_prob = ref[:, column - experts :].astype(F32)[:, experts : experts + 1]
+            grad_ref[whole_rows, part] = (window_prob * product_ref[rows, part]).astype(BF16)
+        store = pltpu.make_async_copy(grad_ref.at[:, part], grad_hbm.at[:, part], sems.at[t])
+        store.start()
+        stores.append(store)
+    for store in stores:
+        store.wait()
+
+
+def hidden_gradient(place, product, picked, other, experts, tiles):
+    return pl.pallas_call(
+        functools.partial(hidden_kernel, experts),
+        out_shape=jax.ShapeDtypeStruct(product.shape, BF16),
+        in_specs=[SMEM] + [VMEM] * 3,
+        out_specs=HBM,
+        scratch_shapes=[pltpu.VMEM(product.shape, BF16), pltpu.SemaphoreType.DMA((tiles,))],
+        compiler_params=params(),
+        cost_estimate=cost(0, 0),
+        name="hidden_gradient",
+    )(place, product, picked, other)
+
+
+def finish(place, partial, far, outer, hidden_state, picked, other, experts, shards):
     rows, hidden = far.shape
     capacity = picked.shape[0]
     width = (picked.shape[1] - 2 * LANES) // shards
     return pl.pallas_call(
         functools.partial(finish_kernel, experts),
         out_shape=(
-            jax.ShapeDtypeStruct((rows, hidden), BF16),
+            pltpu.VMEM((rows, hidden), F32),
             jax.ShapeDtypeStruct((8, capacity), F32),
             jax.ShapeDtypeStruct((8, capacity), F32),
             jax.ShapeDtypeStruct((shards, experts, width + LANES), F32),
         ),
-        in_specs=[SMEM] + [VMEM] * 8,
-        out_specs=(HBM, VMEM, VMEM, VMEM),
-        scratch_shapes=[pltpu.VMEM((rows, hidden), BF16), pltpu.SemaphoreType.DMA((tiles,))],
+        in_specs=[SMEM] + [VMEM] * 6,
+        out_specs=(VMEM,) * 4,
         compiler_params=params(),
         cost_estimate=cost(8 * rows * hidden, 10 * rows * hidden),
         name="finish",
-    )(place, own, near, middle, far, outer, hidden_state, picked, other)
+    )(place, partial, far, outer, hidden_state, picked, other)
 
 
 def token_kernel(prob_ref, prob_got_ref, slots_ref, info_ref, router_ref, token_hbm, token_ref, sems):
@@ -391,19 +433,28 @@
     )(prob, prob_got, slots, info, router)
 
 
-def adapter_late_kernel(place, early_ref, late_ref, mixed_ref, router_ref, down_ref, up_ref):
+def adapter_late_kernel(
+    place, early_ref, late_ref, mixed_ref, router_ref, down_hbm, up_hbm, down_ref, up_ref, sems
+):
     groups, rows, _ = early_ref.shape
     half = groups // 2
     rank, width = up_ref.shape
+    parts = [slice(g * rows, (g + 1) * rows) for g in range(half)]
+    down = jnp.dot(
+        mixed_ref[...], late_ref[:, :width], precision=EXACT, preferred_element_type=F32
+    )
+    for g, part in enumerate(parts):
+        down_ref[part] = early_ref[(g + half) ^ place[1], :, :width].astype(F32) + down[part]
+    store_down = pltpu.make_async_copy(down_ref, down_hbm, sems.at[0])
+    store_down.start()
     router = feature_block(router_ref, place, 0, width).astype(F32)
     up = ADAPTER_SCALE * contract(late_ref[:, width : width + rank], router, 0, 0, EXACT)
-    down = jnp.dot(
-        mixed_ref[...], late_ref[:, :width], precision=EXACT, preferred_element_type=F32
-    )
-    for g in range(half):
-        part = slice(g * rows, (g + 1) * rows)
+    for g, part in enumerate(parts):
         up_ref[part] = early_ref[g ^ place[1], :, :width].astype(F32) + up[part]
-        down_ref[part] = early_ref[(g + half) ^ place[1], :, :width].astype(F32) + down[part]
+    store_up = pltpu.make_async_copy(up_ref, up_hbm, sems.at[1])
+    store_up.start()
+    store_down.wait()
+    store_up.wait()
 
 
 def adapter_late(place, early, late, mixed, router):
@@ -413,7 +464,8 @@
         adapter_late_kernel,
         out_shape=(out, out),
         in_specs=[SMEM] + [VMEM] * 4,
-        out_specs=(whole(out.shape),) * 2,
+        out_specs=(HBM, HBM),
+        scratch_shapes=[pltpu.VMEM(out.shape, F32)] * 2 + [pltpu.SemaphoreType.DMA((2,))],
         compiler_params=params(),
         cost_estimate=cost(64 * groups * rows * width, 8 * groups * rows * width),
         name="adapter_late",
@@ -472,22 +524,25 @@
     forward = add_near(place, far, near)
     across = swap(forward, "shard", 4, 2)
     forward, last, middle = lax.optimization_barrier((forward, last, middle))
-    outer = swap(last, "shard", 4, 1)
+    outer = lax.ppermute(last, "shard", [(0, 1), (3, 2)])
     forward, early, picked = lax.optimization_barrier((forward, early, picked))
     other_picked = swap(picked, "expert", 2, 1)
     early = early[:4] + swap(early[4:].astype(BF16), "expert", 2, 1).astype(F32)
+    partial = add_first(place, own, near, middle)
+    early, partial = lax.optimization_barrier((early, partial))
     parts = early.astype(BF16)
     early = early[0] + sum(swap(parts[k], "dp", 4, k).astype(F32) for k in range(1, 4))
     across, early, other_picked = lax.optimization_barrier((across, early, other_picked))
     across, outer = lax.optimization_barrier((across, outer))
 
-    hidden_grad, prob, prob_other, late = finish(
-        place, own, near, middle, across, outer, stored_hidden_state[0, 0], picked, other_picked,
-        experts, 4, 4,
+    product, prob, prob_other, late = finish(
+        place, partial, across, outer, stored_hidden_state[0, 0], picked, other_picked, experts, 4
     )
     early = jnp.pad(early, ((0, 0), (0, 0), (0, LANES)))
     late = jnp.concatenate([late, early], 1)
     late = late[:2] + swap(late[2:].astype(BF16), "shard", 4, 2).astype(F32)
+    hidden_grad = hidden_gradient(place, product, picked, other_picked, experts, 4)
+    late, hidden_grad = lax.optimization_barrier((late, hidden_grad))
     prob_got = swap(prob_other, "expert", 2, 1)
     late = late[0] + swap(late[1].astype(BF16), "shard", 4, 1).astype(F32)
     late, early = late[:experts], late[experts:].astype(BF16)

time: 83.6 us -> 82.6 us (0.988)
  waiting for transfers between devices: 45.9 us -> 41 us
  starting transfers between devices: 18.2 us -> 20.8 us
  Pallas kernels: 17.8 us -> 19 us
    ppermute x19 -> x18, waiting for transfers between devices: 45.9 us -> 41 us  [swap(): return lax.ppermute(value, axis, xor_pairs(count, bits))]
    ppermute x0 -> x1, starting transfers between devices: none -> 2.96 us  [direct_device(): outer = lax.ppermute(last, 'shard', [(0, 1), (3, 2)])]
    pallas_call x1 -> x3, Pallas kernels: 2.46 us -> 3.68 us  [the longest x1 1.49 us: finish(): pl.pallas_call(functools.partial(finish_kernel, experts), out_shape=(pltp...]
    ppermute x19 -> x18, starting transfers between devices: 17.6 us -> 17.2 us  [swap(): return lax.ppermute(value, axis, xor_pairs(count, bits))]
  transfers between devices with their start and end apart: 20 -> 20, of which waited for: 13 -> 12; matrix products, arithmetic and copies ran while one was open for 0% -> 0% of each run, Pallas kernels for 12% -> 15%
where the time goes in v3:
time: 82.6 us; the launch traced here: 82.4 us
  waiting for transfers between devices  41 us (50%)
  starting transfers between devices  20.8 us (25%)
  Pallas kernels  19 us (23%)
  between operations  0.96 us (1%)
    ppermute x18, waiting for transfers between devices, swap(): return lax.ppermute(value, axis, xor_pairs(count, bits))  41 us
    ppermute x18, starting transfers between devices, swap(): return lax.ppermute(value, axis, xor_pairs(count, bits))  17.2 us
    pallas_call x1, Pallas kernels, adapter_early(): pl.pallas_call(adapter_kernel, out_shape=(jax.ShapeDtypeStruct((groups, s...  3.47 us
    pallas_call x2, Pallas kernels, products(): pl.pallas_call(functools.partial(product_kernel, len(before) // 4), out_s...  3.07 us
    pallas_call x1, Pallas kernels, dequantize(): pl.pallas_call(weight_kernel, out_shape=pltpu.VMEM(codes.shape, BF16), in...  3.05 us
    ppermute x1, starting transfers between devices, direct_device(): outer = lax.ppermute(last, 'shard', [(0, 1), (3, 2)])  2.96 us
    pallas_call x1, Pallas kernels, route(): pl.pallas_call(route_kernel, out_shape=(jax.ShapeDtypeStruct((shards, cap...  1.99 us
    pallas_call x1, Pallas kernels, adapter_late(): pl.pallas_call(adapter_late_kernel, out_shape=(out, out), in_specs=[SMEM]...  1.69 us
  transfers between devices with their start and end apart: 20, of which 12 were waited for; matrix products, arithmetic and copies ran while one was open for 0% of the time, Pallas kernels for 15%

profile of v3, /device:TPU:0, one launch (start us, length us, event | category | flops | bytes accessed | tf_op | source)
XLA Modules:
  0.0 82.4 jit_solution(7014588285380199525)
XLA Ops:
  0.6 0.1 pad_add_fusion.place
  0.7 2.0 %route.1 = (bf16[4,32,768]{2,1,0:T(8,128)(2,1)S(1)}, f32[32,128]{1,0:T(8,128)S(1)}, f32[16,128]{1,0:T(8,128)S(1)}) custom-call(s32[4]{0:T(128)S(1)} %pad_add_fusion.place, f32[8,128]{1,0:T(8,128)} %bitcast.36, s32[2,128]{1,0:T(2,128)} %bitcast.37, bf16[128,3072]{1,0:T(8,128)(2,1)} %grad_hbm.3), custom_call_target="tpu_custom_call" | custom-call | flops 25165824 | bytes 786432 | tf_op jit(solution)/shard_map/route/pallas_call | solution.py:96
  2.7 5.1 %collective-permute-start.2 = (bf16[32,768]{1,0:T(8,128)(2,1)S(1)}, bf16[32,768]{1,0:T(8,128)(2,1)S(1)}, u32[]{:S(2)}, u32[]{:S(2)}) collective-permute-start(bf16[32,768]{1,0:T(8,128)(2,1)S(1)} %get-tuple-element.90), channel_id=1, source_target_pairs={{0,3},{1,2},{2,1},{3,0},{4,7},{5,6},{6,5},{7,4},{8,11},{9,10},{10,... | collective-permute-start | bytes 147464 | tf_op jit(solution)/shard_map/ppermute | solution.py:476
  7.9 0.0 collective-permute-start.1
  7.9 0.6 collective-permute-start
  8.5 3.1 %dequantize.1.weight_ref = bf16[768,4096]{1,0:T(8,128)(2,1)S(1)} custom-call(bf16[768,4096]{1,0:T(8,128)(2,1)} %codes_hbm.1, bf16[12,4096]{1,0:T(8,128)(2,1)} %scales_hbm.1), custom_call_target="tpu_custom_call" | custom-call | flops 3145728 | bytes 12582912 | tf_op jit(solution)/shard_map/dequantize/pallas_call | solution.py:212
  11.6 0.0 collective-permute-done.2
  11.6 1.3 %collective-permute-done.1 = bf16[32,768]{1,0:T(8,128)(2,1)S(1)} collective-permute-done((bf16[32,768]{1,0:T(8,128)(2,1)S(1)}, bf16[32,768]{1,0:T(8,128)(2,1)S(1)}, u32[]{:S(2)}, u32[]{:S(2)}) %collective-permute-start.1) | collective-permute-done | bytes 49184 | tf_op jit(solution)/shard_map/ppermute | solution.py:476
  12.8 0.0 collective-permute-done
  12.9 0.1 collective-permute-start.3
  13.0 1.5 %products.2 = (bf16[64,4096]{1,0:T(8,128)(2,1)S(1)}, bf16[64,4096]{1,0:T(8,128)(2,1)S(1)}, bf16[64,4096]{1,0:T(8,128)(2,1)S(1)}, f32[64,4096]{1,0:T(8,128)S(1)}) custom-call(s32[4]{0:T(128)S(1)} %pad_add_fusion.place, bf16[4,32,768]{2,1,0:T(8,128)(2,1)S(1)} %pad_maximum_fusion.rows_ref, bf16[768,4096]{1,0:T(8,128)(2,1)S(1)} %dequantize.1.weight_ref), custom_call_target="tpu_custom_call" | custom-call | flops 805306368 | bytes 6291456 | tf_op jit(solution)/shard_map/products/pallas_call | solution.py:137
  14.5 0.0 collective-permute-done.3.rows_ref
  14.5 1.5 %products.3 = (bf16[64,4096]{1,0:T(8,128)(2,1)S(1)}, bf16[64,4096]{1,0:T(8,128)(2,1)S(1)}, bf16[64,4096]{1,0:T(8,128)(2,1)S(1)}, f32[64,4096]{1,0:T(8,128)S(1)}) custom-call(s32[4]{0:T(128)S(1)} %pad_add_fusion.place, ...), custom_call_target="tpu_custom_call", output_to_operand_aliasing={{0}: (3, {}), {1}: (4, {}), {2}: (5, {}), {3}: (6, {})} | custom-call | flops 805306368 | bytes 6291456 | tf_op jit(solution)/shard_map/products/pallas_call | solution.py:137
  16.1 0.0 copy-start
  16.1 0.7 collective-permute-start.4
  16.8 0.7 collective-permute-start.6
  17.5 3.5 %adapter_early.1 = (f32[8,4,16,768]{3,2,1,0:T(8,128)S(1)}, bf16[32,3328]{1,0:T(8,128)(2,1)S(1)}, f32[64,8]{1,0:T(8,128)S(1)}) custom-call(s32[4]{0:T(128)S(1)} %pad_add_fusion.place, bf16[128,3072]{1,0:T(8,128)(2,1)} %grad_hbm.3, bf16[128,3072]{1,0:T(8,128)(2,1)} %context_hbm.1, bf16[64,3072]{1,0:T(8,128)(2,1)} %down_hbm.1, bf16[64,3072]{1,0:T(8,128)(2,1)} %up_hbm.1, ...), custom_call_target="tpu_custom_call" | custom-call | tf_op jit(solution)/shard_map/adapter_early/pallas_call | solution.py:282
  20.9 9.5 %collective-permute-done.4.near_ref = bf16[64,4096]{1,0:T(8,128)(2,1)S(1)} collective-permute-done((bf16[64,4096]{1,0:T(8,128)(2,1)S(1)}, bf16[64,4096]{1,0:T(8,128)(2,1)S(1)}, u32[]{:S(2)}, u32[]{:S(2)}) %collective-permute-start.4) | collective-permute-done | bytes 524320 | tf_op jit(solution)/shard_map/ppermute | solution.py:476
  30.5 0.1 collective-permute-start.5
  30.6 0.7 add_near.1
  31.3 2.1 %collective-permute-start.7 = (bf16[64,4096]{1,0:T(8,128)(2,1)S(1)}, bf16[64,4096]{1,0:T(8,128)(2,1)S(1)}, u32[]{:S(2)}, u32[]{:S(2)}) collective-permute-start(bf16[64,4096]{1,0:T(8,128)(2,1)S(1)} %add_near.1), channel_id=1, source_target_pairs={{0,2},{1,3},{2,0},{3,1},{4,6},{5,7},{6,4},{7,5},{8,10},{9,11},{10,... | collective-permute-start | bytes 1572872 | tf_op jit(solution)/shard_map/ppermute | solution.py:476
  33.4 0.0 collective-permute-done.6.middle_ref
  33.4 3.0 %collective-permute-start.12 = (bf16[64,4096]{1,0:T(8,128)(2,1)S(1)}, bf16[64,4096]{1,0:T(8,128)(2,1)S(1)}, u32[]{:S(2)}, u32[]{:S(2)}) collective-permute-start(bf16[64,4096]{1,0:T(8,128)(2,1)S(1)} %get-tuple-element.70), channel_id=1, source_target_pairs={{0,1},{3,2},{4,5},{7,6},{8,9},{11,10},{12,13},{15,14},{16,17},{19,... | collective-permute-start | bytes 1572872 | tf_op jit(solution)/shard_map/ppermute | solution.py:527
  36.3 0.7 add_first.1.partial_ref
  37.1 0.0 copy-start.1
  37.1 0.0 collective-permute-done.5
  37.1 0.1 convert_add_fusion
  37.3 1.6 %collective-permute-start.8 = (bf16[4,16,768]{2,1,0:T(8,128)(2,1)S(1)}, bf16[4,16,768]{2,1,0:T(8,128)(2,1)S(1)}, u32[]{:S(2)}, u32[]{:S(2)}) collective-permute-start(bf16[4,16,768]{2,1,0:T(8,128)(2,1)S(1)} %get-tuple-element.86), channel_id=1, source_target_pairs={{0,8},{8,0},{16,24},{24,16},{1,9},{9,1},{17,25},{25,17},{2,10},{10... | collective-permute-start | bytes 294920 | tf_op jit(solution)/shard_map/ppermute | solution.py:476
  38.9 1.5 %collective-permute-start.10 = (bf16[4,16,768]{2,1,0:T(8,128)(2,1)S(1)}, bf16[4,16,768]{2,1,0:T(8,128)(2,1)S(1)}, u32[]{:S(2)}, u32[]{:S(2)}) collective-permute-start(bf16[4,16,768]{2,1,0:T(8,128)(2,1)S(1)} %get-tuple-element.87), channel_id=1, source_target_pairs={{0,24},{8,16},{16,8},{24,0},{1,25},{9,17},{17,9},{25,1},{2,26},{10... | collective-permute-start | bytes 294920 | tf_op jit(solution)/shard_map/ppermute | solution.py:476
  40.3 0.5 collective-permute-start.9
  40.9 1.1 %collective-permute-done.8 = bf16[4,16,768]{2,1,0:T(8,128)(2,1)S(1)} collective-permute-done((bf16[4,16,768]{2,1,0:T(8,128)(2,1)S(1)}, bf16[4,16,768]{2,1,0:T(8,128)(2,1)S(1)}, u32[]{:S(2)}, u32[]{:S(2)}) %collective-permute-start.8) | collective-permute-done | bytes 98336 | tf_op jit(solution)/shard_map/ppermute | solution.py:476
  42.0 0.0 collective-permute-start.11
  42.0 3.2 %collective-permute-done.10 = bf16[4,16,768]{2,1,0:T(8,128)(2,1)S(1)} collective-permute-done((bf16[4,16,768]{2,1,0:T(8,128)(2,1)S(1)}, bf16[4,16,768]{2,1,0:T(8,128)(2,1)S(1)}, u32[]{:S(2)}, u32[]{:S(2)}) %collective-permute-start.10) | collective-permute-done | bytes 98336 | tf_op jit(solution)/shard_map/ppermute | solution.py:476
  45.2 1.2 %collective-permute-done.9 = bf16[4,16,768]{2,1,0:T(8,128)(2,1)S(1)} collective-permute-done((bf16[4,16,768]{2,1,0:T(8,128)(2,1)S(1)}, bf16[4,16,768]{2,1,0:T(8,128)(2,1)S(1)}, u32[]{:S(2)}, u32[]{:S(2)}) %collective-permute-start.9) | collective-permute-done | bytes 98336 | tf_op jit(solution)/shard_map/ppermute | solution.py:476
  46.4 0.0 collective-permute-done.11.other_ref
  46.4 11.4 %collective-permute-done.7.far_ref = bf16[64,4096]{1,0:T(8,128)(2,1)S(1)} collective-permute-done((bf16[64,4096]{1,0:T(8,128)(2,1)S(1)}, bf16[64,4096]{1,0:T(8,128)(2,1)S(1)}, u32[]{:S(2)}, u32[]{:S(2)}) %collective-permute-start.7) | collective-permute-done | bytes 524320 | tf_op jit(solution)/shard_map/ppermute | solution.py:476
  57.8 0.0 collective-permute-done.12.outer_ref
  57.8 0.0 copy-done
  57.8 1.5 %finish.1 = (f32[64,4096]{1,0:T(8,128)S(1)}, f32[8,32]{1,0:T(8,128)S(1)}, f32[8,32]{1,0:T(8,128)S(1)}, f32[4,8,896]{2,1,0:T(8,128)S(1)}) custom-call(s32[4]{0:T(128)S(1)} %pad_add_fusion.place, f32[64,4096]{1,0:T(8,128)S(1)} %add_first.1.partial_ref, bf16[64,4096]{1,0:T(8,128)(2,1)S(1)} %collective-permute-done.7.far_ref, ...), custom_call_target="tpu_custom_call" | custom-call | flops 2097152 | bytes 2621440 | tf_op jit(solution)/shard_map/finish/pallas_call | solution.py:387
  59.4 0.7 collective-permute-start.13
  60.1 1.4 %hidden_gradient.1 = bf16[64,4096]{1,0:T(8,128)(2,1)} custom-call(s32[4]{0:T(128)S(1)} %pad_add_fusion.place, f32[64,4096]{1,0:T(8,128)S(1)} %get-tuple-element.76.product_ref, bf16[32,3328]{1,0:T(8,128)(2,1)S(1)} %get-tuple-element.68.picked_ref, bf16[32,3328]{1,0:T(8,128)(2,1)S(1)} %collective-permute-done.11.other_ref), custom_call_target="tpu_custom_call" | custom-call | tf_op jit(solution)/shard_map/hidden_gradient/pallas_call | solution.py:371
  61.6 5.0 %collective-permute-done.13 = bf16[2,24,896]{2,1,0:T(8,128)(2,1)S(1)} collective-permute-done((bf16[2,24,896]{2,1,0:T(8,128)(2,1)S(1)}, bf16[2,24,896]{2,1,0:T(8,128)(2,1)S(1)}, u32[]{:S(2)}, u32[]{:S(2)}) %collective-permute-start.13) | collective-permute-done | bytes 86048 | tf_op jit(solution)/shard_map/ppermute | solution.py:476
  66.6 0.1 collective-permute-start.15
  66.7 4.0 %collective-permute-done.15 = bf16[24,896]{1,0:T(8,128)(2,1)S(1)} collective-permute-done((bf16[24,896]{1,0:T(8,128)(2,1)S(1)}, bf16[24,896]{1,0:T(8,128)(2,1)S(1)}, u32[]{:S(2)}, u32[]{:S(2)}) %collective-permute-start.15) | collective-permute-done | bytes 43040 | tf_op jit(solution)/shard_map/ppermute | solution.py:476
  70.7 2.5 %collective-permute-start.18 = (bf16[24,896]{1,0:T(8,128)(2,1)S(1)}, bf16[24,896]{1,0:T(8,128)(2,1)S(1)}, u32[]{:S(2)}, u32[]{:S(2)}) collective-permute-start(bf16[24,896]{1,0:T(8,128)(2,1)S(1)} %pad_maximum_fusion.1), channel_id=1, source_target_pairs={{0,24},{8,16},{16,8},{24,0},{1,25},{9,17},{17,9},{25,1},{2,26},{10... | collective-permute-start | bytes 129032 | tf_op jit(solution)/shard_map/ppermute | solution.py:476
  73.2 0.5 collective-permute-start.17
  73.8 0.5 collective-permute-start.16
  74.3 1.9 %collective-permute-done.18 = bf16[24,896]{1,0:T(8,128)(2,1)S(1)} collective-permute-done((bf16[24,896]{1,0:T(8,128)(2,1)S(1)}, bf16[24,896]{1,0:T(8,128)(2,1)S(1)}, u32[]{:S(2)}, u32[]{:S(2)}) %collective-permute-start.18) | collective-permute-done | bytes 43040 | tf_op jit(solution)/shard_map/ppermute | solution.py:476
  76.2 1.1 %collective-permute-done.17 = bf16[24,896]{1,0:T(8,128)(2,1)S(1)} collective-permute-done((bf16[24,896]{1,0:T(8,128)(2,1)S(1)}, bf16[24,896]{1,0:T(8,128)(2,1)S(1)}, u32[]{:S(2)}, u32[]{:S(2)}) %collective-permute-start.17) | collective-permute-done | bytes 43040 | tf_op jit(solution)/shard_map/ppermute | solution.py:476
  77.3 0.5 collective-permute-done.16
  77.9 0.1 collective-permute-start.19
  77.9 0.5 collective-permute-start.14
  78.4 0.8 %collective-permute-done.14.prob_got_ref = f32[8,32]{1,0:T(8,128)S(1)} collective-permute-done((f32[8,32]{1,0:T(8,128)S(1)}, f32[8,32]{1,0:T(8,128)S(1)}, u32[]{:S(2)}, u32[]{:S(2)}) %collective-permute-start.14) | collective-permute-done | bytes 1056 | tf_op jit(solution)/shard_map/ppermute | solution.py:476
  79.3 0.0 copy-done.1
  79.3 1.3 %token_gradient.1 = bf16[128,3072]{1,0:T(8,128)(2,1)} custom-call(f32[8,32]{1,0:T(8,128)S(1)} %get-tuple-element.78.prob_ref, f32[8,32]{1,0:T(8,128)S(1)} %collective-permute-done.14.prob_got_ref, f32[32,128]{1,0:T(8,128)S(1)} %get-tuple-element.55.slots_ref, f32[16,128]{1,0:T(8,128)S(1)} %get-tuple-element.56.info_ref, bf16[8,3072]{1,0:T(8,128)(2,1)S(1)} %copy-done.1), custom_call_target="tpu_custom_call" | custom-call | flops 6291456 | bytes 786432 | tf_op jit(solution)/shard_map/token_gradient/pallas_call | solution.py:424
  80.6 0.0 collective-permute-done.19
  80.7 1.7 %adapter_late.1 = (f32[64,768]{1,0:T(8,128)}, f32[64,768]{1,0:T(8,128)}) custom-call(s32[4]{0:T(128)S(1)} %pad_add_fusion.place, bf16[8,16,896]{2,1,0:T(8,128)(2,1)S(1)} %bitcast.31, f32[8,896]{1,0:T(8,128)S(1)} %convert_add_fusion.1.late_ref, f32[64,8]{1,0:T(8,128)S(1)} %get-tuple-element.81.mixed_ref, bf16[8,3072]{1,0:T(8,128)(2,1)S(1)} %copy-done.1), custom_call_target="tpu_custom_call" | custom-call | flops 7340032 | bytes 917504 | tf_op jit(solution)/shard_map/adapter_late/pallas_call | solution.py:463
  (21 shorter events, 0.4 us)
Async XLA Ops:
  2.7 8.8 %collective-permute-start.2 = (bf16[32,768]{1,0:T(8,128)(2,1)S(1)}, bf16[32,768]{1,0:T(8,128)(2,1)S(1)}, u32[]{:S(2)}, u32[]{:S(2)}) collective-permute-start(bf16[32,768]{1,0:T(8,128)(2,1)S(1)} %get-tuple-element.90), channel_id=1, source_target_pairs={{0,3},{1,2},{2,1},{3,0},{4,7},{5,6},{6,5},{7,4},{8,11},{9,10},{10,... | collective-permute-start | bytes 147464 | tf_op jit(solution)/shard_map/ppermute | solution.py:476
  7.9 5.0 %collective-permute-start.1 = (bf16[32,768]{1,0:T(8,128)(2,1)S(1)}, bf16[32,768]{1,0:T(8,128)(2,1)S(1)}, u32[]{:S(2)}, u32[]{:S(2)}) collective-permute-start(bf16[32,768]{1,0:T(8,128)(2,1)S(1)} %get-tuple-element.91), channel_id=1, source_target_pairs={{0,2},{1,3},{2,0},{3,1},{4,6},{5,7},{6,4},{7,5},{8,10},{9,11},{10,... | collective-permute-start | bytes 147464 | tf_op jit(solution)/shard_map/ppermute | solution.py:476
  7.9 5.0 %collective-permute-start = (bf16[32,768]{1,0:T(8,128)(2,1)S(1)}, bf16[32,768]{1,0:T(8,128)(2,1)S(1)}, u32[]{:S(2)}, u32[]{:S(2)}) collective-permute-start(bf16[32,768]{1,0:T(8,128)(2,1)S(1)} %get-tuple-element.92), channel_id=1, source_target_pairs={{0,1},{1,0},{2,3},{3,2},{4,5},{5,4},{6,7},{7,6},{8,9},{9,8},{10,11... | collective-permute-start | bytes 147464 | tf_op jit(solution)/shard_map/ppermute | solution.py:476
  12.9 1.6 %collective-permute-start.3 = (bf16[4,32,768]{2,1,0:T(8,128)(2,1)S(1)}, bf16[4,32,768]{2,1,0:T(8,128)(2,1)S(1)}, u32[]{:S(2)}, u32[]{:S(2)}) collective-permute-start(bf16[4,32,768]{2,1,0:T(8,128)(2,1)S(1)} %pad_maximum_fusion.rows_ref), channel_id=1, source_target_pairs={{0,4},{4,0},{1,5},{5,1},{2,6},{6,2},{3,7},{7,3},{8,12},{12,8},{9,1... | collective-permute-start | bytes 589832 | tf_op jit(solution)/shard_map/ppermute | solution.py:476
  16.1 41.8 %copy-start = (bf16[1,1,64,4096]{3,2,1,0:T(8,128)(2,1)S(1)}, bf16[1,1,64,4096]{3,2,1,0:T(8,128)(2,1)}, u32[]{:S(2)}) copy-start(bf16[1,1,64,4096]{3,2,1,0:T(8,128)(2,1)} %param.16) | copy-start | bytes 1572868
  16.1 14.4 %collective-permute-start.4 = (bf16[64,4096]{1,0:T(8,128)(2,1)S(1)}, bf16[64,4096]{1,0:T(8,128)(2,1)S(1)}, u32[]{:S(2)}, u32[]{:S(2)}) collective-permute-start(bf16[64,4096]{1,0:T(8,128)(2,1)S(1)} %get-tuple-element.52), channel_id=1, source_target_pairs={{0,1},{1,0},{2,3},{3,2},{4,5},{5,4},{6,7},{7,6},{8,9},{9,8},{10,11... | collective-permute-start | bytes 1572872 | tf_op jit(solution)/shard_map/ppermute | solution.py:476
  16.8 16.6 %collective-permute-start.6 = (bf16[64,4096]{1,0:T(8,128)(2,1)S(1)}, bf16[64,4096]{1,0:T(8,128)(2,1)S(1)}, u32[]{:S(2)}, u32[]{:S(2)}) collective-permute-start(bf16[64,4096]{1,0:T(8,128)(2,1)S(1)} %get-tuple-element.70), channel_id=1, source_target_pairs={{1,2},{2,1},{5,6},{6,5},{9,10},{10,9},{13,14},{14,13},{17,18},{18,... | collective-permute-start | bytes 1572872 | tf_op jit(solution)/shard_map/ppermute | solution.py:518
  30.5 6.6 %collective-permute-start.5 = (bf16[4,4,16,768]{3,2,1,0:T(8,128)(2,1)S(1)}, bf16[4,4,16,768]{3,2,1,0:T(8,128)(2,1)S(1)}, u32[]{:S(2)}, u32[]{:S(2)}) collective-permute-start(bf16[4,4,16,768]{3,2,1,0:T(8,128)(2,1)S(1)} %slice.162), channel_id=1, source_target_pairs={{0,4},{4,0},{1,5},{5,1},{2,6},{6,2},{3,7},{7,3},{8,12},{12,8},{9,1... | collective-permute-start | bytes 1179656 | tf_op jit(solution)/shard_map/ppermute | solution.py:476
  31.3 26.5 %collective-permute-start.7 = (bf16[64,4096]{1,0:T(8,128)(2,1)S(1)}, bf16[64,4096]{1,0:T(8,128)(2,1)S(1)}, u32[]{:S(2)}, u32[]{:S(2)}) collective-permute-start(bf16[64,4096]{1,0:T(8,128)(2,1)S(1)} %add_near.1), channel_id=1, source_target_pairs={{0,2},{1,3},{2,0},{3,1},{4,6},{5,7},{6,4},{7,5},{8,10},{9,11},{10,... | collective-permute-start | bytes 1572872 | tf_op jit(solution)/shard_map/ppermute | solution.py:476
  33.4 24.4 %collective-permute-start.12 = (bf16[64,4096]{1,0:T(8,128)(2,1)S(1)}, bf16[64,4096]{1,0:T(8,128)(2,1)S(1)}, u32[]{:S(2)}, u32[]{:S(2)}) collective-permute-start(bf16[64,4096]{1,0:T(8,128)(2,1)S(1)} %get-tuple-element.70), channel_id=1, source_target_pairs={{0,1},{3,2},{4,5},{7,6},{8,9},{11,10},{12,13},{15,14},{16,17},{19,... | collective-permute-start | bytes 1572872 | tf_op jit(solution)/shard_map/ppermute | solution.py:527
  37.1 42.2 %copy-start.1 = (bf16[8,3072]{1,0:T(8,128)(2,1)S(1)}, bf16[8,3072]{1,0:T(8,128)(2,1)}, u32[]{:S(2)}) copy-start(bf16[8,3072]{1,0:T(8,128)(2,1)} %router_ref.3) | copy-start | bytes 147460
  37.3 4.7 %collective-permute-start.8 = (bf16[4,16,768]{2,1,0:T(8,128)(2,1)S(1)}, bf16[4,16,768]{2,1,0:T(8,128)(2,1)S(1)}, u32[]{:S(2)}, u32[]{:S(2)}) collective-permute-start(bf16[4,16,768]{2,1,0:T(8,128)(2,1)S(1)} %get-tuple-element.86), channel_id=1, source_target_pairs={{0,8},{8,0},{16,24},{24,16},{1,9},{9,1},{17,25},{25,17},{2,10},{10... | collective-permute-start | bytes 294920 | tf_op jit(solution)/shard_map/ppermute | solution.py:476
  38.9 6.3 %collective-permute-start.10 = (bf16[4,16,768]{2,1,0:T(8,128)(2,1)S(1)}, bf16[4,16,768]{2,1,0:T(8,128)(2,1)S(1)}, u32[]{:S(2)}, u32[]{:S(2)}) collective-permute-start(bf16[4,16,768]{2,1,0:T(8,128)(2,1)S(1)} %get-tuple-element.87), channel_id=1, source_target_pairs={{0,24},{8,16},{16,8},{24,0},{1,25},{9,17},{17,9},{25,1},{2,26},{10... | collective-permute-start | bytes 294920 | tf_op jit(solution)/shard_map/ppermute | solution.py:476
  40.3 6.0 %collective-permute-start.9 = (bf16[4,16,768]{2,1,0:T(8,128)(2,1)S(1)}, bf16[4,16,768]{2,1,0:T(8,128)(2,1)S(1)}, u32[]{:S(2)}, u32[]{:S(2)}) collective-permute-start(bf16[4,16,768]{2,1,0:T(8,128)(2,1)S(1)} %get-tuple-element.88), channel_id=1, source_target_pairs={{0,16},{8,24},{16,0},{24,8},{1,17},{9,25},{17,1},{25,9},{2,18},{10... | collective-permute-start | bytes 294920 | tf_op jit(solution)/shard_map/ppermute | solution.py:476
  42.0 4.4 %collective-permute-start.11 = (bf16[32,3328]{1,0:T(8,128)(2,1)S(1)}, bf16[32,3328]{1,0:T(8,128)(2,1)S(1)}, u32[]{:S(2)}, u32[]{:S(2)}) collective-permute-start(bf16[32,3328]{1,0:T(8,128)(2,1)S(1)} %get-tuple-element.68.picked_ref), channel_id=1, source_target_pairs={{0,4},{4,0},{1,5},{5,1},{2,6},{6,2},{3,7},{7,3},{8,12},{12,8},{9,1... | collective-permute-start | bytes 638984 | tf_op jit(solution)/shard_map/ppermute | solution.py:476
  59.4 7.2 %collective-permute-start.13 = (bf16[2,24,896]{2,1,0:T(8,128)(2,1)S(1)}, bf16[2,24,896]{2,1,0:T(8,128)(2,1)S(1)}, u32[]{:S(2)}, u32[]{:S(2)}) collective-permute-start(bf16[2,24,896]{2,1,0:T(8,128)(2,1)S(1)} %slice.163), channel_id=1, source_target_pairs={{0,2},{1,3},{2,0},{3,1},{4,6},{5,7},{6,4},{7,5},{8,10},{9,11},{10,... | collective-permute-start | bytes 258056 | tf_op jit(solution)/shard_map/ppermute | solution.py:476
  66.6 4.1 %collective-permute-start.15 = (bf16[24,896]{1,0:T(8,128)(2,1)S(1)}, bf16[24,896]{1,0:T(8,128)(2,1)S(1)}, u32[]{:S(2)}, u32[]{:S(2)}) collective-permute-start(bf16[24,896]{1,0:T(8,128)(2,1)S(1)} %fusion), channel_id=1, source_target_pairs={{0,1},{1,0},{2,3},{3,2},{4,5},{5,4},{6,7},{7,6},{8,9},{9,8},{10,11... | collective-permute-start | bytes 129032 | tf_op jit(solution)/shard_map/ppermute | solution.py:476
  70.7 5.4 %collective-permute-start.18 = (bf16[24,896]{1,0:T(8,128)(2,1)S(1)}, bf16[24,896]{1,0:T(8,128)(2,1)S(1)}, u32[]{:S(2)}, u32[]{:S(2)}) collective-permute-start(bf16[24,896]{1,0:T(8,128)(2,1)S(1)} %pad_maximum_fusion.1), channel_id=1, source_target_pairs={{0,24},{8,16},{16,8},{24,0},{1,25},{9,17},{17,9},{25,1},{2,26},{10... | collective-permute-start | bytes 129032 | tf_op jit(solution)/shard_map/ppermute | solution.py:476
  73.2 4.0 %collective-permute-start.17 = (bf16[24,896]{1,0:T(8,128)(2,1)S(1)}, bf16[24,896]{1,0:T(8,128)(2,1)S(1)}, u32[]{:S(2)}, u32[]{:S(2)}) collective-permute-start(bf16[24,896]{1,0:T(8,128)(2,1)S(1)} %pad_maximum_fusion.1), channel_id=1, source_target_pairs={{0,16},{8,24},{16,0},{24,8},{1,17},{9,25},{17,1},{25,9},{2,18},{10... | collective-permute-start | bytes 129032 | tf_op jit(solution)/shard_map/ppermute | solution.py:476
  73.8 4.0 %collective-permute-start.16 = (bf16[24,896]{1,0:T(8,128)(2,1)S(1)}, bf16[24,896]{1,0:T(8,128)(2,1)S(1)}, u32[]{:S(2)}, u32[]{:S(2)}) collective-permute-start(bf16[24,896]{1,0:T(8,128)(2,1)S(1)} %pad_maximum_fusion.1), channel_id=1, source_target_pairs={{0,8},{8,0},{16,24},{24,16},{1,9},{9,1},{17,25},{25,17},{2,10},{10... | collective-permute-start | bytes 129032 | tf_op jit(solution)/shard_map/ppermute | solution.py:476
  77.9 2.8 %collective-permute-start.19 = (bf16[72,896]{1,0:T(8,128)(2,1)S(1)}, bf16[72,896]{1,0:T(8,128)(2,1)S(1)}, u32[]{:S(2)}, u32[]{:S(2)}) collective-permute-start(bf16[72,896]{1,0:T(8,128)(2,1)S(1)} %get-tuple-element.93), channel_id=1, source_target_pairs={{0,4},{4,0},{1,5},{5,1},{2,6},{6,2},{3,7},{7,3},{8,12},{12,8},{9,1... | collective-permute-start | bytes 387080 | tf_op jit(solution)/shard_map/ppermute | solution.py:476
  77.9 1.3 %collective-permute-start.14 = (f32[8,32]{1,0:T(8,128)S(1)}, f32[8,32]{1,0:T(8,128)S(1)}, u32[]{:S(2)}, u32[]{:S(2)}) collective-permute-start(f32[8,32]{1,0:T(8,128)S(1)} %get-tuple-element.79), channel_id=1, source_target_pairs={{0,4},{4,0},{1,5},{5,1},{2,6},{6,2},{3,7},{7,3},{8,12},{12,8},{9,1... | collective-permute-start | bytes 3080 | tf_op jit(solution)/shard_map/ppermute | solution.py:476

commit v4 on v3

--- a/solution.py
+++ b/solution.py
@@ -164,25 +164,26 @@
     )(place, far, near)
 
 
-def partial_kernel(place, own_ref, near_ref, middle_ref, out_ref):
+def partial_kernel(place, own_ref, near_ref, middle_ref, far_ref, out_ref):
     is_end = place[3].astype(F32)
     out_ref[...] = (
         own_ref[...]
         + is_end * near_ref[...].astype(F32)
         + (1.0 - is_end) * middle_ref[...].astype(F32)
-    )
-
-
-def add_first(place, own, near, middle):
+        + far_ref[...].astype(F32)
+    )
+
+
+def add_far(place, own, near, middle, far):
     return pl.pallas_call(
         partial_kernel,
         out_shape=pltpu.VMEM(own.shape, F32),
-        in_specs=[SMEM] + [VMEM] * 3,
+        in_specs=[SMEM] + [VMEM] * 4,
         out_specs=VMEM,
         compiler_params=params(),
-        cost_estimate=cost(0, 0),
-        name="add_first",
-    )(place, own, near, middle)
+        cost_estimate=cost(round(3.0 * 1e9), 14 * own.size),
+        name="add_far",
+    )(place, own, near, middle, far)
 
 
 def weight_kernel(codes_hbm, scales_hbm, weight_ref, codes_ref, scales_ref, scale_sem, sems):
@@ -297,14 +298,14 @@
 
 
 def finish_kernel(
-    experts, place, partial_ref, far_ref, outer_ref, hidden_ref, picked_ref, other_ref,
+    experts, place, partial_ref, outer_ref, hidden_ref, picked_ref, other_ref,
     product_ref, prob_ref, prob_other_ref, late_ref,
 ):
     shards, _, late_width = late_ref.shape
     width = late_width - LANES
     features = shards * width
     is_end = place[3].astype(F32)
-    hidden = far_ref.shape[1]
+    hidden = outer_ref.shape[1]
     tile = 512
     capacity = picked_ref.shape[0]
     pickeds = (picked_ref, other_ref)
@@ -315,24 +316,16 @@
         for half in range(2):
             rows = slice(half * capacity, (half + 1) * capacity)
             whole_rows = pl.ds(pl.multiple_of((place[2] ^ half) * capacity, capacity), capacity)
-            product = (
-                partial_ref[rows, part]
-                + far_ref[rows, part].astype(F32)
-                + (1.0 - is_end) * outer_ref[rows, part].astype(F32)
-            )
+            product = partial_ref[rows, part] + (1.0 - is_end) * outer_ref[rows, part].astype(F32)
             product_ref[rows, part] = product
             weighted = hidden_ref[whole_rows, part].astype(F32) * product
             for j in range(tile // LANES):
                 totals[half] = totals[half] + weighted[:, j * LANES : (j + 1) * LANES]
-    diagonal = lax.broadcasted_iota(jnp.int32, (capacity, capacity), 0) == lax.broadcasted_iota(
-        jnp.int32, (capacity, capacity), 1
-    )
     lane = lax.broadcasted_iota(jnp.int32, (capacity, LANES), 1)
     logits = []
     for info, total, out in zip(infos, totals, (prob_ref, prob_other_ref), strict=True):
         prob = jnp.sum(total, axis=1, keepdims=True)
-        flat = jnp.sum(jnp.where(diagonal, prob, 0.0), axis=0, keepdims=True)
-        out[...] = jnp.broadcast_to(flat, out.shape)
+        out[...] = jnp.broadcast_to(prob, out.shape)
         logits.append(jnp.where(lane < experts, info * prob, 0.0).astype(BF16))
 
     def late(columns):
@@ -380,30 +373,30 @@
     )(place, product, picked, other)
 
 
-def finish(place, partial, far, outer, hidden_state, picked, other, experts, shards):
-    rows, hidden = far.shape
+def finish(place, partial, outer, hidden_state, picked, other, experts, shards):
+    rows, hidden = outer.shape
     capacity = picked.shape[0]
     width = (picked.shape[1] - 2 * LANES) // shards
     return pl.pallas_call(
         functools.partial(finish_kernel, experts),
         out_shape=(
             pltpu.VMEM((rows, hidden), F32),
-            jax.ShapeDtypeStruct((8, capacity), F32),
-            jax.ShapeDtypeStruct((8, capacity), F32),
+            jax.ShapeDtypeStruct((capacity, LANES), F32),
+            jax.ShapeDtypeStruct((capacity, LANES), F32),
             jax.ShapeDtypeStruct((shards, experts, width + LANES), F32),
         ),
-        in_specs=[SMEM] + [VMEM] * 6,
+        in_specs=[SMEM] + [VMEM] * 5,
         out_specs=(VMEM,) * 4,
         compiler_params=params(),
         cost_estimate=cost(8 * rows * hidden, 10 * rows * hidden),
         name="finish",
-    )(place, partial, far, outer, hidden_state, picked, other)
+    )(place, partial, outer, hidden_state, picked, other)
 
 
 def token_kernel(prob_ref, prob_got_ref, slots_ref, info_ref, router_ref, token_hbm, token_ref, sems):
     experts = router_ref.shape[0]
-    own = prob_ref[...] + prob_got_ref[...]
-    window = jnp.dot(own, slots_ref[...], precision=EXACT, preferred_element_type=F32)[0:1]
+    own = prob_ref[:, 0:1] + prob_got_ref[:, 0:1]
+    window = jnp.sum(slots_ref[...] * own, axis=0, keepdims=True)
     logits = (info_ref[:experts] * window).astype(BF16)
     tiles = sems.shape[0]
     tile = token_ref.shape[1] // tiles
@@ -441,14 +434,16 @@
     rank, width = up_ref.shape
     parts = [slice(g * rows, (g + 1) * rows) for g in range(half)]
     down = jnp.dot(
-        mixed_ref[...], late_ref[:, :width], precision=EXACT, preferred_element_type=F32
+        mixed_ref[...].astype(BF16),
+        late_ref[:, :width].astype(BF16),
+        preferred_element_type=F32,
     )
     for g, part in enumerate(parts):
         down_ref[part] = early_ref[(g + half) ^ place[1], :, :width].astype(F32) + down[part]
     store_down = pltpu.make_async_copy(down_ref, down_hbm, sems.at[0])
     store_down.start()
-    router = feature_block(router_ref, place, 0, width).astype(F32)
-    up = ADAPTER_SCALE * contract(late_ref[:, width : width + rank], router, 0, 0, EXACT)
+    router = feature_block(router_ref, place, 0, width)
+    up = ADAPTER_SCALE * contract(late_ref[:, width : width + rank].astype(BF16), router, 0, 0)
     for g, part in enumerate(parts):
         up_ref[part] = early_ref[g ^ place[1], :, :width].astype(F32) + up[part]
     store_up = pltpu.make_async_copy(up_ref, up_hbm, sems.at[1])
@@ -474,6 +469,11 @@
 
 def swap(value, axis, count, bits):
     return lax.ppermute(value, axis, xor_pairs(count, bits))
+
+
+def swap_group(value, bits):
+    pairs = [(d * 2 + e, (d ^ (bits & 3)) * 2 + (e ^ (bits >> 2))) for d in range(4) for e in range(2)]
+    return lax.ppermute(value, ("dp", "expert"), pairs)
 
 
 def after(value, *others):
@@ -527,16 +527,15 @@
     outer = lax.ppermute(last, "shard", [(0, 1), (3, 2)])
     forward, early, picked = lax.optimization_barrier((forward, early, picked))
     other_picked = swap(picked, "expert", 2, 1)
-    early = early[:4] + swap(early[4:].astype(BF16), "expert", 2, 1).astype(F32)
-    partial = add_first(place, own, near, middle)
-    early, partial = lax.optimization_barrier((early, partial))
     parts = early.astype(BF16)
-    early = early[0] + sum(swap(parts[k], "dp", 4, k).astype(F32) for k in range(1, 4))
-    across, early, other_picked = lax.optimization_barrier((across, early, other_picked))
-    across, outer = lax.optimization_barrier((across, outer))
+    early = early[0] + sum(swap_group(parts[g], g).astype(F32) for g in range(1, 8))
+    partial = add_far(place, own, near, middle, across)
+    partial, outer, early, other_picked = lax.optimization_barrier(
+        (partial, outer, early, other_picked)
+    )
 
     product, prob, prob_other, late = finish(
-        place, partial, across, outer, stored_hidden_state[0, 0], picked, other_picked, experts, 4
+        place, partial, outer, stored_hidden_state[0, 0], picked, other_picked, experts, 4
     )
     early = jnp.pad(early, ((0, 0), (0, 0), (0, LANES)))
     late = jnp.concatenate([late, early], 1)

time: 82.6 us -> 81.8 us (level)
  waiting for transfers between devices: 41 us -> 33.6 us
  starting transfers between devices: 20.8 us -> 27.8 us
    ppermute x18 -> x14, waiting for transfers between devices: 41 us -> 28 us  [swap(): return lax.ppermute(value, axis, xor_pairs(count, bits))]
    ppermute x0 -> x7, starting transfers between devices: none -> 6.84 us  [swap_group(): return lax.ppermute(value, ('dp', 'expert'), pairs)]
    ppermute x0 -> x7, waiting for transfers between devices: none -> 5.11 us  [swap_group(): return lax.ppermute(value, ('dp', 'expert'), pairs)]
    ppermute x18 -> x14, starting transfers between devices: 17.2 us -> 17.1 us  [swap(): return lax.ppermute(value, axis, xor_pairs(count, bits))]
  transfers between devices with their start and end apart: 20 -> 23, of which waited for: 12 -> 13; matrix products, arithmetic and copies ran while one was open for 0% -> 0% of each run, Pallas kernels for 15% -> 15%
where the time goes in v4:
time: 81.8 us; the launch traced here: 81.6 us
  waiting for transfers between devices  33.6 us (41%)
  starting transfers between devices  27.8 us (34%)
  Pallas kernels  18.7 us (23%)
  between operations  0.92 us (1%)
    ppermute x14, waiting for transfers between devices, swap(): return lax.ppermute(value, axis, xor_pairs(count, bits))  28 us
    ppermute x14, starting transfers between devices, swap(): return lax.ppermute(value, axis, xor_pairs(count, bits))  17.1 us
    ppermute x7, starting transfers between devices, swap_group(): return lax.ppermute(value, ('dp', 'expert'), pairs)  6.84 us
    ppermute x7, waiting for transfers between devices, swap_group(): return lax.ppermute(value, ('dp', 'expert'), pairs)  5.11 us
    pallas_call x1, Pallas kernels, adapter_early(): pl.pallas_call(adapter_kernel, out_shape=(jax.ShapeDtypeStruct((groups, s...  3.47 us
    ppermute x1, starting transfers between devices, direct_device(): outer = lax.ppermute(last, 'shard', [(0, 1), (3, 2)])  3.24 us
    pallas_call x2, Pallas kernels, products(): pl.pallas_call(functools.partial(product_kernel, len(before) // 4), out_s...  3.07 us
    pallas_call x1, Pallas kernels, dequantize(): pl.pallas_call(weight_kernel, out_shape=pltpu.VMEM(codes.shape, BF16), in...  3.05 us
  transfers between devices with their start and end apart: 23, of which 13 were waited for; matrix products, arithmetic and copies ran while one was open for 0% of the time, Pallas kernels for 15%

profile of v4, /device:TPU:0, one launch (start us, length us, event | category | flops | bytes accessed | tf_op | source)
XLA Modules:
  0.0 81.6 jit_solution(13204189942737084771)
XLA Ops:
  0.6 0.1 pad_add_fusion.place
  0.7 2.0 %route.1 = (bf16[4,32,768]{2,1,0:T(8,128)(2,1)S(1)}, f32[32,128]{1,0:T(8,128)S(1)}, f32[16,128]{1,0:T(8,128)S(1)}) custom-call(s32[4]{0:T(128)S(1)} %pad_add_fusion.place, f32[8,128]{1,0:T(8,128)} %bitcast.44, s32[2,128]{1,0:T(2,128)} %bitcast.45, bf16[128,3072]{1,0:T(8,128)(2,1)} %grad_hbm.3), custom_call_target="tpu_custom_call" | custom-call | flops 25165824 | bytes 786432 | tf_op jit(solution)/shard_map/route/pallas_call | solution.py:96
  2.7 5.1 %collective-permute-start.2 = (bf16[32,768]{1,0:T(8,128)(2,1)S(1)}, bf16[32,768]{1,0:T(8,128)(2,1)S(1)}, u32[]{:S(2)}, u32[]{:S(2)}) collective-permute-start(bf16[32,768]{1,0:T(8,128)(2,1)S(1)} %get-tuple-element.88), channel_id=1, source_target_pairs={{0,3},{1,2},{2,1},{3,0},{4,7},{5,6},{6,5},{7,4},{8,11},{9,10},{10,... | collective-permute-start | bytes 147464 | tf_op jit(solution)/shard_map/ppermute | solution.py:471
  7.9 0.0 collective-permute-start.1
  7.9 0.6 collective-permute-start
  8.5 3.1 %dequantize.1.weight_ref = bf16[768,4096]{1,0:T(8,128)(2,1)S(1)} custom-call(bf16[768,4096]{1,0:T(8,128)(2,1)} %codes_hbm.1, bf16[12,4096]{1,0:T(8,128)(2,1)} %scales_hbm.1), custom_call_target="tpu_custom_call" | custom-call | flops 3145728 | bytes 12582912 | tf_op jit(solution)/shard_map/dequantize/pallas_call | solution.py:213
  11.6 0.0 collective-permute-done.2
  11.6 1.3 %collective-permute-done.1 = bf16[32,768]{1,0:T(8,128)(2,1)S(1)} collective-permute-done((bf16[32,768]{1,0:T(8,128)(2,1)S(1)}, bf16[32,768]{1,0:T(8,128)(2,1)S(1)}, u32[]{:S(2)}, u32[]{:S(2)}) %collective-permute-start.1) | collective-permute-done | bytes 49184 | tf_op jit(solution)/shard_map/ppermute | solution.py:471
  12.8 0.0 collective-permute-done
  12.9 0.1 collective-permute-start.3
  13.0 1.5 %products.2 = (bf16[64,4096]{1,0:T(8,128)(2,1)S(1)}, bf16[64,4096]{1,0:T(8,128)(2,1)S(1)}, bf16[64,4096]{1,0:T(8,128)(2,1)S(1)}, f32[64,4096]{1,0:T(8,128)S(1)}) custom-call(s32[4]{0:T(128)S(1)} %pad_add_fusion.place, bf16[4,32,768]{2,1,0:T(8,128)(2,1)S(1)} %pad_maximum_fusion.rows_ref, bf16[768,4096]{1,0:T(8,128)(2,1)S(1)} %dequantize.1.weight_ref), custom_call_target="tpu_custom_call" | custom-call | flops 805306368 | bytes 6291456 | tf_op jit(solution)/shard_map/products/pallas_call | solution.py:137
  14.5 0.0 collective-permute-done.3.rows_ref
  14.5 1.5 %products.3 = (bf16[64,4096]{1,0:T(8,128)(2,1)S(1)}, bf16[64,4096]{1,0:T(8,128)(2,1)S(1)}, bf16[64,4096]{1,0:T(8,128)(2,1)S(1)}, f32[64,4096]{1,0:T(8,128)S(1)}) custom-call(s32[4]{0:T(128)S(1)} %pad_add_fusion.place, ...), custom_call_target="tpu_custom_call", output_to_operand_aliasing={{0}: (3, {}), {1}: (4, {}), {2}: (5, {}), {3}: (6, {})} | custom-call | flops 805306368 | bytes 6291456 | tf_op jit(solution)/shard_map/products/pallas_call | solution.py:137
  16.1 0.7 collective-permute-start.4
  16.8 0.7 collective-permute-start.5
  17.4 3.5 %adapter_early.1 = (f32[8,4,16,768]{3,2,1,0:T(8,128)S(1)}, bf16[32,3328]{1,0:T(8,128)(2,1)S(1)}, f32[64,8]{1,0:T(8,128)S(1)}) custom-call(s32[4]{0:T(128)S(1)} %pad_add_fusion.place, bf16[128,3072]{1,0:T(8,128)(2,1)} %grad_hbm.3, bf16[128,3072]{1,0:T(8,128)(2,1)} %context_hbm.1, bf16[64,3072]{1,0:T(8,128)(2,1)} %down_hbm.1, bf16[64,3072]{1,0:T(8,128)(2,1)} %up_hbm.1, ...), custom_call_target="tpu_custom_call" | custom-call | tf_op jit(solution)/shard_map/adapter_early/pallas_call | solution.py:283
  20.9 9.5 %collective-permute-done.4.near_ref = bf16[64,4096]{1,0:T(8,128)(2,1)S(1)} collective-permute-done((bf16[64,4096]{1,0:T(8,128)(2,1)S(1)}, bf16[64,4096]{1,0:T(8,128)(2,1)S(1)}, u32[]{:S(2)}, u32[]{:S(2)}) %collective-permute-start.4) | collective-permute-done | bytes 524320 | tf_op jit(solution)/shard_map/ppermute | solution.py:471
  30.4 0.7 add_near.1
  31.1 2.1 %collective-permute-start.6 = (bf16[64,4096]{1,0:T(8,128)(2,1)S(1)}, bf16[64,4096]{1,0:T(8,128)(2,1)S(1)}, u32[]{:S(2)}, u32[]{:S(2)}) collective-permute-start(bf16[64,4096]{1,0:T(8,128)(2,1)S(1)} %add_near.1), channel_id=1, source_target_pairs={{0,2},{1,3},{2,0},{3,1},{4,6},{5,7},{6,4},{7,5},{8,10},{9,11},{10,... | collective-permute-start | bytes 1572872 | tf_op jit(solution)/shard_map/ppermute | solution.py:471
  33.2 0.1 convert_element_type.57
  33.3 0.1 slice_bitcast_fusion.6
  33.4 0.0 copy-start
  33.4 1.6 %collective-permute-start.8 = (bf16[4,16,768]{2,1,0:T(8,128)(2,1)S(1)}, bf16[4,16,768]{2,1,0:T(8,128)(2,1)S(1)}, u32[]{:S(2)}, u32[]{:S(2)}) collective-permute-start(bf16[4,16,768]{2,1,0:T(8,128)(2,1)S(1)} %get-tuple-element.80), channel_id=1, source_target_pairs={{0,8},{4,12},{8,0},{12,4},{16,24},{20,28},{24,16},{28,20},{1,9},{5... | collective-permute-start | bytes 294920 | tf_op jit(solution)/shard_map/ppermute | solution.py:476
  35.0 0.3 collective-permute-start.14
  35.2 1.5 %collective-permute-start.13 = (bf16[4,16,768]{2,1,0:T(8,128)(2,1)S(1)}, bf16[4,16,768]{2,1,0:T(8,128)(2,1)S(1)}, u32[]{:S(2)}, u32[]{:S(2)}) collective-permute-start(bf16[4,16,768]{2,1,0:T(8,128)(2,1)S(1)} %get-tuple-element.82), channel_id=1, source_target_pairs={{0,20},{4,16},{8,28},{12,24},{16,4},{20,0},{24,12},{28,8},{1,21},{... | collective-permute-start | bytes 294920 | tf_op jit(solution)/shard_map/ppermute | solution.py:476
  36.7 0.0 collective-permute-done.5.middle_ref
  36.7 1.0 %collective-permute-start.12 = (bf16[4,16,768]{2,1,0:T(8,128)(2,1)S(1)}, bf16[4,16,768]{2,1,0:T(8,128)(2,1)S(1)}, u32[]{:S(2)}, u32[]{:S(2)}) collective-permute-start(bf16[4,16,768]{2,1,0:T(8,128)(2,1)S(1)} %get-tuple-element.83), channel_id=1, source_target_pairs={{0,12},{4,8},{8,4},{12,0},{16,28},{20,24},{24,20},{28,16},{1,13},{... | collective-permute-start | bytes 294920 | tf_op jit(solution)/shard_map/ppermute | solution.py:476
  37.7 0.4 collective-permute-done.8
  38.1 0.2 collective-permute-start.11
  38.3 2.7 %collective-permute-done.14 = bf16[4,16,768]{2,1,0:T(8,128)(2,1)S(1)} collective-permute-done((bf16[4,16,768]{2,1,0:T(8,128)(2,1)S(1)}, bf16[4,16,768]{2,1,0:T(8,128)(2,1)S(1)}, u32[]{:S(2)}, u32[]{:S(2)}) %collective-permute-start.14) | collective-permute-done | bytes 98336 | tf_op jit(solution)/shard_map/ppermute | solution.py:476
  41.0 1.5 %collective-permute-start.10 = (bf16[4,16,768]{2,1,0:T(8,128)(2,1)S(1)}, bf16[4,16,768]{2,1,0:T(8,128)(2,1)S(1)}, u32[]{:S(2)}, u32[]{:S(2)}) collective-permute-start(bf16[4,16,768]{2,1,0:T(8,128)(2,1)S(1)} %get-tuple-element.85), channel_id=1, source_target_pairs={{0,24},{4,28},{8,16},{12,20},{16,8},{20,12},{24,0},{28,4},{1,25},{... | collective-permute-start | bytes 294920 | tf_op jit(solution)/shard_map/ppermute | solution.py:476
  42.5 0.0 collective-permute-done.13
  42.5 0.8 %collective-permute-start.9 = (bf16[4,16,768]{2,1,0:T(8,128)(2,1)S(1)}, bf16[4,16,768]{2,1,0:T(8,128)(2,1)S(1)}, u32[]{:S(2)}, u32[]{:S(2)}) collective-permute-start(bf16[4,16,768]{2,1,0:T(8,128)(2,1)S(1)} %get-tuple-element.86), channel_id=1, source_target_pairs={{0,16},{4,20},{8,24},{12,28},{16,0},{20,4},{24,8},{28,12},{1,17},{... | collective-permute-start | bytes 294920 | tf_op jit(solution)/shard_map/ppermute | solution.py:476
  43.4 0.0 collective-permute-done.12
  43.4 0.3 collective-permute-start.15
  43.6 0.0 collective-permute-done.11
  43.6 3.2 %collective-permute-start.7 = (bf16[64,4096]{1,0:T(8,128)(2,1)S(1)}, bf16[64,4096]{1,0:T(8,128)(2,1)S(1)}, u32[]{:S(2)}, u32[]{:S(2)}) collective-permute-start(bf16[64,4096]{1,0:T(8,128)(2,1)S(1)} %get-tuple-element.60), channel_id=1, source_target_pairs={{0,1},{3,2},{4,5},{7,6},{8,9},{11,10},{12,13},{15,14},{16,17},{19,... | collective-permute-start | bytes 1572872 | tf_op jit(solution)/shard_map/ppermute | solution.py:527
  46.9 0.0 collective-permute-done.10
  46.9 2.0 %collective-permute-done.9 = bf16[4,16,768]{2,1,0:T(8,128)(2,1)S(1)} collective-permute-done((bf16[4,16,768]{2,1,0:T(8,128)(2,1)S(1)}, bf16[4,16,768]{2,1,0:T(8,128)(2,1)S(1)}, u32[]{:S(2)}, u32[]{:S(2)}) %collective-permute-start.9) | collective-permute-done | bytes 98336 | tf_op jit(solution)/shard_map/ppermute | solution.py:476
  48.9 0.1 bitcast_add_fusion
  49.0 7.9 %collective-permute-done.6.far_ref = bf16[64,4096]{1,0:T(8,128)(2,1)S(1)} collective-permute-done((bf16[64,4096]{1,0:T(8,128)(2,1)S(1)}, bf16[64,4096]{1,0:T(8,128)(2,1)S(1)}, u32[]{:S(2)}, u32[]{:S(2)}) %collective-permute-start.6) | collective-permute-done | bytes 524320 | tf_op jit(solution)/shard_map/ppermute | solution.py:471
  56.9 0.8 %add_far.1.partial_ref = f32[64,4096]{1,0:T(8,128)S(1)} custom-call(s32[4]{0:T(128)S(1)} %pad_add_fusion.place, f32[64,4096]{1,0:T(8,128)S(1)} %get-tuple-element.48.own_ref, bf16[64,4096]{1,0:T(8,128)(2,1)S(1)} %collective-permute-done.4.near_ref, bf16[64,4096]{1,0:T(8,128)(2,1)S(1)} %collective-permute-done.5.middle_ref, ...), custom_call_target="tpu_custom_call" | custom-call | flops 3000000000 | bytes 3670016 | tf_op jit(solution)/shard_map/add_far/pallas_call | solution.py:178
  57.7 0.0 collective-permute-done.15.other_ref
  57.7 0.5 collective-permute-done.7.outer_ref
  58.2 0.0 copy-done
  58.2 1.4 %finish.1 = (f32[64,4096]{1,0:T(8,128)S(1)}, f32[32,128]{1,0:T(8,128)S(1)}, f32[32,128]{1,0:T(8,128)S(1)}, f32[4,8,896]{2,1,0:T(8,128)S(1)}) custom-call(s32[4]{0:T(128)S(1)} %pad_add_fusion.place, f32[64,4096]{1,0:T(8,128)S(1)} %add_far.1.partial_ref, bf16[64,4096]{1,0:T(8,128)(2,1)S(1)} %collective-permute-done.7.outer_ref, bf16[64,4096]{1,0:T(8,128)(2,1)S(1)} %bitcast.38, ...), custom_call_target="tpu_custom_call" | custom-call | flops 2097152 | bytes 2621440 | tf_op jit(solution)/shard_map/finish/pallas_call | solution.py:380
  59.7 2.4 %collective-permute-start.16 = (bf16[2,24,896]{2,1,0:T(8,128)(2,1)S(1)}, bf16[2,24,896]{2,1,0:T(8,128)(2,1)S(1)}, u32[]{:S(2)}, u32[]{:S(2)}) collective-permute-start(bf16[2,24,896]{2,1,0:T(8,128)(2,1)S(1)} %slice.174), channel_id=1, source_target_pairs={{0,2},{1,3},{2,0},{3,1},{4,6},{5,7},{6,4},{7,5},{8,10},{9,11},{10,... | collective-permute-start | bytes 258056 | tf_op jit(solution)/shard_map/ppermute | solution.py:471
  62.1 1.4 %hidden_gradient.1 = bf16[64,4096]{1,0:T(8,128)(2,1)} custom-call(s32[4]{0:T(128)S(1)} %pad_add_fusion.place, f32[64,4096]{1,0:T(8,128)S(1)} %get-tuple-element.70.product_ref, bf16[32,3328]{1,0:T(8,128)(2,1)S(1)} %get-tuple-element.64.picked_ref, bf16[32,3328]{1,0:T(8,128)(2,1)S(1)} %collective-permute-done.15.other_ref), custom_call_target="tpu_custom_call" | custom-call | tf_op jit(solution)/shard_map/hidden_gradient/pallas_call | solution.py:364
  63.6 2.5 %collective-permute-done.16 = bf16[2,24,896]{2,1,0:T(8,128)(2,1)S(1)} collective-permute-done((bf16[2,24,896]{2,1,0:T(8,128)(2,1)S(1)}, bf16[2,24,896]{2,1,0:T(8,128)(2,1)S(1)}, u32[]{:S(2)}, u32[]{:S(2)}) %collective-permute-start.16) | collective-permute-done | bytes 86048 | tf_op jit(solution)/shard_map/ppermute | solution.py:471
  66.1 1.6 %collective-permute-start.18 = (bf16[24,896]{1,0:T(8,128)(2,1)S(1)}, bf16[24,896]{1,0:T(8,128)(2,1)S(1)}, u32[]{:S(2)}, u32[]{:S(2)}) collective-permute-start(bf16[24,896]{1,0:T(8,128)(2,1)S(1)} %fusion), channel_id=1, source_target_pairs={{0,1},{1,0},{2,3},{3,2},{4,5},{5,4},{6,7},{7,6},{8,9},{9,8},{10,11... | collective-permute-start | bytes 129032 | tf_op jit(solution)/shard_map/ppermute | solution.py:471
  67.7 2.5 %collective-permute-done.18 = bf16[24,896]{1,0:T(8,128)(2,1)S(1)} collective-permute-done((bf16[24,896]{1,0:T(8,128)(2,1)S(1)}, bf16[24,896]{1,0:T(8,128)(2,1)S(1)}, u32[]{:S(2)}, u32[]{:S(2)}) %collective-permute-start.18) | collective-permute-done | bytes 43040 | tf_op jit(solution)/shard_map/ppermute | solution.py:471
  70.3 2.1 %collective-permute-start.21 = (bf16[24,896]{1,0:T(8,128)(2,1)S(1)}, bf16[24,896]{1,0:T(8,128)(2,1)S(1)}, u32[]{:S(2)}, u32[]{:S(2)}) collective-permute-start(bf16[24,896]{1,0:T(8,128)(2,1)S(1)} %pad_maximum_fusion.1), channel_id=1, source_target_pairs={{0,24},{8,16},{16,8},{24,0},{1,25},{9,17},{17,9},{25,1},{2,26},{10... | collective-permute-start | bytes 129032 | tf_op jit(solution)/shard_map/ppermute | solution.py:471
  72.3 0.9 %collective-permute-start.20 = (bf16[24,896]{1,0:T(8,128)(2,1)S(1)}, bf16[24,896]{1,0:T(8,128)(2,1)S(1)}, u32[]{:S(2)}, u32[]{:S(2)}) collective-permute-start(bf16[24,896]{1,0:T(8,128)(2,1)S(1)} %pad_maximum_fusion.1), channel_id=1, source_target_pairs={{0,16},{8,24},{16,0},{24,8},{1,17},{9,25},{17,1},{25,9},{2,18},{10... | collective-permute-start | bytes 129032 | tf_op jit(solution)/shard_map/ppermute | solution.py:471
  73.3 0.5 collective-permute-start.19
  73.8 1.4 %collective-permute-done.21 = bf16[24,896]{1,0:T(8,128)(2,1)S(1)} collective-permute-done((bf16[24,896]{1,0:T(8,128)(2,1)S(1)}, bf16[24,896]{1,0:T(8,128)(2,1)S(1)}, u32[]{:S(2)}, u32[]{:S(2)}) %collective-permute-start.21) | collective-permute-done | bytes 43040 | tf_op jit(solution)/shard_map/ppermute | solution.py:471
  75.2 1.1 %collective-permute-done.20 = bf16[24,896]{1,0:T(8,128)(2,1)S(1)} collective-permute-done((bf16[24,896]{1,0:T(8,128)(2,1)S(1)}, bf16[24,896]{1,0:T(8,128)(2,1)S(1)}, u32[]{:S(2)}, u32[]{:S(2)}) %collective-permute-start.20) | collective-permute-done | bytes 43040 | tf_op jit(solution)/shard_map/ppermute | solution.py:471
  76.3 0.9 %collective-permute-done.19 = bf16[24,896]{1,0:T(8,128)(2,1)S(1)} collective-permute-done((bf16[24,896]{1,0:T(8,128)(2,1)S(1)}, bf16[24,896]{1,0:T(8,128)(2,1)S(1)}, u32[]{:S(2)}, u32[]{:S(2)}) %collective-permute-start.19) | collective-permute-done | bytes 43040 | tf_op jit(solution)/shard_map/ppermute | solution.py:471
  77.4 0.1 collective-permute-start.22
  77.4 0.5 collective-permute-start.17
  77.9 0.9 %collective-permute-done.17.prob_got_ref = f32[32,128]{1,0:T(8,128)S(1)} collective-permute-done((f32[32,128]{1,0:T(8,128)S(1)}, f32[32,128]{1,0:T(8,128)S(1)}, u32[]{:S(2)}, u32[]{:S(2)}) %collective-permute-start.17) | collective-permute-done | bytes 16416 | tf_op jit(solution)/shard_map/ppermute | solution.py:471
  78.8 0.0 copy-done.1
  78.8 1.2 %token_gradient.1 = bf16[128,3072]{1,0:T(8,128)(2,1)} custom-call(f32[32,128]{1,0:T(8,128)S(1)} %get-tuple-element.72.prob_ref, f32[32,128]{1,0:T(8,128)S(1)} %collective-permute-done.17.prob_got_ref, f32[32,128]{1,0:T(8,128)S(1)} %get-tuple-element.53.slots_ref, f32[16,128]{1,0:T(8,128)S(1)} %get-tuple-element.54.info_ref, bf16[8,3072]{1,0:T(8,128)(2,1)S(1)} %copy-done.1), custom_call_target="tpu_custom_call" | custom-call | flops 6291456 | bytes 786432 | tf_op jit(solution)/shard_map/token_gradient/pallas_call | solution.py:417
  80.0 0.0 collective-permute-done.22
  80.1 1.5 %adapter_late.1 = (f32[64,768]{1,0:T(8,128)}, f32[64,768]{1,0:T(8,128)}) custom-call(s32[4]{0:T(128)S(1)} %pad_add_fusion.place, bf16[8,16,896]{2,1,0:T(8,128)(2,1)S(1)} %bitcast.39, f32[8,896]{1,0:T(8,128)S(1)} %convert_add_fusion.late_ref, f32[64,8]{1,0:T(8,128)S(1)} %get-tuple-element.75.mixed_ref, bf16[8,3072]{1,0:T(8,128)(2,1)S(1)} %copy-done.1), custom_call_target="tpu_custom_call" | custom-call | flops 7340032 | bytes 917504 | tf_op jit(solution)/shard_map/adapter_late/pallas_call | solution.py:458
  (18 shorter events, 0.2 us)
Async XLA Ops:
  2.7 8.8 %collective-permute-start.2 = (bf16[32,768]{1,0:T(8,128)(2,1)S(1)}, bf16[32,768]{1,0:T(8,128)(2,1)S(1)}, u32[]{:S(2)}, u32[]{:S(2)}) collective-permute-start(bf16[32,768]{1,0:T(8,128)(2,1)S(1)} %get-tuple-element.88), channel_id=1, source_target_pairs={{0,3},{1,2},{2,1},{3,0},{4,7},{5,6},{6,5},{7,4},{8,11},{9,10},{10,... | collective-permute-start | bytes 147464 | tf_op jit(solution)/shard_map/ppermute | solution.py:471
  7.9 5.0 %collective-permute-start.1 = (bf16[32,768]{1,0:T(8,128)(2,1)S(1)}, bf16[32,768]{1,0:T(8,128)(2,1)S(1)}, u32[]{:S(2)}, u32[]{:S(2)}) collective-permute-start(bf16[32,768]{1,0:T(8,128)(2,1)S(1)} %get-tuple-element.89), channel_id=1, source_target_pairs={{0,2},{1,3},{2,0},{3,1},{4,6},{5,7},{6,4},{7,5},{8,10},{9,11},{10,... | collective-permute-start | bytes 147464 | tf_op jit(solution)/shard_map/ppermute | solution.py:471
  7.9 5.0 %collective-permute-start = (bf16[32,768]{1,0:T(8,128)(2,1)S(1)}, bf16[32,768]{1,0:T(8,128)(2,1)S(1)}, u32[]{:S(2)}, u32[]{:S(2)}) collective-permute-start(bf16[32,768]{1,0:T(8,128)(2,1)S(1)} %get-tuple-element.90), channel_id=1, source_target_pairs={{0,1},{1,0},{2,3},{3,2},{4,5},{5,4},{6,7},{7,6},{8,9},{9,8},{10,11... | collective-permute-start | bytes 147464 | tf_op jit(solution)/shard_map/ppermute | solution.py:471
  12.9 1.6 %collective-permute-start.3 = (bf16[4,32,768]{2,1,0:T(8,128)(2,1)S(1)}, bf16[4,32,768]{2,1,0:T(8,128)(2,1)S(1)}, u32[]{:S(2)}, u32[]{:S(2)}) collective-permute-start(bf16[4,32,768]{2,1,0:T(8,128)(2,1)S(1)} %pad_maximum_fusion.rows_ref), channel_id=1, source_target_pairs={{0,4},{4,0},{1,5},{5,1},{2,6},{6,2},{3,7},{7,3},{8,12},{12,8},{9,1... | collective-permute-start | bytes 589832 | tf_op jit(solution)/shard_map/ppermute | solution.py:471
  16.1 14.4 %collective-permute-start.4 = (bf16[64,4096]{1,0:T(8,128)(2,1)S(1)}, bf16[64,4096]{1,0:T(8,128)(2,1)S(1)}, u32[]{:S(2)}, u32[]{:S(2)}) collective-permute-start(bf16[64,4096]{1,0:T(8,128)(2,1)S(1)} %get-tuple-element.50), channel_id=1, source_target_pairs={{0,1},{1,0},{2,3},{3,2},{4,5},{5,4},{6,7},{7,6},{8,9},{9,8},{10,11... | collective-permute-start | bytes 1572872 | tf_op jit(solution)/shard_map/ppermute | solution.py:471
  16.8 19.9 %collective-permute-start.5 = (bf16[64,4096]{1,0:T(8,128)(2,1)S(1)}, bf16[64,4096]{1,0:T(8,128)(2,1)S(1)}, u32[]{:S(2)}, u32[]{:S(2)}) collective-permute-start(bf16[64,4096]{1,0:T(8,128)(2,1)S(1)} %get-tuple-element.60), channel_id=1, source_target_pairs={{1,2},{2,1},{5,6},{6,5},{9,10},{10,9},{13,14},{14,13},{17,18},{18,... | collective-permute-start | bytes 1572872 | tf_op jit(solution)/shard_map/ppermute | solution.py:518
  31.1 25.7 %collective-permute-start.6 = (bf16[64,4096]{1,0:T(8,128)(2,1)S(1)}, bf16[64,4096]{1,0:T(8,128)(2,1)S(1)}, u32[]{:S(2)}, u32[]{:S(2)}) collective-permute-start(bf16[64,4096]{1,0:T(8,128)(2,1)S(1)} %add_near.1), channel_id=1, source_target_pairs={{0,2},{1,3},{2,0},{3,1},{4,6},{5,7},{6,4},{7,5},{8,10},{9,11},{10,... | collective-permute-start | bytes 1572872 | tf_op jit(solution)/shard_map/ppermute | solution.py:471
  33.4 24.8 %copy-start = (bf16[1,1,64,4096]{3,2,1,0:T(8,128)(2,1)S(1)}, bf16[1,1,64,4096]{3,2,1,0:T(8,128)(2,1)}, u32[]{:S(2)}) copy-start(bf16[1,1,64,4096]{3,2,1,0:T(8,128)(2,1)} %param.16) | copy-start | bytes 1572868
  33.4 4.7 %collective-permute-start.8 = (bf16[4,16,768]{2,1,0:T(8,128)(2,1)S(1)}, bf16[4,16,768]{2,1,0:T(8,128)(2,1)S(1)}, u32[]{:S(2)}, u32[]{:S(2)}) collective-permute-start(bf16[4,16,768]{2,1,0:T(8,128)(2,1)S(1)} %get-tuple-element.80), channel_id=1, source_target_pairs={{0,8},{4,12},{8,0},{12,4},{16,24},{20,28},{24,16},{28,20},{1,9},{5... | collective-permute-start | bytes 294920 | tf_op jit(solution)/shard_map/ppermute | solution.py:476
  35.0 6.0 %collective-permute-start.14 = (bf16[4,16,768]{2,1,0:T(8,128)(2,1)S(1)}, bf16[4,16,768]{2,1,0:T(8,128)(2,1)S(1)}, u32[]{:S(2)}, u32[]{:S(2)}) collective-permute-start(bf16[4,16,768]{2,1,0:T(8,128)(2,1)S(1)} %get-tuple-element.81), channel_id=1, source_target_pairs={{0,28},{4,24},{8,20},{12,16},{16,12},{20,8},{24,4},{28,0},{1,29},{... | collective-permute-start | bytes 294920 | tf_op jit(solution)/shard_map/ppermute | solution.py:476
  35.2 7.3 %collective-permute-start.13 = (bf16[4,16,768]{2,1,0:T(8,128)(2,1)S(1)}, bf16[4,16,768]{2,1,0:T(8,128)(2,1)S(1)}, u32[]{:S(2)}, u32[]{:S(2)}) collective-permute-start(bf16[4,16,768]{2,1,0:T(8,128)(2,1)S(1)} %get-tuple-element.82), channel_id=1, source_target_pairs={{0,20},{4,16},{8,28},{12,24},{16,4},{20,0},{24,12},{28,8},{1,21},{... | collective-permute-start | bytes 294920 | tf_op jit(solution)/shard_map/ppermute | solution.py:476
  36.7 6.7 %collective-permute-start.12 = (bf16[4,16,768]{2,1,0:T(8,128)(2,1)S(1)}, bf16[4,16,768]{2,1,0:T(8,128)(2,1)S(1)}, u32[]{:S(2)}, u32[]{:S(2)}) collective-permute-start(bf16[4,16,768]{2,1,0:T(8,128)(2,1)S(1)} %get-tuple-element.83), channel_id=1, source_target_pairs={{0,12},{4,8},{8,4},{12,0},{16,28},{20,24},{24,20},{28,16},{1,13},{... | collective-permute-start | bytes 294920 | tf_op jit(solution)/shard_map/ppermute | solution.py:476
  38.1 5.5 %collective-permute-start.11 = (bf16[4,16,768]{2,1,0:T(8,128)(2,1)S(1)}, bf16[4,16,768]{2,1,0:T(8,128)(2,1)S(1)}, u32[]{:S(2)}, u32[]{:S(2)}) collective-permute-start(bf16[4,16,768]{2,1,0:T(8,128)(2,1)S(1)} %get-tuple-element.84), channel_id=1, source_target_pairs={{0,4},{4,0},{8,12},{12,8},{16,20},{20,16},{24,28},{28,24},{1,5},{5... | collective-permute-start | bytes 294920 | tf_op jit(solution)/shard_map/ppermute | solution.py:476
  41.0 5.9 %collective-permute-start.10 = (bf16[4,16,768]{2,1,0:T(8,128)(2,1)S(1)}, bf16[4,16,768]{2,1,0:T(8,128)(2,1)S(1)}, u32[]{:S(2)}, u32[]{:S(2)}) collective-permute-start(bf16[4,16,768]{2,1,0:T(8,128)(2,1)S(1)} %get-tuple-element.85), channel_id=1, source_target_pairs={{0,24},{4,28},{8,16},{12,20},{16,8},{20,12},{24,0},{28,4},{1,25},{... | collective-permute-start | bytes 294920 | tf_op jit(solution)/shard_map/ppermute | solution.py:476
  42.5 6.4 %collective-permute-start.9 = (bf16[4,16,768]{2,1,0:T(8,128)(2,1)S(1)}, bf16[4,16,768]{2,1,0:T(8,128)(2,1)S(1)}, u32[]{:S(2)}, u32[]{:S(2)}) collective-permute-start(bf16[4,16,768]{2,1,0:T(8,128)(2,1)S(1)} %get-tuple-element.86), channel_id=1, source_target_pairs={{0,16},{4,20},{8,24},{12,28},{16,0},{20,4},{24,8},{28,12},{1,17},{... | collective-permute-start | bytes 294920 | tf_op jit(solution)/shard_map/ppermute | solution.py:476
  43.4 14.4 %collective-permute-start.15 = (bf16[32,3328]{1,0:T(8,128)(2,1)S(1)}, bf16[32,3328]{1,0:T(8,128)(2,1)S(1)}, u32[]{:S(2)}, u32[]{:S(2)}) collective-permute-start(bf16[32,3328]{1,0:T(8,128)(2,1)S(1)} %get-tuple-element.64.picked_ref), channel_id=1, source_target_pairs={{0,4},{4,0},{1,5},{5,1},{2,6},{6,2},{3,7},{7,3},{8,12},{12,8},{9,1... | collective-permute-start | bytes 638984 | tf_op jit(solution)/shard_map/ppermute | solution.py:471
  43.6 14.6 %collective-permute-start.7 = (bf16[64,4096]{1,0:T(8,128)(2,1)S(1)}, bf16[64,4096]{1,0:T(8,128)(2,1)S(1)}, u32[]{:S(2)}, u32[]{:S(2)}) collective-permute-start(bf16[64,4096]{1,0:T(8,128)(2,1)S(1)} %get-tuple-element.60), channel_id=1, source_target_pairs={{0,1},{3,2},{4,5},{7,6},{8,9},{11,10},{12,13},{15,14},{16,17},{19,... | collective-permute-start | bytes 1572872 | tf_op jit(solution)/shard_map/ppermute | solution.py:527
  56.9 21.9 %copy-start.1 = (bf16[8,3072]{1,0:T(8,128)(2,1)S(1)}, bf16[8,3072]{1,0:T(8,128)(2,1)}, u32[]{:S(2)}) copy-start(bf16[8,3072]{1,0:T(8,128)(2,1)} %router_ref.3) | copy-start | bytes 147460
  59.7 6.4 %collective-permute-start.16 = (bf16[2,24,896]{2,1,0:T(8,128)(2,1)S(1)}, bf16[2,24,896]{2,1,0:T(8,128)(2,1)S(1)}, u32[]{:S(2)}, u32[]{:S(2)}) collective-permute-start(bf16[2,24,896]{2,1,0:T(8,128)(2,1)S(1)} %slice.174), channel_id=1, source_target_pairs={{0,2},{1,3},{2,0},{3,1},{4,6},{5,7},{6,4},{7,5},{8,10},{9,11},{10,... | collective-permute-start | bytes 258056 | tf_op jit(solution)/shard_map/ppermute | solution.py:471
  66.1 4.1 %collective-permute-start.18 = (bf16[24,896]{1,0:T(8,128)(2,1)S(1)}, bf16[24,896]{1,0:T(8,128)(2,1)S(1)}, u32[]{:S(2)}, u32[]{:S(2)}) collective-permute-start(bf16[24,896]{1,0:T(8,128)(2,1)S(1)} %fusion), channel_id=1, source_target_pairs={{0,1},{1,0},{2,3},{3,2},{4,5},{5,4},{6,7},{7,6},{8,9},{9,8},{10,11... | collective-permute-start | bytes 129032 | tf_op jit(solution)/shard_map/ppermute | solution.py:471
  70.3 5.0 %collective-permute-start.21 = (bf16[24,896]{1,0:T(8,128)(2,1)S(1)}, bf16[24,896]{1,0:T(8,128)(2,1)S(1)}, u32[]{:S(2)}, u32[]{:S(2)}) collective-permute-start(bf16[24,896]{1,0:T(8,128)(2,1)S(1)} %pad_maximum_fusion.1), channel_id=1, source_target_pairs={{0,24},{8,16},{16,8},{24,0},{1,25},{9,17},{17,9},{25,1},{2,26},{10... | collective-permute-start | bytes 129032 | tf_op jit(solution)/shard_map/ppermute | solution.py:471
  72.3 4.0 %collective-permute-start.20 = (bf16[24,896]{1,0:T(8,128)(2,1)S(1)}, bf16[24,896]{1,0:T(8,128)(2,1)S(1)}, u32[]{:S(2)}, u32[]{:S(2)}) collective-permute-start(bf16[24,896]{1,0:T(8,128)(2,1)S(1)} %pad_maximum_fusion.1), channel_id=1, source_target_pairs={{0,16},{8,24},{16,0},{24,8},{1,17},{9,25},{17,1},{25,9},{2,18},{10... | collective-permute-start | bytes 129032 | tf_op jit(solution)/shard_map/ppermute | solution.py:471
  73.3 4.0 %collective-permute-start.19 = (bf16[24,896]{1,0:T(8,128)(2,1)S(1)}, bf16[24,896]{1,0:T(8,128)(2,1)S(1)}, u32[]{:S(2)}, u32[]{:S(2)}) collective-permute-start(bf16[24,896]{1,0:T(8,128)(2,1)S(1)} %pad_maximum_fusion.1), channel_id=1, source_target_pairs={{0,8},{8,0},{16,24},{24,16},{1,9},{9,1},{17,25},{25,17},{2,10},{10... | collective-permute-start | bytes 129032 | tf_op jit(solution)/shard_map/ppermute | solution.py:471
  77.4 2.7 %collective-permute-start.22 = (bf16[72,896]{1,0:T(8,128)(2,1)S(1)}, bf16[72,896]{1,0:T(8,128)(2,1)S(1)}, u32[]{:S(2)}, u32[]{:S(2)}) collective-permute-start(bf16[72,896]{1,0:T(8,128)(2,1)S(1)} %get-tuple-element.91), channel_id=1, source_target_pairs={{0,4},{4,0},{1,5},{5,1},{2,6},{6,2},{3,7},{7,3},{8,12},{12,8},{9,1... | collective-permute-start | bytes 387080 | tf_op jit(solution)/shard_map/ppermute | solution.py:471
  77.4 1.4 %collective-permute-start.17 = (f32[32,128]{1,0:T(8,128)S(1)}, f32[32,128]{1,0:T(8,128)S(1)}, u32[]{:S(2)}, u32[]{:S(2)}) collective-permute-start(f32[32,128]{1,0:T(8,128)S(1)} %get-tuple-element.73), channel_id=1, source_target_pairs={{0,4},{4,0},{1,5},{5,1},{2,6},{6,2},{3,7},{7,3},{8,12},{12,8},{9,1... | collective-permute-start | bytes 49160 | tf_op jit(solution)/shard_map/ppermute | solution.py:471

commit v5 on v4

--- a/solution.py
+++ b/solution.py
@@ -548,6 +548,7 @@
     mine = jnp.concatenate([late.astype(BF16), early], 0)
     got = [swap(mine, "dp", 4, k) for k in range(1, 4)]
     token_grad = token_gradient(prob, prob_got, slots, info, router_matrix, 4)
+    got, token_grad = lax.optimization_barrier((got, token_grad))
     late = late + sum(other[:experts].astype(F32) for other in got)
     early = jnp.concatenate([early] + [other[experts:] for other in got], 0)
     got = swap(jnp.concatenate([late.astype(BF16), early], 0), "expert", 2, 1)

time: 81.8 us -> 80.5 us (0.984)
  no operation moved by 1% of the time
where the time goes in v5:
time: 80.5 us; the launch traced here: 80.3 us
  waiting for transfers between devices  32.8 us (41%)
  starting transfers between devices  27.3 us (34%)
  Pallas kernels  18.7 us (23%)
  between operations  0.91 us (1%)
    ppermute x14, waiting for transfers between devices, swap(): return lax.ppermute(value, axis, xor_pairs(count, bits))  27.2 us
    ppermute x14, starting transfers between devices, swap(): return lax.ppermute(value, axis, xor_pairs(count, bits))  16.6 us
    ppermute x7, starting transfers between devices, swap_group(): return lax.ppermute(value, ('dp', 'expert'), pairs)  6.84 us
    ppermute x7, waiting for transfers between devices, swap_group(): return lax.ppermute(value, ('dp', 'expert'), pairs)  5.11 us
    pallas_call x1, Pallas kernels, adapter_early(): pl.pallas_call(adapter_kernel, out_shape=(jax.ShapeDtypeStruct((groups, s...  3.47 us
    ppermute x1, starting transfers between devices, direct_device(): outer = lax.ppermute(last, 'shard', [(0, 1), (3, 2)])  3.24 us
    pallas_call x2, Pallas kernels, products(): pl.pallas_call(functools.partial(product_kernel, len(before) // 4), out_s...  3.07 us
    pallas_call x1, Pallas kernels, dequantize(): pl.pallas_call(weight_kernel, out_shape=pltpu.VMEM(codes.shape, BF16), in...  3.05 us
  transfers between devices with their start and end apart: 23, of which 13 were waited for; matrix products, arithmetic and copies ran while one was open for 0% of the time, Pallas kernels for 15%

profile of v5, /device:TPU:0, one launch (start us, length us, event | category | flops | bytes accessed | tf_op | source)
XLA Modules:
  0.0 80.3 jit_solution(6103516377393696477)
XLA Ops:
  0.6 0.1 pad_add_fusion.place
  0.7 2.0 %route.1 = (bf16[4,32,768]{2,1,0:T(8,128)(2,1)S(1)}, f32[32,128]{1,0:T(8,128)S(1)}, f32[16,128]{1,0:T(8,128)S(1)}) custom-call(s32[4]{0:T(128)S(1)} %pad_add_fusion.place, f32[8,128]{1,0:T(8,128)} %bitcast.44, s32[2,128]{1,0:T(2,128)} %bitcast.45, bf16[128,3072]{1,0:T(8,128)(2,1)} %grad_hbm.3), custom_call_target="tpu_custom_call" | custom-call | flops 25165824 | bytes 786432 | tf_op jit(solution)/shard_map/route/pallas_call | solution.py:96
  2.7 5.1 %collective-permute-start.2 = (bf16[32,768]{1,0:T(8,128)(2,1)S(1)}, bf16[32,768]{1,0:T(8,128)(2,1)S(1)}, u32[]{:S(2)}, u32[]{:S(2)}) collective-permute-start(bf16[32,768]{1,0:T(8,128)(2,1)S(1)} %get-tuple-element.96), channel_id=1, source_target_pairs={{0,3},{1,2},{2,1},{3,0},{4,7},{5,6},{6,5},{7,4},{8,11},{9,10},{10,... | collective-permute-start | bytes 147464 | tf_op jit(solution)/shard_map/ppermute | solution.py:471
  7.9 0.0 collective-permute-start.1
  7.9 0.6 collective-permute-start
  8.5 3.1 %dequantize.1.weight_ref = bf16[768,4096]{1,0:T(8,128)(2,1)S(1)} custom-call(bf16[768,4096]{1,0:T(8,128)(2,1)} %codes_hbm.1, bf16[12,4096]{1,0:T(8,128)(2,1)} %scales_hbm.1), custom_call_target="tpu_custom_call" | custom-call | flops 3145728 | bytes 12582912 | tf_op jit(solution)/shard_map/dequantize/pallas_call | solution.py:213
  11.6 0.0 collective-permute-done.2
  11.6 1.3 %collective-permute-done.1 = bf16[32,768]{1,0:T(8,128)(2,1)S(1)} collective-permute-done((bf16[32,768]{1,0:T(8,128)(2,1)S(1)}, bf16[32,768]{1,0:T(8,128)(2,1)S(1)}, u32[]{:S(2)}, u32[]{:S(2)}) %collective-permute-start.1) | collective-permute-done | bytes 49184 | tf_op jit(solution)/shard_map/ppermute | solution.py:471
  12.8 0.0 collective-permute-done
  12.9 0.1 collective-permute-start.3
  13.0 1.5 %products.2 = (bf16[64,4096]{1,0:T(8,128)(2,1)S(1)}, bf16[64,4096]{1,0:T(8,128)(2,1)S(1)}, bf16[64,4096]{1,0:T(8,128)(2,1)S(1)}, f32[64,4096]{1,0:T(8,128)S(1)}) custom-call(s32[4]{0:T(128)S(1)} %pad_add_fusion.place, bf16[4,32,768]{2,1,0:T(8,128)(2,1)S(1)} %pad_maximum_fusion.rows_ref, bf16[768,4096]{1,0:T(8,128)(2,1)S(1)} %dequantize.1.weight_ref), custom_call_target="tpu_custom_call" | custom-call | flops 805306368 | bytes 6291456 | tf_op jit(solution)/shard_map/products/pallas_call | solution.py:137
  14.5 0.0 collective-permute-done.3.rows_ref
  14.5 1.5 %products.3 = (bf16[64,4096]{1,0:T(8,128)(2,1)S(1)}, bf16[64,4096]{1,0:T(8,128)(2,1)S(1)}, bf16[64,4096]{1,0:T(8,128)(2,1)S(1)}, f32[64,4096]{1,0:T(8,128)S(1)}) custom-call(s32[4]{0:T(128)S(1)} %pad_add_fusion.place, ...), custom_call_target="tpu_custom_call", output_to_operand_aliasing={{0}: (3, {}), {1}: (4, {}), {2}: (5, {}), {3}: (6, {})} | custom-call | flops 805306368 | bytes 6291456 | tf_op jit(solution)/shard_map/products/pallas_call | solution.py:137
  16.1 0.7 collective-permute-start.4
  16.8 0.7 collective-permute-start.5
  17.4 3.5 %adapter_early.1 = (f32[8,4,16,768]{3,2,1,0:T(8,128)S(1)}, bf16[32,3328]{1,0:T(8,128)(2,1)S(1)}, f32[64,8]{1,0:T(8,128)S(1)}) custom-call(s32[4]{0:T(128)S(1)} %pad_add_fusion.place, bf16[128,3072]{1,0:T(8,128)(2,1)} %grad_hbm.3, bf16[128,3072]{1,0:T(8,128)(2,1)} %context_hbm.1, bf16[64,3072]{1,0:T(8,128)(2,1)} %down_hbm.1, bf16[64,3072]{1,0:T(8,128)(2,1)} %up_hbm.1, ...), custom_call_target="tpu_custom_call" | custom-call | tf_op jit(solution)/shard_map/adapter_early/pallas_call | solution.py:283
  20.9 9.5 %collective-permute-done.4.near_ref = bf16[64,4096]{1,0:T(8,128)(2,1)S(1)} collective-permute-done((bf16[64,4096]{1,0:T(8,128)(2,1)S(1)}, bf16[64,4096]{1,0:T(8,128)(2,1)S(1)}, u32[]{:S(2)}, u32[]{:S(2)}) %collective-permute-start.4) | collective-permute-done | bytes 524320 | tf_op jit(solution)/shard_map/ppermute | solution.py:471
  30.4 0.7 add_near.1
  31.1 2.1 %collective-permute-start.6 = (bf16[64,4096]{1,0:T(8,128)(2,1)S(1)}, bf16[64,4096]{1,0:T(8,128)(2,1)S(1)}, u32[]{:S(2)}, u32[]{:S(2)}) collective-permute-start(bf16[64,4096]{1,0:T(8,128)(2,1)S(1)} %add_near.1), channel_id=1, source_target_pairs={{0,2},{1,3},{2,0},{3,1},{4,6},{5,7},{6,4},{7,5},{8,10},{9,11},{10,... | collective-permute-start | bytes 1572872 | tf_op jit(solution)/shard_map/ppermute | solution.py:471
  33.2 0.1 convert_element_type.57
  33.3 0.1 slice_bitcast_fusion.6
  33.4 0.0 copy-start
  33.4 1.6 %collective-permute-start.8 = (bf16[4,16,768]{2,1,0:T(8,128)(2,1)S(1)}, bf16[4,16,768]{2,1,0:T(8,128)(2,1)S(1)}, u32[]{:S(2)}, u32[]{:S(2)}) collective-permute-start(bf16[4,16,768]{2,1,0:T(8,128)(2,1)S(1)} %get-tuple-element.88), channel_id=1, source_target_pairs={{0,8},{4,12},{8,0},{12,4},{16,24},{20,28},{24,16},{28,20},{1,9},{5... | collective-permute-start | bytes 294920 | tf_op jit(solution)/shard_map/ppermute | solution.py:476
  35.0 0.3 collective-permute-start.14
  35.2 1.5 %collective-permute-start.13 = (bf16[4,16,768]{2,1,0:T(8,128)(2,1)S(1)}, bf16[4,16,768]{2,1,0:T(8,128)(2,1)S(1)}, u32[]{:S(2)}, u32[]{:S(2)}) collective-permute-start(bf16[4,16,768]{2,1,0:T(8,128)(2,1)S(1)} %get-tuple-element.90), channel_id=1, source_target_pairs={{0,20},{4,16},{8,28},{12,24},{16,4},{20,0},{24,12},{28,8},{1,21},{... | collective-permute-start | bytes 294920 | tf_op jit(solution)/shard_map/ppermute | solution.py:476
  36.7 0.0 collective-permute-done.5.middle_ref
  36.7 1.0 %collective-permute-start.12 = (bf16[4,16,768]{2,1,0:T(8,128)(2,1)S(1)}, bf16[4,16,768]{2,1,0:T(8,128)(2,1)S(1)}, u32[]{:S(2)}, u32[]{:S(2)}) collective-permute-start(bf16[4,16,768]{2,1,0:T(8,128)(2,1)S(1)} %get-tuple-element.91), channel_id=1, source_target_pairs={{0,12},{4,8},{8,4},{12,0},{16,28},{20,24},{24,20},{28,16},{1,13},{... | collective-permute-start | bytes 294920 | tf_op jit(solution)/shard_map/ppermute | solution.py:476
  37.7 0.4 collective-permute-done.8
  38.1 0.2 collective-permute-start.11
  38.3 2.7 %collective-permute-done.14 = bf16[4,16,768]{2,1,0:T(8,128)(2,1)S(1)} collective-permute-done((bf16[4,16,768]{2,1,0:T(8,128)(2,1)S(1)}, bf16[4,16,768]{2,1,0:T(8,128)(2,1)S(1)}, u32[]{:S(2)}, u32[]{:S(2)}) %collective-permute-start.14) | collective-permute-done | bytes 98336 | tf_op jit(solution)/shard_map/ppermute | solution.py:476
  41.0 1.5 %collective-permute-start.10 = (bf16[4,16,768]{2,1,0:T(8,128)(2,1)S(1)}, bf16[4,16,768]{2,1,0:T(8,128)(2,1)S(1)}, u32[]{:S(2)}, u32[]{:S(2)}) collective-permute-start(bf16[4,16,768]{2,1,0:T(8,128)(2,1)S(1)} %get-tuple-element.93), channel_id=1, source_target_pairs={{0,24},{4,28},{8,16},{12,20},{16,8},{20,12},{24,0},{28,4},{1,25},{... | collective-permute-start | bytes 294920 | tf_op jit(solution)/shard_map/ppermute | solution.py:476
  42.5 0.0 collective-permute-done.13
  42.5 0.8 %collective-permute-start.9 = (bf16[4,16,768]{2,1,0:T(8,128)(2,1)S(1)}, bf16[4,16,768]{2,1,0:T(8,128)(2,1)S(1)}, u32[]{:S(2)}, u32[]{:S(2)}) collective-permute-start(bf16[4,16,768]{2,1,0:T(8,128)(2,1)S(1)} %get-tuple-element.94), channel_id=1, source_target_pairs={{0,16},{4,20},{8,24},{12,28},{16,0},{20,4},{24,8},{28,12},{1,17},{... | collective-permute-start | bytes 294920 | tf_op jit(solution)/shard_map/ppermute | solution.py:476
  43.4 0.0 collective-permute-done.12
  43.4 0.3 collective-permute-start.15
  43.6 0.0 collective-permute-done.11
  43.6 3.2 %collective-permute-start.7 = (bf16[64,4096]{1,0:T(8,128)(2,1)S(1)}, bf16[64,4096]{1,0:T(8,128)(2,1)S(1)}, u32[]{:S(2)}, u32[]{:S(2)}) collective-permute-start(bf16[64,4096]{1,0:T(8,128)(2,1)S(1)} %get-tuple-element.64), channel_id=1, source_target_pairs={{0,1},{3,2},{4,5},{7,6},{8,9},{11,10},{12,13},{15,14},{16,17},{19,... | collective-permute-start | bytes 1572872 | tf_op jit(solution)/shard_map/ppermute | solution.py:527
  46.9 0.0 collective-permute-done.10
  46.9 2.0 %collective-permute-done.9 = bf16[4,16,768]{2,1,0:T(8,128)(2,1)S(1)} collective-permute-done((bf16[4,16,768]{2,1,0:T(8,128)(2,1)S(1)}, bf16[4,16,768]{2,1,0:T(8,128)(2,1)S(1)}, u32[]{:S(2)}, u32[]{:S(2)}) %collective-permute-start.9) | collective-permute-done | bytes 98336 | tf_op jit(solution)/shard_map/ppermute | solution.py:476
  48.9 0.1 bitcast_add_fusion
  49.0 7.9 %collective-permute-done.6.far_ref = bf16[64,4096]{1,0:T(8,128)(2,1)S(1)} collective-permute-done((bf16[64,4096]{1,0:T(8,128)(2,1)S(1)}, bf16[64,4096]{1,0:T(8,128)(2,1)S(1)}, u32[]{:S(2)}, u32[]{:S(2)}) %collective-permute-start.6) | collective-permute-done | bytes 524320 | tf_op jit(solution)/shard_map/ppermute | solution.py:471
  56.9 0.8 %add_far.1.partial_ref = f32[64,4096]{1,0:T(8,128)S(1)} custom-call(s32[4]{0:T(128)S(1)} %pad_add_fusion.place, f32[64,4096]{1,0:T(8,128)S(1)} %get-tuple-element.52.own_ref, bf16[64,4096]{1,0:T(8,128)(2,1)S(1)} %collective-permute-done.4.near_ref, bf16[64,4096]{1,0:T(8,128)(2,1)S(1)} %collective-permute-done.5.middle_ref, ...), custom_call_target="tpu_custom_call" | custom-call | flops 3000000000 | bytes 3670016 | tf_op jit(solution)/shard_map/add_far/pallas_call | solution.py:178
  57.7 0.0 collective-permute-done.15.other_ref
  57.7 0.5 collective-permute-done.7.outer_ref
  58.2 0.0 copy-done
  58.2 1.4 %finish.1 = (f32[64,4096]{1,0:T(8,128)S(1)}, f32[32,128]{1,0:T(8,128)S(1)}, f32[32,128]{1,0:T(8,128)S(1)}, f32[4,8,896]{2,1,0:T(8,128)S(1)}) custom-call(s32[4]{0:T(128)S(1)} %pad_add_fusion.place, f32[64,4096]{1,0:T(8,128)S(1)} %add_far.1.partial_ref, bf16[64,4096]{1,0:T(8,128)(2,1)S(1)} %collective-permute-done.7.outer_ref, bf16[64,4096]{1,0:T(8,128)(2,1)S(1)} %bitcast.38, ...), custom_call_target="tpu_custom_call" | custom-call | flops 2097152 | bytes 2621440 | tf_op jit(solution)/shard_map/finish/pallas_call | solution.py:380
  59.7 2.4 %collective-permute-start.16 = (bf16[2,24,896]{2,1,0:T(8,128)(2,1)S(1)}, bf16[2,24,896]{2,1,0:T(8,128)(2,1)S(1)}, u32[]{:S(2)}, u32[]{:S(2)}) collective-permute-start(bf16[2,24,896]{2,1,0:T(8,128)(2,1)S(1)} %slice.168), channel_id=1, source_target_pairs={{0,2},{1,3},{2,0},{3,1},{4,6},{5,7},{6,4},{7,5},{8,10},{9,11},{10,... | collective-permute-start | bytes 258056 | tf_op jit(solution)/shard_map/ppermute | solution.py:471
  62.1 1.4 %hidden_gradient.1 = bf16[64,4096]{1,0:T(8,128)(2,1)} custom-call(s32[4]{0:T(128)S(1)} %pad_add_fusion.place, f32[64,4096]{1,0:T(8,128)S(1)} %get-tuple-element.74.product_ref, bf16[32,3328]{1,0:T(8,128)(2,1)S(1)} %get-tuple-element.68.picked_ref, bf16[32,3328]{1,0:T(8,128)(2,1)S(1)} %collective-permute-done.15.other_ref), custom_call_target="tpu_custom_call" | custom-call | tf_op jit(solution)/shard_map/hidden_gradient/pallas_call | solution.py:364
  63.6 2.5 %collective-permute-done.16 = bf16[2,24,896]{2,1,0:T(8,128)(2,1)S(1)} collective-permute-done((bf16[2,24,896]{2,1,0:T(8,128)(2,1)S(1)}, bf16[2,24,896]{2,1,0:T(8,128)(2,1)S(1)}, u32[]{:S(2)}, u32[]{:S(2)}) %collective-permute-start.16) | collective-permute-done | bytes 86048 | tf_op jit(solution)/shard_map/ppermute | solution.py:471
  66.1 1.6 %collective-permute-start.17 = (bf16[24,896]{1,0:T(8,128)(2,1)S(1)}, bf16[24,896]{1,0:T(8,128)(2,1)S(1)}, u32[]{:S(2)}, u32[]{:S(2)}) collective-permute-start(bf16[24,896]{1,0:T(8,128)(2,1)S(1)} %fusion), channel_id=1, source_target_pairs={{0,1},{1,0},{2,3},{3,2},{4,5},{5,4},{6,7},{7,6},{8,9},{9,8},{10,11... | collective-permute-start | bytes 129032 | tf_op jit(solution)/shard_map/ppermute | solution.py:471
  67.7 2.5 %collective-permute-done.17 = bf16[24,896]{1,0:T(8,128)(2,1)S(1)} collective-permute-done((bf16[24,896]{1,0:T(8,128)(2,1)S(1)}, bf16[24,896]{1,0:T(8,128)(2,1)S(1)}, u32[]{:S(2)}, u32[]{:S(2)}) %collective-permute-start.17) | collective-permute-done | bytes 43040 | tf_op jit(solution)/shard_map/ppermute | solution.py:471
  70.3 2.1 %collective-permute-start.20 = (bf16[24,896]{1,0:T(8,128)(2,1)S(1)}, bf16[24,896]{1,0:T(8,128)(2,1)S(1)}, u32[]{:S(2)}, u32[]{:S(2)}) collective-permute-start(bf16[24,896]{1,0:T(8,128)(2,1)S(1)} %pad_maximum_fusion.1), channel_id=1, source_target_pairs={{0,24},{8,16},{16,8},{24,0},{1,25},{9,17},{17,9},{25,1},{2,26},{10... | collective-permute-start | bytes 129032 | tf_op jit(solution)/shard_map/ppermute | solution.py:471
  72.3 0.9 %collective-permute-start.19 = (bf16[24,896]{1,0:T(8,128)(2,1)S(1)}, bf16[24,896]{1,0:T(8,128)(2,1)S(1)}, u32[]{:S(2)}, u32[]{:S(2)}) collective-permute-start(bf16[24,896]{1,0:T(8,128)(2,1)S(1)} %pad_maximum_fusion.1), channel_id=1, source_target_pairs={{0,16},{8,24},{16,0},{24,8},{1,17},{9,25},{17,1},{25,9},{2,18},{10... | collective-permute-start | bytes 129032 | tf_op jit(solution)/shard_map/ppermute | solution.py:471
  73.3 0.5 collective-permute-start.18
  73.8 0.0 collective-permute-start.21
  73.8 1.2 %collective-permute-done.21.prob_got_ref = f32[32,128]{1,0:T(8,128)S(1)} collective-permute-done((f32[32,128]{1,0:T(8,128)S(1)}, f32[32,128]{1,0:T(8,128)S(1)}, u32[]{:S(2)}, u32[]{:S(2)}) %collective-permute-start.21) | collective-permute-done | bytes 16416 | tf_op jit(solution)/shard_map/ppermute | solution.py:471
  75.0 0.0 copy-done.1
  75.0 1.2 %token_gradient.1 = bf16[128,3072]{1,0:T(8,128)(2,1)} custom-call(f32[32,128]{1,0:T(8,128)S(1)} %get-tuple-element.77.prob_ref, f32[32,128]{1,0:T(8,128)S(1)} %collective-permute-done.21.prob_got_ref, f32[32,128]{1,0:T(8,128)S(1)} %get-tuple-element.57.slots_ref, f32[16,128]{1,0:T(8,128)S(1)} %get-tuple-element.58.info_ref, bf16[8,3072]{1,0:T(8,128)(2,1)S(1)} %copy-done.1), custom_call_target="tpu_custom_call" | custom-call | flops 6291456 | bytes 786432 | tf_op jit(solution)/shard_map/token_gradient/pallas_call | solution.py:417
  76.2 0.0 collective-permute-done.20
  76.3 0.1 collective-permute-done.19
  76.3 0.9 %collective-permute-done.18 = bf16[24,896]{1,0:T(8,128)(2,1)S(1)} collective-permute-done((bf16[24,896]{1,0:T(8,128)(2,1)S(1)}, bf16[24,896]{1,0:T(8,128)(2,1)S(1)}, u32[]{:S(2)}, u32[]{:S(2)}) %collective-permute-start.18) | collective-permute-done | bytes 43040 | tf_op jit(solution)/shard_map/ppermute | solution.py:471
  77.4 0.1 collective-permute-start.22
  77.4 1.3 %collective-permute-done.22 = bf16[72,896]{1,0:T(8,128)(2,1)S(1)} collective-permute-done((bf16[72,896]{1,0:T(8,128)(2,1)S(1)}, bf16[72,896]{1,0:T(8,128)(2,1)S(1)}, u32[]{:S(2)}, u32[]{:S(2)}) %collective-permute-start.22) | collective-permute-done | bytes 129056 | tf_op jit(solution)/shard_map/ppermute | solution.py:471
  78.8 1.5 %adapter_late.1 = (f32[64,768]{1,0:T(8,128)}, f32[64,768]{1,0:T(8,128)}) custom-call(s32[4]{0:T(128)S(1)} %pad_add_fusion.place, bf16[8,16,896]{2,1,0:T(8,128)(2,1)S(1)} %bitcast.39, f32[8,896]{1,0:T(8,128)S(1)} %convert_add_fusion.late_ref, f32[64,8]{1,0:T(8,128)S(1)} %get-tuple-element.83.mixed_ref, bf16[8,3072]{1,0:T(8,128)(2,1)S(1)} %copy-done.1), custom_call_target="tpu_custom_call" | custom-call | flops 7340032 | bytes 917504 | tf_op jit(solution)/shard_map/adapter_late/pallas_call | solution.py:458
  (18 shorter events, 0.2 us)
Async XLA Ops:
  2.7 8.8 %collective-permute-start.2 = (bf16[32,768]{1,0:T(8,128)(2,1)S(1)}, bf16[32,768]{1,0:T(8,128)(2,1)S(1)}, u32[]{:S(2)}, u32[]{:S(2)}) collective-permute-start(bf16[32,768]{1,0:T(8,128)(2,1)S(1)} %get-tuple-element.96), channel_id=1, source_target_pairs={{0,3},{1,2},{2,1},{3,0},{4,7},{5,6},{6,5},{7,4},{8,11},{9,10},{10,... | collective-permute-start | bytes 147464 | tf_op jit(solution)/shard_map/ppermute | solution.py:471
  7.9 5.0 %collective-permute-start.1 = (bf16[32,768]{1,0:T(8,128)(2,1)S(1)}, bf16[32,768]{1,0:T(8,128)(2,1)S(1)}, u32[]{:S(2)}, u32[]{:S(2)}) collective-permute-start(bf16[32,768]{1,0:T(8,128)(2,1)S(1)} %get-tuple-element.97), channel_id=1, source_target_pairs={{0,2},{1,3},{2,0},{3,1},{4,6},{5,7},{6,4},{7,5},{8,10},{9,11},{10,... | collective-permute-start | bytes 147464 | tf_op jit(solution)/shard_map/ppermute | solution.py:471
  7.9 5.0 %collective-permute-start = (bf16[32,768]{1,0:T(8,128)(2,1)S(1)}, bf16[32,768]{1,0:T(8,128)(2,1)S(1)}, u32[]{:S(2)}, u32[]{:S(2)}) collective-permute-start(bf16[32,768]{1,0:T(8,128)(2,1)S(1)} %get-tuple-element.98), channel_id=1, source_target_pairs={{0,1},{1,0},{2,3},{3,2},{4,5},{5,4},{6,7},{7,6},{8,9},{9,8},{10,11... | collective-permute-start | bytes 147464 | tf_op jit(solution)/shard_map/ppermute | solution.py:471
  12.9 1.6 %collective-permute-start.3 = (bf16[4,32,768]{2,1,0:T(8,128)(2,1)S(1)}, bf16[4,32,768]{2,1,0:T(8,128)(2,1)S(1)}, u32[]{:S(2)}, u32[]{:S(2)}) collective-permute-start(bf16[4,32,768]{2,1,0:T(8,128)(2,1)S(1)} %pad_maximum_fusion.rows_ref), channel_id=1, source_target_pairs={{0,4},{4,0},{1,5},{5,1},{2,6},{6,2},{3,7},{7,3},{8,12},{12,8},{9,1... | collective-permute-start | bytes 589832 | tf_op jit(solution)/shard_map/ppermute | solution.py:471
  16.1 14.4 %collective-permute-start.4 = (bf16[64,4096]{1,0:T(8,128)(2,1)S(1)}, bf16[64,4096]{1,0:T(8,128)(2,1)S(1)}, u32[]{:S(2)}, u32[]{:S(2)}) collective-permute-start(bf16[64,4096]{1,0:T(8,128)(2,1)S(1)} %get-tuple-element.54), channel_id=1, source_target_pairs={{0,1},{1,0},{2,3},{3,2},{4,5},{5,4},{6,7},{7,6},{8,9},{9,8},{10,11... | collective-permute-start | bytes 1572872 | tf_op jit(solution)/shard_map/ppermute | solution.py:471
  16.8 19.9 %collective-permute-start.5 = (bf16[64,4096]{1,0:T(8,128)(2,1)S(1)}, bf16[64,4096]{1,0:T(8,128)(2,1)S(1)}, u32[]{:S(2)}, u32[]{:S(2)}) collective-permute-start(bf16[64,4096]{1,0:T(8,128)(2,1)S(1)} %get-tuple-element.64), channel_id=1, source_target_pairs={{1,2},{2,1},{5,6},{6,5},{9,10},{10,9},{13,14},{14,13},{17,18},{18,... | collective-permute-start | bytes 1572872 | tf_op jit(solution)/shard_map/ppermute | solution.py:518
  31.1 25.7 %collective-permute-start.6 = (bf16[64,4096]{1,0:T(8,128)(2,1)S(1)}, bf16[64,4096]{1,0:T(8,128)(2,1)S(1)}, u32[]{:S(2)}, u32[]{:S(2)}) collective-permute-start(bf16[64,4096]{1,0:T(8,128)(2,1)S(1)} %add_near.1), channel_id=1, source_target_pairs={{0,2},{1,3},{2,0},{3,1},{4,6},{5,7},{6,4},{7,5},{8,10},{9,11},{10,... | collective-permute-start | bytes 1572872 | tf_op jit(solution)/shard_map/ppermute | solution.py:471
  33.4 24.8 %copy-start = (bf16[1,1,64,4096]{3,2,1,0:T(8,128)(2,1)S(1)}, bf16[1,1,64,4096]{3,2,1,0:T(8,128)(2,1)}, u32[]{:S(2)}) copy-start(bf16[1,1,64,4096]{3,2,1,0:T(8,128)(2,1)} %param.16) | copy-start | bytes 1572868
  33.4 4.7 %collective-permute-start.8 = (bf16[4,16,768]{2,1,0:T(8,128)(2,1)S(1)}, bf16[4,16,768]{2,1,0:T(8,128)(2,1)S(1)}, u32[]{:S(2)}, u32[]{:S(2)}) collective-permute-start(bf16[4,16,768]{2,1,0:T(8,128)(2,1)S(1)} %get-tuple-element.88), channel_id=1, source_target_pairs={{0,8},{4,12},{8,0},{12,4},{16,24},{20,28},{24,16},{28,20},{1,9},{5... | collective-permute-start | bytes 294920 | tf_op jit(solution)/shard_map/ppermute | solution.py:476
  35.0 6.0 %collective-permute-start.14 = (bf16[4,16,768]{2,1,0:T(8,128)(2,1)S(1)}, bf16[4,16,768]{2,1,0:T(8,128)(2,1)S(1)}, u32[]{:S(2)}, u32[]{:S(2)}) collective-permute-start(bf16[4,16,768]{2,1,0:T(8,128)(2,1)S(1)} %get-tuple-element.89), channel_id=1, source_target_pairs={{0,28},{4,24},{8,20},{12,16},{16,12},{20,8},{24,4},{28,0},{1,29},{... | collective-permute-start | bytes 294920 | tf_op jit(solution)/shard_map/ppermute | solution.py:476
  35.2 7.3 %collective-permute-start.13 = (bf16[4,16,768]{2,1,0:T(8,128)(2,1)S(1)}, bf16[4,16,768]{2,1,0:T(8,128)(2,1)S(1)}, u32[]{:S(2)}, u32[]{:S(2)}) collective-permute-start(bf16[4,16,768]{2,1,0:T(8,128)(2,1)S(1)} %get-tuple-element.90), channel_id=1, source_target_pairs={{0,20},{4,16},{8,28},{12,24},{16,4},{20,0},{24,12},{28,8},{1,21},{... | collective-permute-start | bytes 294920 | tf_op jit(solution)/shard_map/ppermute | solution.py:476
  36.7 6.7 %collective-permute-start.12 = (bf16[4,16,768]{2,1,0:T(8,128)(2,1)S(1)}, bf16[4,16,768]{2,1,0:T(8,128)(2,1)S(1)}, u32[]{:S(2)}, u32[]{:S(2)}) collective-permute-start(bf16[4,16,768]{2,1,0:T(8,128)(2,1)S(1)} %get-tuple-element.91), channel_id=1, source_target_pairs={{0,12},{4,8},{8,4},{12,0},{16,28},{20,24},{24,20},{28,16},{1,13},{... | collective-permute-start | bytes 294920 | tf_op jit(solution)/shard_map/ppermute | solution.py:476
  38.1 5.5 %collective-permute-start.11 = (bf16[4,16,768]{2,1,0:T(8,128)(2,1)S(1)}, bf16[4,16,768]{2,1,0:T(8,128)(2,1)S(1)}, u32[]{:S(2)}, u32[]{:S(2)}) collective-permute-start(bf16[4,16,768]{2,1,0:T(8,128)(2,1)S(1)} %get-tuple-element.92), channel_id=1, source_target_pairs={{0,4},{4,0},{8,12},{12,8},{16,20},{20,16},{24,28},{28,24},{1,5},{5... | collective-permute-start | bytes 294920 | tf_op jit(solution)/shard_map/ppermute | solution.py:476
  41.0 5.9 %collective-permute-start.10 = (bf16[4,16,768]{2,1,0:T(8,128)(2,1)S(1)}, bf16[4,16,768]{2,1,0:T(8,128)(2,1)S(1)}, u32[]{:S(2)}, u32[]{:S(2)}) collective-permute-start(bf16[4,16,768]{2,1,0:T(8,128)(2,1)S(1)} %get-tuple-element.93), channel_id=1, source_target_pairs={{0,24},{4,28},{8,16},{12,20},{16,8},{20,12},{24,0},{28,4},{1,25},{... | collective-permute-start | bytes 294920 | tf_op jit(solution)/shard_map/ppermute | solution.py:476
  42.5 6.4 %collective-permute-start.9 = (bf16[4,16,768]{2,1,0:T(8,128)(2,1)S(1)}, bf16[4,16,768]{2,1,0:T(8,128)(2,1)S(1)}, u32[]{:S(2)}, u32[]{:S(2)}) collective-permute-start(bf16[4,16,768]{2,1,0:T(8,128)(2,1)S(1)} %get-tuple-element.94), channel_id=1, source_target_pairs={{0,16},{4,20},{8,24},{12,28},{16,0},{20,4},{24,8},{28,12},{1,17},{... | collective-permute-start | bytes 294920 | tf_op jit(solution)/shard_map/ppermute | solution.py:476
  43.4 14.4 %collective-permute-start.15 = (bf16[32,3328]{1,0:T(8,128)(2,1)S(1)}, bf16[32,3328]{1,0:T(8,128)(2,1)S(1)}, u32[]{:S(2)}, u32[]{:S(2)}) collective-permute-start(bf16[32,3328]{1,0:T(8,128)(2,1)S(1)} %get-tuple-element.68.picked_ref), channel_id=1, source_target_pairs={{0,4},{4,0},{1,5},{5,1},{2,6},{6,2},{3,7},{7,3},{8,12},{12,8},{9,1... | collective-permute-start | bytes 638984 | tf_op jit(solution)/shard_map/ppermute | solution.py:471
  43.6 14.6 %collective-permute-start.7 = (bf16[64,4096]{1,0:T(8,128)(2,1)S(1)}, bf16[64,4096]{1,0:T(8,128)(2,1)S(1)}, u32[]{:S(2)}, u32[]{:S(2)}) collective-permute-start(bf16[64,4096]{1,0:T(8,128)(2,1)S(1)} %get-tuple-element.64), channel_id=1, source_target_pairs={{0,1},{3,2},{4,5},{7,6},{8,9},{11,10},{12,13},{15,14},{16,17},{19,... | collective-permute-start | bytes 1572872 | tf_op jit(solution)/shard_map/ppermute | solution.py:527
  56.9 18.1 %copy-start.1 = (bf16[8,3072]{1,0:T(8,128)(2,1)S(1)}, bf16[8,3072]{1,0:T(8,128)(2,1)}, u32[]{:S(2)}) copy-start(bf16[8,3072]{1,0:T(8,128)(2,1)} %router_ref.3) | copy-start | bytes 147460
  59.7 6.4 %collective-permute-start.16 = (bf16[2,24,896]{2,1,0:T(8,128)(2,1)S(1)}, bf16[2,24,896]{2,1,0:T(8,128)(2,1)S(1)}, u32[]{:S(2)}, u32[]{:S(2)}) collective-permute-start(bf16[2,24,896]{2,1,0:T(8,128)(2,1)S(1)} %slice.168), channel_id=1, source_target_pairs={{0,2},{1,3},{2,0},{3,1},{4,6},{5,7},{6,4},{7,5},{8,10},{9,11},{10,... | collective-permute-start | bytes 258056 | tf_op jit(solution)/shard_map/ppermute | solution.py:471
  66.1 4.1 %collective-permute-start.17 = (bf16[24,896]{1,0:T(8,128)(2,1)S(1)}, bf16[24,896]{1,0:T(8,128)(2,1)S(1)}, u32[]{:S(2)}, u32[]{:S(2)}) collective-permute-start(bf16[24,896]{1,0:T(8,128)(2,1)S(1)} %fusion), channel_id=1, source_target_pairs={{0,1},{1,0},{2,3},{3,2},{4,5},{5,4},{6,7},{7,6},{8,9},{9,8},{10,11... | collective-permute-start | bytes 129032 | tf_op jit(solution)/shard_map/ppermute | solution.py:471
  70.3 6.0 %collective-permute-start.20 = (bf16[24,896]{1,0:T(8,128)(2,1)S(1)}, bf16[24,896]{1,0:T(8,128)(2,1)S(1)}, u32[]{:S(2)}, u32[]{:S(2)}) collective-permute-start(bf16[24,896]{1,0:T(8,128)(2,1)S(1)} %pad_maximum_fusion.1), channel_id=1, source_target_pairs={{0,24},{8,16},{16,8},{24,0},{1,25},{9,17},{17,9},{25,1},{2,26},{10... | collective-permute-start | bytes 129032 | tf_op jit(solution)/shard_map/ppermute | solution.py:471
  72.3 4.0 %collective-permute-start.19 = (bf16[24,896]{1,0:T(8,128)(2,1)S(1)}, bf16[24,896]{1,0:T(8,128)(2,1)S(1)}, u32[]{:S(2)}, u32[]{:S(2)}) collective-permute-start(bf16[24,896]{1,0:T(8,128)(2,1)S(1)} %pad_maximum_fusion.1), channel_id=1, source_target_pairs={{0,16},{8,24},{16,0},{24,8},{1,17},{9,25},{17,1},{25,9},{2,18},{10... | collective-permute-start | bytes 129032 | tf_op jit(solution)/shard_map/ppermute | solution.py:471
  73.3 4.0 %collective-permute-start.18 = (bf16[24,896]{1,0:T(8,128)(2,1)S(1)}, bf16[24,896]{1,0:T(8,128)(2,1)S(1)}, u32[]{:S(2)}, u32[]{:S(2)}) collective-permute-start(bf16[24,896]{1,0:T(8,128)(2,1)S(1)} %pad_maximum_fusion.1), channel_id=1, source_target_pairs={{0,8},{8,0},{16,24},{24,16},{1,9},{9,1},{17,25},{25,17},{2,10},{10... | collective-permute-start | bytes 129032 | tf_op jit(solution)/shard_map/ppermute | solution.py:471
  73.8 1.2 %collective-permute-start.21 = (f32[32,128]{1,0:T(8,128)S(1)}, f32[32,128]{1,0:T(8,128)S(1)}, u32[]{:S(2)}, u32[]{:S(2)}) collective-permute-start(f32[32,128]{1,0:T(8,128)S(1)} %get-tuple-element.78), channel_id=1, source_target_pairs={{0,4},{4,0},{1,5},{5,1},{2,6},{6,2},{3,7},{7,3},{8,12},{12,8},{9,1... | collective-permute-start | bytes 49160 | tf_op jit(solution)/shard_map/ppermute | solution.py:471
  77.4 1.4 %collective-permute-start.22 = (bf16[72,896]{1,0:T(8,128)(2,1)S(1)}, bf16[72,896]{1,0:T(8,128)(2,1)S(1)}, u32[]{:S(2)}, u32[]{:S(2)}) collective-permute-start(bf16[72,896]{1,0:T(8,128)(2,1)S(1)} %get-tuple-element.99), channel_id=1, source_target_pairs={{0,4},{4,0},{1,5},{5,1},{2,6},{6,2},{3,7},{7,3},{8,12},{12,8},{9,1... | collective-permute-start | bytes 387080 | tf_op jit(solution)/shard_map/ppermute | solution.py:471

commit v6 on v5

--- a/solution.py
+++ b/solution.py
@@ -11,6 +11,7 @@
 LANES = 128
 F32 = jnp.float32
 BF16 = jnp.bfloat16
+BLOCKS = (0, 2, 1, 3)
 SMEM = pl.BlockSpec(memory_space=pltpu.SMEM)
 VMEM = pl.BlockSpec(memory_space=pltpu.VMEM)
 HBM = pl.BlockSpec(memory_space=pltpu.HBM)
@@ -257,14 +258,14 @@
     low_grad = (ADAPTER_SCALE * contract(grad_ref[...], up_ref[...], 1, 1)).astype(BF16)
     mixed_ref[...] = ADAPTER_SCALE * contract(up_ref[...], router_ref[...], 1, 1)
     slots = slots_ref[...].astype(BF16)
-    for k in range(shards):
+    for position, k in enumerate(BLOCKS):
         grad = feature_block(grad_ref, place, k, width)
         context = feature_block(context_ref, place, k, width)
         up = ADAPTER_SCALE * contract(low_in, grad, 0, 0)
         down = contract(low_grad, context, 0, 0)
         for g in range(half):
-            early_ref[g ^ place[1], k] = up[g * rows : (g + 1) * rows]
-            early_ref[(g + half) ^ place[1], k] = down[g * rows : (g + 1) * rows]
+            early_ref[g ^ place[1], position] = up[g * rows : (g + 1) * rows]
+            early_ref[(g + half) ^ place[1], position] = down[g * rows : (g + 1) * rows]
         picked_ref[:, k * width : (k + 1) * width] = jnp.dot(
             slots, context, preferred_element_type=F32
         ).astype(BF16)
@@ -335,9 +336,9 @@
         )
 
     low = late(slice(features, features + LANES))
-    for k in range(shards):
-        late_ref[k, :, :width] = late(slice(k * width, (k + 1) * width))
-        late_ref[k, :, width:] = low
+    for position, k in enumerate(BLOCKS):
+        late_ref[position, :, :width] = late(slice(k * width, (k + 1) * width))
+        late_ref[position, :, width:] = low
 
 
 def hidden_kernel(experts, place, product_ref, picked_ref, other_ref, grad_hbm, grad_ref, sems):
@@ -539,11 +540,11 @@
     )
     early = jnp.pad(early, ((0, 0), (0, 0), (0, LANES)))
     late = jnp.concatenate([late, early], 1)
-    late = late[:2] + swap(late[2:].astype(BF16), "shard", 4, 2).astype(F32)
+    late = late[:2] + swap(late[2:].astype(BF16), "shard", 4, 1).astype(F32)
     hidden_grad = hidden_gradient(place, product, picked, other_picked, experts, 4)
     late, hidden_grad = lax.optimization_barrier((late, hidden_grad))
     prob_got = swap(prob_other, "expert", 2, 1)
-    late = late[0] + swap(late[1].astype(BF16), "shard", 4, 1).astype(F32)
+    late = late[0] + swap(late[1].astype(BF16), "shard", 4, 2).astype(F32)
     late, early = late[:experts], late[experts:].astype(BF16)
     mine = jnp.concatenate([late.astype(BF16), early], 0)
     got = [swap(mine, "dp", 4, k) for k in range(1, 4)]

time: 80.5 us -> 80 us (level)
  waiting for transfers between devices: 32.8 us -> 31.9 us
    ppermute x14, waiting for transfers between devices: 27.2 us -> 26.3 us  [swap(): return lax.ppermute(value, axis, xor_pairs(count, bits))]
where the time goes in v6:
time: 80 us; the launch traced here: 79.8 us
  waiting for transfers between devices  31.9 us (40%)
  starting transfers between devices  27.8 us (35%)
  Pallas kernels  18.7 us (23%)
  between operations  0.91 us (1%)
    ppermute x14, waiting for transfers between devices, swap(): return lax.ppermute(value, axis, xor_pairs(count, bits))  26.3 us
    ppermute x14, starting transfers between devices, swap(): return lax.ppermute(value, axis, xor_pairs(count, bits))  17 us
    ppermute x7, starting transfers between devices, swap_group(): return lax.ppermute(value, ('dp', 'expert'), pairs)  6.84 us
    ppermute x7, waiting for transfers between devices, swap_group(): return lax.ppermute(value, ('dp', 'expert'), pairs)  5.11 us
    pallas_call x1, Pallas kernels, adapter_early(): pl.pallas_call(adapter_kernel, out_shape=(jax.ShapeDtypeStruct((groups, s...  3.47 us
    ppermute x1, starting transfers between devices, direct_device(): outer = lax.ppermute(last, 'shard', [(0, 1), (3, 2)])  3.24 us
    pallas_call x2, Pallas kernels, products(): pl.pallas_call(functools.partial(product_kernel, len(before) // 4), out_s...  3.07 us
    pallas_call x1, Pallas kernels, dequantize(): pl.pallas_call(weight_kernel, out_shape=pltpu.VMEM(codes.shape, BF16), in...  3.05 us
  transfers between devices with their start and end apart: 23, of which 13 were waited for; matrix products, arithmetic and copies ran while one was open for 0% of the time, Pallas kernels for 15%

profile of v6, /device:TPU:0, one launch (start us, length us, event | category | flops | bytes accessed | tf_op | source)
XLA Modules:
  0.0 79.8 jit_solution(8241603714346107563)
XLA Ops:
  0.6 0.1 pad_add_fusion.place
  0.7 2.0 %route.1 = (bf16[4,32,768]{2,1,0:T(8,128)(2,1)S(1)}, f32[32,128]{1,0:T(8,128)S(1)}, f32[16,128]{1,0:T(8,128)S(1)}) custom-call(s32[4]{0:T(128)S(1)} %pad_add_fusion.place, f32[8,128]{1,0:T(8,128)} %bitcast.44, s32[2,128]{1,0:T(2,128)} %bitcast.45, bf16[128,3072]{1,0:T(8,128)(2,1)} %grad_hbm.3), custom_call_target="tpu_custom_call" | custom-call | flops 25165824 | bytes 786432 | tf_op jit(solution)/shard_map/route/pallas_call | solution.py:97
  2.7 5.1 %collective-permute-start.2 = (bf16[32,768]{1,0:T(8,128)(2,1)S(1)}, bf16[32,768]{1,0:T(8,128)(2,1)S(1)}, u32[]{:S(2)}, u32[]{:S(2)}) collective-permute-start(bf16[32,768]{1,0:T(8,128)(2,1)S(1)} %get-tuple-element.96), channel_id=1, source_target_pairs={{0,3},{1,2},{2,1},{3,0},{4,7},{5,6},{6,5},{7,4},{8,11},{9,10},{10,... | collective-permute-start | bytes 147464 | tf_op jit(solution)/shard_map/ppermute | solution.py:472
  7.9 0.0 collective-permute-start.1
  7.9 0.6 collective-permute-start
  8.5 3.1 %dequantize.1.weight_ref = bf16[768,4096]{1,0:T(8,128)(2,1)S(1)} custom-call(bf16[768,4096]{1,0:T(8,128)(2,1)} %codes_hbm.1, bf16[12,4096]{1,0:T(8,128)(2,1)} %scales_hbm.1), custom_call_target="tpu_custom_call" | custom-call | flops 3145728 | bytes 12582912 | tf_op jit(solution)/shard_map/dequantize/pallas_call | solution.py:214
  11.6 0.0 collective-permute-done.2
  11.6 1.3 %collective-permute-done.1 = bf16[32,768]{1,0:T(8,128)(2,1)S(1)} collective-permute-done((bf16[32,768]{1,0:T(8,128)(2,1)S(1)}, bf16[32,768]{1,0:T(8,128)(2,1)S(1)}, u32[]{:S(2)}, u32[]{:S(2)}) %collective-permute-start.1) | collective-permute-done | bytes 49184 | tf_op jit(solution)/shard_map/ppermute | solution.py:472
  12.8 0.0 collective-permute-done
  12.9 0.1 collective-permute-start.3
  13.0 1.5 %products.2 = (bf16[64,4096]{1,0:T(8,128)(2,1)S(1)}, bf16[64,4096]{1,0:T(8,128)(2,1)S(1)}, bf16[64,4096]{1,0:T(8,128)(2,1)S(1)}, f32[64,4096]{1,0:T(8,128)S(1)}) custom-call(s32[4]{0:T(128)S(1)} %pad_add_fusion.place, bf16[4,32,768]{2,1,0:T(8,128)(2,1)S(1)} %pad_maximum_fusion.rows_ref, bf16[768,4096]{1,0:T(8,128)(2,1)S(1)} %dequantize.1.weight_ref), custom_call_target="tpu_custom_call" | custom-call | flops 805306368 | bytes 6291456 | tf_op jit(solution)/shard_map/products/pallas_call | solution.py:138
  14.5 0.0 collective-permute-done.3.rows_ref
  14.5 1.5 %products.3 = (bf16[64,4096]{1,0:T(8,128)(2,1)S(1)}, bf16[64,4096]{1,0:T(8,128)(2,1)S(1)}, bf16[64,4096]{1,0:T(8,128)(2,1)S(1)}, f32[64,4096]{1,0:T(8,128)S(1)}) custom-call(s32[4]{0:T(128)S(1)} %pad_add_fusion.place, ...), custom_call_target="tpu_custom_call", output_to_operand_aliasing={{0}: (3, {}), {1}: (4, {}), {2}: (5, {}), {3}: (6, {})} | custom-call | flops 805306368 | bytes 6291456 | tf_op jit(solution)/shard_map/products/pallas_call | solution.py:138
  16.1 0.7 collective-permute-start.4
  16.8 0.7 collective-permute-start.5
  17.4 3.5 %adapter_early.1 = (f32[8,4,16,768]{3,2,1,0:T(8,128)S(1)}, bf16[32,3328]{1,0:T(8,128)(2,1)S(1)}, f32[64,8]{1,0:T(8,128)S(1)}) custom-call(s32[4]{0:T(128)S(1)} %pad_add_fusion.place, bf16[128,3072]{1,0:T(8,128)(2,1)} %grad_hbm.3, bf16[128,3072]{1,0:T(8,128)(2,1)} %context_hbm.1, bf16[64,3072]{1,0:T(8,128)(2,1)} %down_hbm.1, bf16[64,3072]{1,0:T(8,128)(2,1)} %up_hbm.1, ...), custom_call_target="tpu_custom_call" | custom-call | tf_op jit(solution)/shard_map/adapter_early/pallas_call | solution.py:284
  20.9 9.5 %collective-permute-done.4.near_ref = bf16[64,4096]{1,0:T(8,128)(2,1)S(1)} collective-permute-done((bf16[64,4096]{1,0:T(8,128)(2,1)S(1)}, bf16[64,4096]{1,0:T(8,128)(2,1)S(1)}, u32[]{:S(2)}, u32[]{:S(2)}) %collective-permute-start.4) | collective-permute-done | bytes 524320 | tf_op jit(solution)/shard_map/ppermute | solution.py:472
  30.4 0.7 add_near.1
  31.1 2.1 %collective-permute-start.6 = (bf16[64,4096]{1,0:T(8,128)(2,1)S(1)}, bf16[64,4096]{1,0:T(8,128)(2,1)S(1)}, u32[]{:S(2)}, u32[]{:S(2)}) collective-permute-start(bf16[64,4096]{1,0:T(8,128)(2,1)S(1)} %add_near.1), channel_id=1, source_target_pairs={{0,2},{1,3},{2,0},{3,1},{4,6},{5,7},{6,4},{7,5},{8,10},{9,11},{10,... | collective-permute-start | bytes 1572872 | tf_op jit(solution)/shard_map/ppermute | solution.py:472
  33.2 0.1 convert_element_type.57
  33.3 0.1 slice_bitcast_fusion.6
  33.4 0.0 copy-start
  33.4 1.6 %collective-permute-start.8 = (bf16[4,16,768]{2,1,0:T(8,128)(2,1)S(1)}, bf16[4,16,768]{2,1,0:T(8,128)(2,1)S(1)}, u32[]{:S(2)}, u32[]{:S(2)}) collective-permute-start(bf16[4,16,768]{2,1,0:T(8,128)(2,1)S(1)} %get-tuple-element.88), channel_id=1, source_target_pairs={{0,8},{4,12},{8,0},{12,4},{16,24},{20,28},{24,16},{28,20},{1,9},{5... | collective-permute-start | bytes 294920 | tf_op jit(solution)/shard_map/ppermute | solution.py:477
  35.0 0.3 collective-permute-start.14
  35.2 1.5 %collective-permute-start.13 = (bf16[4,16,768]{2,1,0:T(8,128)(2,1)S(1)}, bf16[4,16,768]{2,1,0:T(8,128)(2,1)S(1)}, u32[]{:S(2)}, u32[]{:S(2)}) collective-permute-start(bf16[4,16,768]{2,1,0:T(8,128)(2,1)S(1)} %get-tuple-element.90), channel_id=1, source_target_pairs={{0,20},{4,16},{8,28},{12,24},{16,4},{20,0},{24,12},{28,8},{1,21},{... | collective-permute-start | bytes 294920 | tf_op jit(solution)/shard_map/ppermute | solution.py:477
  36.7 0.0 collective-permute-done.5.middle_ref
  36.7 1.0 %collective-permute-start.12 = (bf16[4,16,768]{2,1,0:T(8,128)(2,1)S(1)}, bf16[4,16,768]{2,1,0:T(8,128)(2,1)S(1)}, u32[]{:S(2)}, u32[]{:S(2)}) collective-permute-start(bf16[4,16,768]{2,1,0:T(8,128)(2,1)S(1)} %get-tuple-element.91), channel_id=1, source_target_pairs={{0,12},{4,8},{8,4},{12,0},{16,28},{20,24},{24,20},{28,16},{1,13},{... | collective-permute-start | bytes 294920 | tf_op jit(solution)/shard_map/ppermute | solution.py:477
  37.7 0.4 collective-permute-done.8
  38.1 0.2 collective-permute-start.11
  38.3 2.7 %collective-permute-done.14 = bf16[4,16,768]{2,1,0:T(8,128)(2,1)S(1)} collective-permute-done((bf16[4,16,768]{2,1,0:T(8,128)(2,1)S(1)}, bf16[4,16,768]{2,1,0:T(8,128)(2,1)S(1)}, u32[]{:S(2)}, u32[]{:S(2)}) %collective-permute-start.14) | collective-permute-done | bytes 98336 | tf_op jit(solution)/shard_map/ppermute | solution.py:477
  41.0 1.5 %collective-permute-start.10 = (bf16[4,16,768]{2,1,0:T(8,128)(2,1)S(1)}, bf16[4,16,768]{2,1,0:T(8,128)(2,1)S(1)}, u32[]{:S(2)}, u32[]{:S(2)}) collective-permute-start(bf16[4,16,768]{2,1,0:T(8,128)(2,1)S(1)} %get-tuple-element.93), channel_id=1, source_target_pairs={{0,24},{4,28},{8,16},{12,20},{16,8},{20,12},{24,0},{28,4},{1,25},{... | collective-permute-start | bytes 294920 | tf_op jit(solution)/shard_map/ppermute | solution.py:477
  42.5 0.0 collective-permute-done.13
  42.5 0.8 %collective-permute-start.9 = (bf16[4,16,768]{2,1,0:T(8,128)(2,1)S(1)}, bf16[4,16,768]{2,1,0:T(8,128)(2,1)S(1)}, u32[]{:S(2)}, u32[]{:S(2)}) collective-permute-start(bf16[4,16,768]{2,1,0:T(8,128)(2,1)S(1)} %get-tuple-element.94), channel_id=1, source_target_pairs={{0,16},{4,20},{8,24},{12,28},{16,0},{20,4},{24,8},{28,12},{1,17},{... | collective-permute-start | bytes 294920 | tf_op jit(solution)/shard_map/ppermute | solution.py:477
  43.4 0.0 collective-permute-done.12
  43.4 0.3 collective-permute-start.15
  43.6 0.0 collective-permute-done.11
  43.6 3.2 %collective-permute-start.7 = (bf16[64,4096]{1,0:T(8,128)(2,1)S(1)}, bf16[64,4096]{1,0:T(8,128)(2,1)S(1)}, u32[]{:S(2)}, u32[]{:S(2)}) collective-permute-start(bf16[64,4096]{1,0:T(8,128)(2,1)S(1)} %get-tuple-element.64), channel_id=1, source_target_pairs={{0,1},{3,2},{4,5},{7,6},{8,9},{11,10},{12,13},{15,14},{16,17},{19,... | collective-permute-start | bytes 1572872 | tf_op jit(solution)/shard_map/ppermute | solution.py:528
  46.9 0.0 collective-permute-done.10
  46.9 2.0 %collective-permute-done.9 = bf16[4,16,768]{2,1,0:T(8,128)(2,1)S(1)} collective-permute-done((bf16[4,16,768]{2,1,0:T(8,128)(2,1)S(1)}, bf16[4,16,768]{2,1,0:T(8,128)(2,1)S(1)}, u32[]{:S(2)}, u32[]{:S(2)}) %collective-permute-start.9) | collective-permute-done | bytes 98336 | tf_op jit(solution)/shard_map/ppermute | solution.py:477
  48.9 0.1 bitcast_add_fusion
  49.0 7.9 %collective-permute-done.6.far_ref = bf16[64,4096]{1,0:T(8,128)(2,1)S(1)} collective-permute-done((bf16[64,4096]{1,0:T(8,128)(2,1)S(1)}, bf16[64,4096]{1,0:T(8,128)(2,1)S(1)}, u32[]{:S(2)}, u32[]{:S(2)}) %collective-permute-start.6) | collective-permute-done | bytes 524320 | tf_op jit(solution)/shard_map/ppermute | solution.py:472
  56.9 0.8 %add_far.1.partial_ref = f32[64,4096]{1,0:T(8,128)S(1)} custom-call(s32[4]{0:T(128)S(1)} %pad_add_fusion.place, f32[64,4096]{1,0:T(8,128)S(1)} %get-tuple-element.52.own_ref, bf16[64,4096]{1,0:T(8,128)(2,1)S(1)} %collective-permute-done.4.near_ref, bf16[64,4096]{1,0:T(8,128)(2,1)S(1)} %collective-permute-done.5.middle_ref, ...), custom_call_target="tpu_custom_call" | custom-call | flops 3000000000 | bytes 3670016 | tf_op jit(solution)/shard_map/add_far/pallas_call | solution.py:179
  57.7 0.0 collective-permute-done.15.other_ref
  57.7 0.5 collective-permute-done.7.outer_ref
  58.2 0.0 copy-done
  58.2 1.4 %finish.1 = (f32[64,4096]{1,0:T(8,128)S(1)}, f32[32,128]{1,0:T(8,128)S(1)}, f32[32,128]{1,0:T(8,128)S(1)}, f32[4,8,896]{2,1,0:T(8,128)S(1)}) custom-call(s32[4]{0:T(128)S(1)} %pad_add_fusion.place, f32[64,4096]{1,0:T(8,128)S(1)} %add_far.1.partial_ref, bf16[64,4096]{1,0:T(8,128)(2,1)S(1)} %collective-permute-done.7.outer_ref, bf16[64,4096]{1,0:T(8,128)(2,1)S(1)} %bitcast.38, ...), custom_call_target="tpu_custom_call" | custom-call | flops 2097152 | bytes 2621440 | tf_op jit(solution)/shard_map/finish/pallas_call | solution.py:381
  59.7 2.5 %collective-permute-start.16 = (bf16[2,24,896]{2,1,0:T(8,128)(2,1)S(1)}, bf16[2,24,896]{2,1,0:T(8,128)(2,1)S(1)}, u32[]{:S(2)}, u32[]{:S(2)}) collective-permute-start(bf16[2,24,896]{2,1,0:T(8,128)(2,1)S(1)} %slice.168), channel_id=1, source_target_pairs={{0,1},{1,0},{2,3},{3,2},{4,5},{5,4},{6,7},{7,6},{8,9},{9,8},{10,11... | collective-permute-start | bytes 258056 | tf_op jit(solution)/shard_map/ppermute | solution.py:472
  62.2 1.4 %hidden_gradient.1 = bf16[64,4096]{1,0:T(8,128)(2,1)} custom-call(s32[4]{0:T(128)S(1)} %pad_add_fusion.place, f32[64,4096]{1,0:T(8,128)S(1)} %get-tuple-element.74.product_ref, bf16[32,3328]{1,0:T(8,128)(2,1)S(1)} %get-tuple-element.68.picked_ref, bf16[32,3328]{1,0:T(8,128)(2,1)S(1)} %collective-permute-done.15.other_ref), custom_call_target="tpu_custom_call" | custom-call | tf_op jit(solution)/shard_map/hidden_gradient/pallas_call | solution.py:365
  63.7 1.0 %collective-permute-done.16 = bf16[2,24,896]{2,1,0:T(8,128)(2,1)S(1)} collective-permute-done((bf16[2,24,896]{2,1,0:T(8,128)(2,1)S(1)}, bf16[2,24,896]{2,1,0:T(8,128)(2,1)S(1)}, u32[]{:S(2)}, u32[]{:S(2)}) %collective-permute-start.16) | collective-permute-done | bytes 86048 | tf_op jit(solution)/shard_map/ppermute | solution.py:472
  64.7 2.0 %collective-permute-start.17 = (bf16[24,896]{1,0:T(8,128)(2,1)S(1)}, bf16[24,896]{1,0:T(8,128)(2,1)S(1)}, u32[]{:S(2)}, u32[]{:S(2)}) collective-permute-start(bf16[24,896]{1,0:T(8,128)(2,1)S(1)} %fusion), channel_id=1, source_target_pairs={{0,2},{1,3},{2,0},{3,1},{4,6},{5,7},{6,4},{7,5},{8,10},{9,11},{10,... | collective-permute-start | bytes 129032 | tf_op jit(solution)/shard_map/ppermute | solution.py:472
  66.7 3.0 %collective-permute-done.17 = bf16[24,896]{1,0:T(8,128)(2,1)S(1)} collective-permute-done((bf16[24,896]{1,0:T(8,128)(2,1)S(1)}, bf16[24,896]{1,0:T(8,128)(2,1)S(1)}, u32[]{:S(2)}, u32[]{:S(2)}) %collective-permute-start.17) | collective-permute-done | bytes 43040 | tf_op jit(solution)/shard_map/ppermute | solution.py:472
  69.8 2.1 %collective-permute-start.20 = (bf16[24,896]{1,0:T(8,128)(2,1)S(1)}, bf16[24,896]{1,0:T(8,128)(2,1)S(1)}, u32[]{:S(2)}, u32[]{:S(2)}) collective-permute-start(bf16[24,896]{1,0:T(8,128)(2,1)S(1)} %pad_maximum_fusion.1), channel_id=1, source_target_pairs={{0,24},{8,16},{16,8},{24,0},{1,25},{9,17},{17,9},{25,1},{2,26},{10... | collective-permute-start | bytes 129032 | tf_op jit(solution)/shard_map/ppermute | solution.py:472
  71.9 0.9 %collective-permute-start.19 = (bf16[24,896]{1,0:T(8,128)(2,1)S(1)}, bf16[24,896]{1,0:T(8,128)(2,1)S(1)}, u32[]{:S(2)}, u32[]{:S(2)}) collective-permute-start(bf16[24,896]{1,0:T(8,128)(2,1)S(1)} %pad_maximum_fusion.1), channel_id=1, source_target_pairs={{0,16},{8,24},{16,0},{24,8},{1,17},{9,25},{17,1},{25,9},{2,18},{10... | collective-permute-start | bytes 129032 | tf_op jit(solution)/shard_map/ppermute | solution.py:472
  72.8 0.5 collective-permute-start.18
  73.3 0.0 collective-permute-start.21
  73.3 1.2 %collective-permute-done.21.prob_got_ref = f32[32,128]{1,0:T(8,128)S(1)} collective-permute-done((f32[32,128]{1,0:T(8,128)S(1)}, f32[32,128]{1,0:T(8,128)S(1)}, u32[]{:S(2)}, u32[]{:S(2)}) %collective-permute-start.21) | collective-permute-done | bytes 16416 | tf_op jit(solution)/shard_map/ppermute | solution.py:472
  74.5 0.0 copy-done.1
  74.5 1.2 %token_gradient.1 = bf16[128,3072]{1,0:T(8,128)(2,1)} custom-call(f32[32,128]{1,0:T(8,128)S(1)} %get-tuple-element.77.prob_ref, f32[32,128]{1,0:T(8,128)S(1)} %collective-permute-done.21.prob_got_ref, f32[32,128]{1,0:T(8,128)S(1)} %get-tuple-element.57.slots_ref, f32[16,128]{1,0:T(8,128)S(1)} %get-tuple-element.58.info_ref, bf16[8,3072]{1,0:T(8,128)(2,1)S(1)} %copy-done.1), custom_call_target="tpu_custom_call" | custom-call | flops 6291456 | bytes 786432 | tf_op jit(solution)/shard_map/token_gradient/pallas_call | solution.py:418
  75.8 0.0 collective-permute-done.20
  75.8 0.1 collective-permute-done.19
  75.9 0.9 %collective-permute-done.18 = bf16[24,896]{1,0:T(8,128)(2,1)S(1)} collective-permute-done((bf16[24,896]{1,0:T(8,128)(2,1)S(1)}, bf16[24,896]{1,0:T(8,128)(2,1)S(1)}, u32[]{:S(2)}, u32[]{:S(2)}) %collective-permute-start.18) | collective-permute-done | bytes 43040 | tf_op jit(solution)/shard_map/ppermute | solution.py:472
  76.9 0.1 collective-permute-start.22
  77.0 1.3 %collective-permute-done.22 = bf16[72,896]{1,0:T(8,128)(2,1)S(1)} collective-permute-done((bf16[72,896]{1,0:T(8,128)(2,1)S(1)}, bf16[72,896]{1,0:T(8,128)(2,1)S(1)}, u32[]{:S(2)}, u32[]{:S(2)}) %collective-permute-start.22) | collective-permute-done | bytes 129056 | tf_op jit(solution)/shard_map/ppermute | solution.py:472
  78.4 1.5 %adapter_late.1 = (f32[64,768]{1,0:T(8,128)}, f32[64,768]{1,0:T(8,128)}) custom-call(s32[4]{0:T(128)S(1)} %pad_add_fusion.place, bf16[8,16,896]{2,1,0:T(8,128)(2,1)S(1)} %bitcast.39, f32[8,896]{1,0:T(8,128)S(1)} %convert_add_fusion.late_ref, f32[64,8]{1,0:T(8,128)S(1)} %get-tuple-element.83.mixed_ref, bf16[8,3072]{1,0:T(8,128)(2,1)S(1)} %copy-done.1), custom_call_target="tpu_custom_call" | custom-call | flops 7340032 | bytes 917504 | tf_op jit(solution)/shard_map/adapter_late/pallas_call | solution.py:459
  (18 shorter events, 0.2 us)
Async XLA Ops:
  2.7 8.8 %collective-permute-start.2 = (bf16[32,768]{1,0:T(8,128)(2,1)S(1)}, bf16[32,768]{1,0:T(8,128)(2,1)S(1)}, u32[]{:S(2)}, u32[]{:S(2)}) collective-permute-start(bf16[32,768]{1,0:T(8,128)(2,1)S(1)} %get-tuple-element.96), channel_id=1, source_target_pairs={{0,3},{1,2},{2,1},{3,0},{4,7},{5,6},{6,5},{7,4},{8,11},{9,10},{10,... | collective-permute-start | bytes 147464 | tf_op jit(solution)/shard_map/ppermute | solution.py:472
  7.9 5.0 %collective-permute-start.1 = (bf16[32,768]{1,0:T(8,128)(2,1)S(1)}, bf16[32,768]{1,0:T(8,128)(2,1)S(1)}, u32[]{:S(2)}, u32[]{:S(2)}) collective-permute-start(bf16[32,768]{1,0:T(8,128)(2,1)S(1)} %get-tuple-element.97), channel_id=1, source_target_pairs={{0,2},{1,3},{2,0},{3,1},{4,6},{5,7},{6,4},{7,5},{8,10},{9,11},{10,... | collective-permute-start | bytes 147464 | tf_op jit(solution)/shard_map/ppermute | solution.py:472
  7.9 5.0 %collective-permute-start = (bf16[32,768]{1,0:T(8,128)(2,1)S(1)}, bf16[32,768]{1,0:T(8,128)(2,1)S(1)}, u32[]{:S(2)}, u32[]{:S(2)}) collective-permute-start(bf16[32,768]{1,0:T(8,128)(2,1)S(1)} %get-tuple-element.98), channel_id=1, source_target_pairs={{0,1},{1,0},{2,3},{3,2},{4,5},{5,4},{6,7},{7,6},{8,9},{9,8},{10,11... | collective-permute-start | bytes 147464 | tf_op jit(solution)/shard_map/ppermute | solution.py:472
  12.9 1.6 %collective-permute-start.3 = (bf16[4,32,768]{2,1,0:T(8,128)(2,1)S(1)}, bf16[4,32,768]{2,1,0:T(8,128)(2,1)S(1)}, u32[]{:S(2)}, u32[]{:S(2)}) collective-permute-start(bf16[4,32,768]{2,1,0:T(8,128)(2,1)S(1)} %pad_maximum_fusion.rows_ref), channel_id=1, source_target_pairs={{0,4},{4,0},{1,5},{5,1},{2,6},{6,2},{3,7},{7,3},{8,12},{12,8},{9,1... | collective-permute-start | bytes 589832 | tf_op jit(solution)/shard_map/ppermute | solution.py:472
  16.1 14.4 %collective-permute-start.4 = (bf16[64,4096]{1,0:T(8,128)(2,1)S(1)}, bf16[64,4096]{1,0:T(8,128)(2,1)S(1)}, u32[]{:S(2)}, u32[]{:S(2)}) collective-permute-start(bf16[64,4096]{1,0:T(8,128)(2,1)S(1)} %get-tuple-element.54), channel_id=1, source_target_pairs={{0,1},{1,0},{2,3},{3,2},{4,5},{5,4},{6,7},{7,6},{8,9},{9,8},{10,11... | collective-permute-start | bytes 1572872 | tf_op jit(solution)/shard_map/ppermute | solution.py:472
  16.8 19.9 %collective-permute-start.5 = (bf16[64,4096]{1,0:T(8,128)(2,1)S(1)}, bf16[64,4096]{1,0:T(8,128)(2,1)S(1)}, u32[]{:S(2)}, u32[]{:S(2)}) collective-permute-start(bf16[64,4096]{1,0:T(8,128)(2,1)S(1)} %get-tuple-element.64), channel_id=1, source_target_pairs={{1,2},{2,1},{5,6},{6,5},{9,10},{10,9},{13,14},{14,13},{17,18},{18,... | collective-permute-start | bytes 1572872 | tf_op jit(solution)/shard_map/ppermute | solution.py:519
  31.1 25.7 %collective-permute-start.6 = (bf16[64,4096]{1,0:T(8,128)(2,1)S(1)}, bf16[64,4096]{1,0:T(8,128)(2,1)S(1)}, u32[]{:S(2)}, u32[]{:S(2)}) collective-permute-start(bf16[64,4096]{1,0:T(8,128)(2,1)S(1)} %add_near.1), channel_id=1, source_target_pairs={{0,2},{1,3},{2,0},{3,1},{4,6},{5,7},{6,4},{7,5},{8,10},{9,11},{10,... | collective-permute-start | bytes 1572872 | tf_op jit(solution)/shard_map/ppermute | solution.py:472
  33.4 24.8 %copy-start = (bf16[1,1,64,4096]{3,2,1,0:T(8,128)(2,1)S(1)}, bf16[1,1,64,4096]{3,2,1,0:T(8,128)(2,1)}, u32[]{:S(2)}) copy-start(bf16[1,1,64,4096]{3,2,1,0:T(8,128)(2,1)} %param.16) | copy-start | bytes 1572868
  33.4 4.7 %collective-permute-start.8 = (bf16[4,16,768]{2,1,0:T(8,128)(2,1)S(1)}, bf16[4,16,768]{2,1,0:T(8,128)(2,1)S(1)}, u32[]{:S(2)}, u32[]{:S(2)}) collective-permute-start(bf16[4,16,768]{2,1,0:T(8,128)(2,1)S(1)} %get-tuple-element.88), channel_id=1, source_target_pairs={{0,8},{4,12},{8,0},{12,4},{16,24},{20,28},{24,16},{28,20},{1,9},{5... | collective-permute-start | bytes 294920 | tf_op jit(solution)/shard_map/ppermute | solution.py:477
  35.0 6.0 %collective-permute-start.14 = (bf16[4,16,768]{2,1,0:T(8,128)(2,1)S(1)}, bf16[4,16,768]{2,1,0:T(8,128)(2,1)S(1)}, u32[]{:S(2)}, u32[]{:S(2)}) collective-permute-start(bf16[4,16,768]{2,1,0:T(8,128)(2,1)S(1)} %get-tuple-element.89), channel_id=1, source_target_pairs={{0,28},{4,24},{8,20},{12,16},{16,12},{20,8},{24,4},{28,0},{1,29},{... | collective-permute-start | bytes 294920 | tf_op jit(solution)/shard_map/ppermute | solution.py:477
  35.2 7.3 %collective-permute-start.13 = (bf16[4,16,768]{2,1,0:T(8,128)(2,1)S(1)}, bf16[4,16,768]{2,1,0:T(8,128)(2,1)S(1)}, u32[]{:S(2)}, u32[]{:S(2)}) collective-permute-start(bf16[4,16,768]{2,1,0:T(8,128)(2,1)S(1)} %get-tuple-element.90), channel_id=1, source_target_pairs={{0,20},{4,16},{8,28},{12,24},{16,4},{20,0},{24,12},{28,8},{1,21},{... | collective-permute-start | bytes 294920 | tf_op jit(solution)/shard_map/ppermute | solution.py:477
  36.7 6.7 %collective-permute-start.12 = (bf16[4,16,768]{2,1,0:T(8,128)(2,1)S(1)}, bf16[4,16,768]{2,1,0:T(8,128)(2,1)S(1)}, u32[]{:S(2)}, u32[]{:S(2)}) collective-permute-start(bf16[4,16,768]{2,1,0:T(8,128)(2,1)S(1)} %get-tuple-element.91), channel_id=1, source_target_pairs={{0,12},{4,8},{8,4},{12,0},{16,28},{20,24},{24,20},{28,16},{1,13},{... | collective-permute-start | bytes 294920 | tf_op jit(solution)/shard_map/ppermute | solution.py:477
  38.1 5.5 %collective-permute-start.11 = (bf16[4,16,768]{2,1,0:T(8,128)(2,1)S(1)}, bf16[4,16,768]{2,1,0:T(8,128)(2,1)S(1)}, u32[]{:S(2)}, u32[]{:S(2)}) collective-permute-start(bf16[4,16,768]{2,1,0:T(8,128)(2,1)S(1)} %get-tuple-element.92), channel_id=1, source_target_pairs={{0,4},{4,0},{8,12},{12,8},{16,20},{20,16},{24,28},{28,24},{1,5},{5... | collective-permute-start | bytes 294920 | tf_op jit(solution)/shard_map/ppermute | solution.py:477
  41.0 5.9 %collective-permute-start.10 = (bf16[4,16,768]{2,1,0:T(8,128)(2,1)S(1)}, bf16[4,16,768]{2,1,0:T(8,128)(2,1)S(1)}, u32[]{:S(2)}, u32[]{:S(2)}) collective-permute-start(bf16[4,16,768]{2,1,0:T(8,128)(2,1)S(1)} %get-tuple-element.93), channel_id=1, source_target_pairs={{0,24},{4,28},{8,16},{12,20},{16,8},{20,12},{24,0},{28,4},{1,25},{... | collective-permute-start | bytes 294920 | tf_op jit(solution)/shard_map/ppermute | solution.py:477
  42.5 6.4 %collective-permute-start.9 = (bf16[4,16,768]{2,1,0:T(8,128)(2,1)S(1)}, bf16[4,16,768]{2,1,0:T(8,128)(2,1)S(1)}, u32[]{:S(2)}, u32[]{:S(2)}) collective-permute-start(bf16[4,16,768]{2,1,0:T(8,128)(2,1)S(1)} %get-tuple-element.94), channel_id=1, source_target_pairs={{0,16},{4,20},{8,24},{12,28},{16,0},{20,4},{24,8},{28,12},{1,17},{... | collective-permute-start | bytes 294920 | tf_op jit(solution)/shard_map/ppermute | solution.py:477
  43.4 14.4 %collective-permute-start.15 = (bf16[32,3328]{1,0:T(8,128)(2,1)S(1)}, bf16[32,3328]{1,0:T(8,128)(2,1)S(1)}, u32[]{:S(2)}, u32[]{:S(2)}) collective-permute-start(bf16[32,3328]{1,0:T(8,128)(2,1)S(1)} %get-tuple-element.68.picked_ref), channel_id=1, source_target_pairs={{0,4},{4,0},{1,5},{5,1},{2,6},{6,2},{3,7},{7,3},{8,12},{12,8},{9,1... | collective-permute-start | bytes 638984 | tf_op jit(solution)/shard_map/ppermute | solution.py:472
  43.6 14.6 %collective-permute-start.7 = (bf16[64,4096]{1,0:T(8,128)(2,1)S(1)}, bf16[64,4096]{1,0:T(8,128)(2,1)S(1)}, u32[]{:S(2)}, u32[]{:S(2)}) collective-permute-start(bf16[64,4096]{1,0:T(8,128)(2,1)S(1)} %get-tuple-element.64), channel_id=1, source_target_pairs={{0,1},{3,2},{4,5},{7,6},{8,9},{11,10},{12,13},{15,14},{16,17},{19,... | collective-permute-start | bytes 1572872 | tf_op jit(solution)/shard_map/ppermute | solution.py:528
  56.9 17.6 %copy-start.1 = (bf16[8,3072]{1,0:T(8,128)(2,1)S(1)}, bf16[8,3072]{1,0:T(8,128)(2,1)}, u32[]{:S(2)}) copy-start(bf16[8,3072]{1,0:T(8,128)(2,1)} %router_ref.3) | copy-start | bytes 147460
  59.7 5.0 %collective-permute-start.16 = (bf16[2,24,896]{2,1,0:T(8,128)(2,1)S(1)}, bf16[2,24,896]{2,1,0:T(8,128)(2,1)S(1)}, u32[]{:S(2)}, u32[]{:S(2)}) collective-permute-start(bf16[2,24,896]{2,1,0:T(8,128)(2,1)S(1)} %slice.168), channel_id=1, source_target_pairs={{0,1},{1,0},{2,3},{3,2},{4,5},{5,4},{6,7},{7,6},{8,9},{9,8},{10,11... | collective-permute-start | bytes 258056 | tf_op jit(solution)/shard_map/ppermute | solution.py:472
  64.7 5.0 %collective-permute-start.17 = (bf16[24,896]{1,0:T(8,128)(2,1)S(1)}, bf16[24,896]{1,0:T(8,128)(2,1)S(1)}, u32[]{:S(2)}, u32[]{:S(2)}) collective-permute-start(bf16[24,896]{1,0:T(8,128)(2,1)S(1)} %fusion), channel_id=1, source_target_pairs={{0,2},{1,3},{2,0},{3,1},{4,6},{5,7},{6,4},{7,5},{8,10},{9,11},{10,... | collective-permute-start | bytes 129032 | tf_op jit(solution)/shard_map/ppermute | solution.py:472
  69.8 6.0 %collective-permute-start.20 = (bf16[24,896]{1,0:T(8,128)(2,1)S(1)}, bf16[24,896]{1,0:T(8,128)(2,1)S(1)}, u32[]{:S(2)}, u32[]{:S(2)}) collective-permute-start(bf16[24,896]{1,0:T(8,128)(2,1)S(1)} %pad_maximum_fusion.1), channel_id=1, source_target_pairs={{0,24},{8,16},{16,8},{24,0},{1,25},{9,17},{17,9},{25,1},{2,26},{10... | collective-permute-start | bytes 129032 | tf_op jit(solution)/shard_map/ppermute | solution.py:472
  71.9 4.0 %collective-permute-start.19 = (bf16[24,896]{1,0:T(8,128)(2,1)S(1)}, bf16[24,896]{1,0:T(8,128)(2,1)S(1)}, u32[]{:S(2)}, u32[]{:S(2)}) collective-permute-start(bf16[24,896]{1,0:T(8,128)(2,1)S(1)} %pad_maximum_fusion.1), channel_id=1, source_target_pairs={{0,16},{8,24},{16,0},{24,8},{1,17},{9,25},{17,1},{25,9},{2,18},{10... | collective-permute-start | bytes 129032 | tf_op jit(solution)/shard_map/ppermute | solution.py:472
  72.8 4.0 %collective-permute-start.18 = (bf16[24,896]{1,0:T(8,128)(2,1)S(1)}, bf16[24,896]{1,0:T(8,128)(2,1)S(1)}, u32[]{:S(2)}, u32[]{:S(2)}) collective-permute-start(bf16[24,896]{1,0:T(8,128)(2,1)S(1)} %pad_maximum_fusion.1), channel_id=1, source_target_pairs={{0,8},{8,0},{16,24},{24,16},{1,9},{9,1},{17,25},{25,17},{2,10},{10... | collective-permute-start | bytes 129032 | tf_op jit(solution)/shard_map/ppermute | solution.py:472
  73.3 1.2 %collective-permute-start.21 = (f32[32,128]{1,0:T(8,128)S(1)}, f32[32,128]{1,0:T(8,128)S(1)}, u32[]{:S(2)}, u32[]{:S(2)}) collective-permute-start(f32[32,128]{1,0:T(8,128)S(1)} %get-tuple-element.78), channel_id=1, source_target_pairs={{0,4},{4,0},{1,5},{5,1},{2,6},{6,2},{3,7},{7,3},{8,12},{12,8},{9,1... | collective-permute-start | bytes 49160 | tf_op jit(solution)/shard_map/ppermute | solution.py:472
  76.9 1.4 %collective-permute-start.22 = (bf16[72,896]{1,0:T(8,128)(2,1)S(1)}, bf16[72,896]{1,0:T(8,128)(2,1)S(1)}, u32[]{:S(2)}, u32[]{:S(2)}) collective-permute-start(bf16[72,896]{1,0:T(8,128)(2,1)S(1)} %get-tuple-element.99), channel_id=1, source_target_pairs={{0,4},{4,0},{1,5},{5,1},{2,6},{6,2},{3,7},{7,3},{8,12},{12,8},{9,1... | collective-permute-start | bytes 387080 | tf_op jit(solution)/shard_map/ppermute | solution.py:472

commit v7 on v6

--- a/solution.py
+++ b/solution.py
@@ -123,7 +123,7 @@
     for slot, k in enumerate(order):
         lhs[slot * capacity : (slot + 1) * capacity] = rows_ref[k]
     rows = slice(half * capacity, (half + 1) * capacity)
-    tile = 512
+    tile = 256
     for t in range(weight_ref.shape[1] // tile):
         part = slice(t * tile, (t + 1) * tile)
         result = jnp.dot(lhs[...], weight_ref[:, part], preferred_element_type=F32)

time: 80 us -> 80 us (level)
  no operation moved by 1% of the time
where the time goes in v7:
time: 80 us; the launch traced here: 79.8 us
  waiting for transfers between devices  31.9 us (40%)
  starting transfers between devices  27.8 us (35%)
  Pallas kernels  18.7 us (23%)
  between operations  0.91 us (1%)
    ppermute x14, waiting for transfers between devices, swap(): return lax.ppermute(value, axis, xor_pairs(count, bits))  26.3 us
    ppermute x14, starting transfers between devices, swap(): return lax.ppermute(value, axis, xor_pairs(count, bits))  17 us
    ppermute x7, starting transfers between devices, swap_group(): return lax.ppermute(value, ('dp', 'expert'), pairs)  6.84 us
    ppermute x7, waiting for transfers between devices, swap_group(): return lax.ppermute(value, ('dp', 'expert'), pairs)  5.11 us
    pallas_call x1, Pallas kernels, adapter_early(): pl.pallas_call(adapter_kernel, out_shape=(jax.ShapeDtypeStruct((groups, s...  3.47 us
    ppermute x1, starting transfers between devices, direct_device(): outer = lax.ppermute(last, 'shard', [(0, 1), (3, 2)])  3.24 us
    pallas_call x2, Pallas kernels, products(): pl.pallas_call(functools.partial(product_kernel, len(before) // 4), out_s...  3.07 us
    pallas_call x1, Pallas kernels, dequantize(): pl.pallas_call(weight_kernel, out_shape=pltpu.VMEM(codes.shape, BF16), in...  3.05 us
  transfers between devices with their start and end apart: 23, of which 13 were waited for; matrix products, arithmetic and copies ran while one was open for 0% of the time, Pallas kernels for 15%

profile of v7, /device:TPU:0, one launch (start us, length us, event | category | flops | bytes accessed | tf_op | source)
XLA Modules:
  0.0 79.8 jit_solution(8241603714346107563)
XLA Ops:
  0.6 0.1 pad_add_fusion.place
  0.7 2.0 %route.1 = (bf16[4,32,768]{2,1,0:T(8,128)(2,1)S(1)}, f32[32,128]{1,0:T(8,128)S(1)}, f32[16,128]{1,0:T(8,128)S(1)}) custom-call(s32[4]{0:T(128)S(1)} %pad_add_fusion.place, f32[8,128]{1,0:T(8,128)} %bitcast.44, s32[2,128]{1,0:T(2,128)} %bitcast.45, bf16[128,3072]{1,0:T(8,128)(2,1)} %grad_hbm.3), custom_call_target="tpu_custom_call" | custom-call | flops 25165824 | bytes 786432 | tf_op jit(solution)/shard_map/route/pallas_call | solution.py:97
  2.7 5.1 %collective-permute-start.2 = (bf16[32,768]{1,0:T(8,128)(2,1)S(1)}, bf16[32,768]{1,0:T(8,128)(2,1)S(1)}, u32[]{:S(2)}, u32[]{:S(2)}) collective-permute-start(bf16[32,768]{1,0:T(8,128)(2,1)S(1)} %get-tuple-element.96), channel_id=1, source_target_pairs={{0,3},{1,2},{2,1},{3,0},{4,7},{5,6},{6,5},{7,4},{8,11},{9,10},{10,... | collective-permute-start | bytes 147464 | tf_op jit(solution)/shard_map/ppermute | solution.py:472
  7.9 0.0 collective-permute-start.1
  7.9 0.6 collective-permute-start
  8.5 3.1 %dequantize.1.weight_ref = bf16[768,4096]{1,0:T(8,128)(2,1)S(1)} custom-call(bf16[768,4096]{1,0:T(8,128)(2,1)} %codes_hbm.1, bf16[12,4096]{1,0:T(8,128)(2,1)} %scales_hbm.1), custom_call_target="tpu_custom_call" | custom-call | flops 3145728 | bytes 12582912 | tf_op jit(solution)/shard_map/dequantize/pallas_call | solution.py:214
  11.6 0.0 collective-permute-done.2
  11.6 1.3 %collective-permute-done.1 = bf16[32,768]{1,0:T(8,128)(2,1)S(1)} collective-permute-done((bf16[32,768]{1,0:T(8,128)(2,1)S(1)}, bf16[32,768]{1,0:T(8,128)(2,1)S(1)}, u32[]{:S(2)}, u32[]{:S(2)}) %collective-permute-start.1) | collective-permute-done | bytes 49184 | tf_op jit(solution)/shard_map/ppermute | solution.py:472
  12.8 0.0 collective-permute-done
  12.9 0.1 collective-permute-start.3
  13.0 1.5 %products.2 = (bf16[64,4096]{1,0:T(8,128)(2,1)S(1)}, bf16[64,4096]{1,0:T(8,128)(2,1)S(1)}, bf16[64,4096]{1,0:T(8,128)(2,1)S(1)}, f32[64,4096]{1,0:T(8,128)S(1)}) custom-call(s32[4]{0:T(128)S(1)} %pad_add_fusion.place, bf16[4,32,768]{2,1,0:T(8,128)(2,1)S(1)} %pad_maximum_fusion.rows_ref, bf16[768,4096]{1,0:T(8,128)(2,1)S(1)} %dequantize.1.weight_ref), custom_call_target="tpu_custom_call" | custom-call | flops 805306368 | bytes 6291456 | tf_op jit(solution)/shard_map/products/pallas_call | solution.py:138
  14.5 0.0 collective-permute-done.3.rows_ref
  14.5 1.5 %products.3 = (bf16[64,4096]{1,0:T(8,128)(2,1)S(1)}, bf16[64,4096]{1,0:T(8,128)(2,1)S(1)}, bf16[64,4096]{1,0:T(8,128)(2,1)S(1)}, f32[64,4096]{1,0:T(8,128)S(1)}) custom-call(s32[4]{0:T(128)S(1)} %pad_add_fusion.place, ...), custom_call_target="tpu_custom_call", output_to_operand_aliasing={{0}: (3, {}), {1}: (4, {}), {2}: (5, {}), {3}: (6, {})} | custom-call | flops 805306368 | bytes 6291456 | tf_op jit(solution)/shard_map/products/pallas_call | solution.py:138
  16.1 0.7 collective-permute-start.4
  16.8 0.7 collective-permute-start.5
  17.4 3.5 %adapter_early.1 = (f32[8,4,16,768]{3,2,1,0:T(8,128)S(1)}, bf16[32,3328]{1,0:T(8,128)(2,1)S(1)}, f32[64,8]{1,0:T(8,128)S(1)}) custom-call(s32[4]{0:T(128)S(1)} %pad_add_fusion.place, bf16[128,3072]{1,0:T(8,128)(2,1)} %grad_hbm.3, bf16[128,3072]{1,0:T(8,128)(2,1)} %context_hbm.1, bf16[64,3072]{1,0:T(8,128)(2,1)} %down_hbm.1, bf16[64,3072]{1,0:T(8,128)(2,1)} %up_hbm.1, ...), custom_call_target="tpu_custom_call" | custom-call | tf_op jit(solution)/shard_map/adapter_early/pallas_call | solution.py:284
  20.9 9.5 %collective-permute-done.4.near_ref = bf16[64,4096]{1,0:T(8,128)(2,1)S(1)} collective-permute-done((bf16[64,4096]{1,0:T(8,128)(2,1)S(1)}, bf16[64,4096]{1,0:T(8,128)(2,1)S(1)}, u32[]{:S(2)}, u32[]{:S(2)}) %collective-permute-start.4) | collective-permute-done | bytes 524320 | tf_op jit(solution)/shard_map/ppermute | solution.py:472
  30.4 0.7 add_near.1
  31.1 2.1 %collective-permute-start.6 = (bf16[64,4096]{1,0:T(8,128)(2,1)S(1)}, bf16[64,4096]{1,0:T(8,128)(2,1)S(1)}, u32[]{:S(2)}, u32[]{:S(2)}) collective-permute-start(bf16[64,4096]{1,0:T(8,128)(2,1)S(1)} %add_near.1), channel_id=1, source_target_pairs={{0,2},{1,3},{2,0},{3,1},{4,6},{5,7},{6,4},{7,5},{8,10},{9,11},{10,... | collective-permute-start | bytes 1572872 | tf_op jit(solution)/shard_map/ppermute | solution.py:472
  33.2 0.1 convert_element_type.57
  33.3 0.1 slice_bitcast_fusion.6
  33.4 0.0 copy-start
  33.4 1.6 %collective-permute-start.8 = (bf16[4,16,768]{2,1,0:T(8,128)(2,1)S(1)}, bf16[4,16,768]{2,1,0:T(8,128)(2,1)S(1)}, u32[]{:S(2)}, u32[]{:S(2)}) collective-permute-start(bf16[4,16,768]{2,1,0:T(8,128)(2,1)S(1)} %get-tuple-element.88), channel_id=1, source_target_pairs={{0,8},{4,12},{8,0},{12,4},{16,24},{20,28},{24,16},{28,20},{1,9},{5... | collective-permute-start | bytes 294920 | tf_op jit(solution)/shard_map/ppermute | solution.py:477
  35.0 0.3 collective-permute-start.14
  35.2 1.5 %collective-permute-start.13 = (bf16[4,16,768]{2,1,0:T(8,128)(2,1)S(1)}, bf16[4,16,768]{2,1,0:T(8,128)(2,1)S(1)}, u32[]{:S(2)}, u32[]{:S(2)}) collective-permute-start(bf16[4,16,768]{2,1,0:T(8,128)(2,1)S(1)} %get-tuple-element.90), channel_id=1, source_target_pairs={{0,20},{4,16},{8,28},{12,24},{16,4},{20,0},{24,12},{28,8},{1,21},{... | collective-permute-start | bytes 294920 | tf_op jit(solution)/shard_map/ppermute | solution.py:477
  36.7 0.0 collective-permute-done.5.middle_ref
  36.7 1.0 %collective-permute-start.12 = (bf16[4,16,768]{2,1,0:T(8,128)(2,1)S(1)}, bf16[4,16,768]{2,1,0:T(8,128)(2,1)S(1)}, u32[]{:S(2)}, u32[]{:S(2)}) collective-permute-start(bf16[4,16,768]{2,1,0:T(8,128)(2,1)S(1)} %get-tuple-element.91), channel_id=1, source_target_pairs={{0,12},{4,8},{8,4},{12,0},{16,28},{20,24},{24,20},{28,16},{1,13},{... | collective-permute-start | bytes 294920 | tf_op jit(solution)/shard_map/ppermute | solution.py:477
  37.7 0.4 collective-permute-done.8
  38.1 0.2 collective-permute-start.11
  38.3 2.7 %collective-permute-done.14 = bf16[4,16,768]{2,1,0:T(8,128)(2,1)S(1)} collective-permute-done((bf16[4,16,768]{2,1,0:T(8,128)(2,1)S(1)}, bf16[4,16,768]{2,1,0:T(8,128)(2,1)S(1)}, u32[]{:S(2)}, u32[]{:S(2)}) %collective-permute-start.14) | collective-permute-done | bytes 98336 | tf_op jit(solution)/shard_map/ppermute | solution.py:477
  41.0 1.5 %collective-permute-start.10 = (bf16[4,16,768]{2,1,0:T(8,128)(2,1)S(1)}, bf16[4,16,768]{2,1,0:T(8,128)(2,1)S(1)}, u32[]{:S(2)}, u32[]{:S(2)}) collective-permute-start(bf16[4,16,768]{2,1,0:T(8,128)(2,1)S(1)} %get-tuple-element.93), channel_id=1, source_target_pairs={{0,24},{4,28},{8,16},{12,20},{16,8},{20,12},{24,0},{28,4},{1,25},{... | collective-permute-start | bytes 294920 | tf_op jit(solution)/shard_map/ppermute | solution.py:477
  42.5 0.0 collective-permute-done.13
  42.5 0.8 %collective-permute-start.9 = (bf16[4,16,768]{2,1,0:T(8,128)(2,1)S(1)}, bf16[4,16,768]{2,1,0:T(8,128)(2,1)S(1)}, u32[]{:S(2)}, u32[]{:S(2)}) collective-permute-start(bf16[4,16,768]{2,1,0:T(8,128)(2,1)S(1)} %get-tuple-element.94), channel_id=1, source_target_pairs={{0,16},{4,20},{8,24},{12,28},{16,0},{20,4},{24,8},{28,12},{1,17},{... | collective-permute-start | bytes 294920 | tf_op jit(solution)/shard_map/ppermute | solution.py:477
  43.4 0.0 collective-permute-done.12
  43.4 0.3 collective-permute-start.15
  43.6 0.0 collective-permute-done.11
  43.6 3.2 %collective-permute-start.7 = (bf16[64,4096]{1,0:T(8,128)(2,1)S(1)}, bf16[64,4096]{1,0:T(8,128)(2,1)S(1)}, u32[]{:S(2)}, u32[]{:S(2)}) collective-permute-start(bf16[64,4096]{1,0:T(8,128)(2,1)S(1)} %get-tuple-element.64), channel_id=1, source_target_pairs={{0,1},{3,2},{4,5},{7,6},{8,9},{11,10},{12,13},{15,14},{16,17},{19,... | collective-permute-start | bytes 1572872 | tf_op jit(solution)/shard_map/ppermute | solution.py:528
  46.9 0.0 collective-permute-done.10
  46.9 2.0 %collective-permute-done.9 = bf16[4,16,768]{2,1,0:T(8,128)(2,1)S(1)} collective-permute-done((bf16[4,16,768]{2,1,0:T(8,128)(2,1)S(1)}, bf16[4,16,768]{2,1,0:T(8,128)(2,1)S(1)}, u32[]{:S(2)}, u32[]{:S(2)}) %collective-permute-start.9) | collective-permute-done | bytes 98336 | tf_op jit(solution)/shard_map/ppermute | solution.py:477
  48.9 0.1 bitcast_add_fusion
  49.0 7.9 %collective-permute-done.6.far_ref = bf16[64,4096]{1,0:T(8,128)(2,1)S(1)} collective-permute-done((bf16[64,4096]{1,0:T(8,128)(2,1)S(1)}, bf16[64,4096]{1,0:T(8,128)(2,1)S(1)}, u32[]{:S(2)}, u32[]{:S(2)}) %collective-permute-start.6) | collective-permute-done | bytes 524320 | tf_op jit(solution)/shard_map/ppermute | solution.py:472
  56.9 0.8 %add_far.1.partial_ref = f32[64,4096]{1,0:T(8,128)S(1)} custom-call(s32[4]{0:T(128)S(1)} %pad_add_fusion.place, f32[64,4096]{1,0:T(8,128)S(1)} %get-tuple-element.52.own_ref, bf16[64,4096]{1,0:T(8,128)(2,1)S(1)} %collective-permute-done.4.near_ref, bf16[64,4096]{1,0:T(8,128)(2,1)S(1)} %collective-permute-done.5.middle_ref, ...), custom_call_target="tpu_custom_call" | custom-call | flops 3000000000 | bytes 3670016 | tf_op jit(solution)/shard_map/add_far/pallas_call | solution.py:179
  57.7 0.0 collective-permute-done.15.other_ref
  57.7 0.5 collective-permute-done.7.outer_ref
  58.2 0.0 copy-done
  58.2 1.4 %finish.1 = (f32[64,4096]{1,0:T(8,128)S(1)}, f32[32,128]{1,0:T(8,128)S(1)}, f32[32,128]{1,0:T(8,128)S(1)}, f32[4,8,896]{2,1,0:T(8,128)S(1)}) custom-call(s32[4]{0:T(128)S(1)} %pad_add_fusion.place, f32[64,4096]{1,0:T(8,128)S(1)} %add_far.1.partial_ref, bf16[64,4096]{1,0:T(8,128)(2,1)S(1)} %collective-permute-done.7.outer_ref, bf16[64,4096]{1,0:T(8,128)(2,1)S(1)} %bitcast.38, ...), custom_call_target="tpu_custom_call" | custom-call | flops 2097152 | bytes 2621440 | tf_op jit(solution)/shard_map/finish/pallas_call | solution.py:381
  59.7 2.5 %collective-permute-start.16 = (bf16[2,24,896]{2,1,0:T(8,128)(2,1)S(1)}, bf16[2,24,896]{2,1,0:T(8,128)(2,1)S(1)}, u32[]{:S(2)}, u32[]{:S(2)}) collective-permute-start(bf16[2,24,896]{2,1,0:T(8,128)(2,1)S(1)} %slice.168), channel_id=1, source_target_pairs={{0,1},{1,0},{2,3},{3,2},{4,5},{5,4},{6,7},{7,6},{8,9},{9,8},{10,11... | collective-permute-start | bytes 258056 | tf_op jit(solution)/shard_map/ppermute | solution.py:472
  62.2 1.4 %hidden_gradient.1 = bf16[64,4096]{1,0:T(8,128)(2,1)} custom-call(s32[4]{0:T(128)S(1)} %pad_add_fusion.place, f32[64,4096]{1,0:T(8,128)S(1)} %get-tuple-element.74.product_ref, bf16[32,3328]{1,0:T(8,128)(2,1)S(1)} %get-tuple-element.68.picked_ref, bf16[32,3328]{1,0:T(8,128)(2,1)S(1)} %collective-permute-done.15.other_ref), custom_call_target="tpu_custom_call" | custom-call | tf_op jit(solution)/shard_map/hidden_gradient/pallas_call | solution.py:365
  63.7 1.0 %collective-permute-done.16 = bf16[2,24,896]{2,1,0:T(8,128)(2,1)S(1)} collective-permute-done((bf16[2,24,896]{2,1,0:T(8,128)(2,1)S(1)}, bf16[2,24,896]{2,1,0:T(8,128)(2,1)S(1)}, u32[]{:S(2)}, u32[]{:S(2)}) %collective-permute-start.16) | collective-permute-done | bytes 86048 | tf_op jit(solution)/shard_map/ppermute | solution.py:472
  64.7 2.0 %collective-permute-start.17 = (bf16[24,896]{1,0:T(8,128)(2,1)S(1)}, bf16[24,896]{1,0:T(8,128)(2,1)S(1)}, u32[]{:S(2)}, u32[]{:S(2)}) collective-permute-start(bf16[24,896]{1,0:T(8,128)(2,1)S(1)} %fusion), channel_id=1, source_target_pairs={{0,2},{1,3},{2,0},{3,1},{4,6},{5,7},{6,4},{7,5},{8,10},{9,11},{10,... | collective-permute-start | bytes 129032 | tf_op jit(solution)/shard_map/ppermute | solution.py:472
  66.7 3.0 %collective-permute-done.17 = bf16[24,896]{1,0:T(8,128)(2,1)S(1)} collective-permute-done((bf16[24,896]{1,0:T(8,128)(2,1)S(1)}, bf16[24,896]{1,0:T(8,128)(2,1)S(1)}, u32[]{:S(2)}, u32[]{:S(2)}) %collective-permute-start.17) | collective-permute-done | bytes 43040 | tf_op jit(solution)/shard_map/ppermute | solution.py:472
  69.8 2.1 %collective-permute-start.20 = (bf16[24,896]{1,0:T(8,128)(2,1)S(1)}, bf16[24,896]{1,0:T(8,128)(2,1)S(1)}, u32[]{:S(2)}, u32[]{:S(2)}) collective-permute-start(bf16[24,896]{1,0:T(8,128)(2,1)S(1)} %pad_maximum_fusion.1), channel_id=1, source_target_pairs={{0,24},{8,16},{16,8},{24,0},{1,25},{9,17},{17,9},{25,1},{2,26},{10... | collective-permute-start | bytes 129032 | tf_op jit(solution)/shard_map/ppermute | solution.py:472
  71.9 0.9 %collective-permute-start.19 = (bf16[24,896]{1,0:T(8,128)(2,1)S(1)}, bf16[24,896]{1,0:T(8,128)(2,1)S(1)}, u32[]{:S(2)}, u32[]{:S(2)}) collective-permute-start(bf16[24,896]{1,0:T(8,128)(2,1)S(1)} %pad_maximum_fusion.1), channel_id=1, source_target_pairs={{0,16},{8,24},{16,0},{24,8},{1,17},{9,25},{17,1},{25,9},{2,18},{10... | collective-permute-start | bytes 129032 | tf_op jit(solution)/shard_map/ppermute | solution.py:472
  72.8 0.5 collective-permute-start.18
  73.3 0.0 collective-permute-start.21
  73.3 1.2 %collective-permute-done.21.prob_got_ref = f32[32,128]{1,0:T(8,128)S(1)} collective-permute-done((f32[32,128]{1,0:T(8,128)S(1)}, f32[32,128]{1,0:T(8,128)S(1)}, u32[]{:S(2)}, u32[]{:S(2)}) %collective-permute-start.21) | collective-permute-done | bytes 16416 | tf_op jit(solution)/shard_map/ppermute | solution.py:472
  74.5 0.0 copy-done.1
  74.5 1.2 %token_gradient.1 = bf16[128,3072]{1,0:T(8,128)(2,1)} custom-call(f32[32,128]{1,0:T(8,128)S(1)} %get-tuple-element.77.prob_ref, f32[32,128]{1,0:T(8,128)S(1)} %collective-permute-done.21.prob_got_ref, f32[32,128]{1,0:T(8,128)S(1)} %get-tuple-element.57.slots_ref, f32[16,128]{1,0:T(8,128)S(1)} %get-tuple-element.58.info_ref, bf16[8,3072]{1,0:T(8,128)(2,1)S(1)} %copy-done.1), custom_call_target="tpu_custom_call" | custom-call | flops 6291456 | bytes 786432 | tf_op jit(solution)/shard_map/token_gradient/pallas_call | solution.py:418
  75.8 0.0 collective-permute-done.20
  75.8 0.1 collective-permute-done.19
  75.9 0.9 %collective-permute-done.18 = bf16[24,896]{1,0:T(8,128)(2,1)S(1)} collective-permute-done((bf16[24,896]{1,0:T(8,128)(2,1)S(1)}, bf16[24,896]{1,0:T(8,128)(2,1)S(1)}, u32[]{:S(2)}, u32[]{:S(2)}) %collective-permute-start.18) | collective-permute-done | bytes 43040 | tf_op jit(solution)/shard_map/ppermute | solution.py:472
  76.9 0.1 collective-permute-start.22
  77.0 1.3 %collective-permute-done.22 = bf16[72,896]{1,0:T(8,128)(2,1)S(1)} collective-permute-done((bf16[72,896]{1,0:T(8,128)(2,1)S(1)}, bf16[72,896]{1,0:T(8,128)(2,1)S(1)}, u32[]{:S(2)}, u32[]{:S(2)}) %collective-permute-start.22) | collective-permute-done | bytes 129056 | tf_op jit(solution)/shard_map/ppermute | solution.py:472
  78.4 1.5 %adapter_late.1 = (f32[64,768]{1,0:T(8,128)}, f32[64,768]{1,0:T(8,128)}) custom-call(s32[4]{0:T(128)S(1)} %pad_add_fusion.place, bf16[8,16,896]{2,1,0:T(8,128)(2,1)S(1)} %bitcast.39, f32[8,896]{1,0:T(8,128)S(1)} %convert_add_fusion.late_ref, f32[64,8]{1,0:T(8,128)S(1)} %get-tuple-element.83.mixed_ref, bf16[8,3072]{1,0:T(8,128)(2,1)S(1)} %copy-done.1), custom_call_target="tpu_custom_call" | custom-call | flops 7340032 | bytes 917504 | tf_op jit(solution)/shard_map/adapter_late/pallas_call | solution.py:459
  (18 shorter events, 0.2 us)
Async XLA Ops:
  2.7 8.8 %collective-permute-start.2 = (bf16[32,768]{1,0:T(8,128)(2,1)S(1)}, bf16[32,768]{1,0:T(8,128)(2,1)S(1)}, u32[]{:S(2)}, u32[]{:S(2)}) collective-permute-start(bf16[32,768]{1,0:T(8,128)(2,1)S(1)} %get-tuple-element.96), channel_id=1, source_target_pairs={{0,3},{1,2},{2,1},{3,0},{4,7},{5,6},{6,5},{7,4},{8,11},{9,10},{10,... | collective-permute-start | bytes 147464 | tf_op jit(solution)/shard_map/ppermute | solution.py:472
  7.9 5.0 %collective-permute-start.1 = (bf16[32,768]{1,0:T(8,128)(2,1)S(1)}, bf16[32,768]{1,0:T(8,128)(2,1)S(1)}, u32[]{:S(2)}, u32[]{:S(2)}) collective-permute-start(bf16[32,768]{1,0:T(8,128)(2,1)S(1)} %get-tuple-element.97), channel_id=1, source_target_pairs={{0,2},{1,3},{2,0},{3,1},{4,6},{5,7},{6,4},{7,5},{8,10},{9,11},{10,... | collective-permute-start | bytes 147464 | tf_op jit(solution)/shard_map/ppermute | solution.py:472
  7.9 5.0 %collective-permute-start = (bf16[32,768]{1,0:T(8,128)(2,1)S(1)}, bf16[32,768]{1,0:T(8,128)(2,1)S(1)}, u32[]{:S(2)}, u32[]{:S(2)}) collective-permute-start(bf16[32,768]{1,0:T(8,128)(2,1)S(1)} %get-tuple-element.98), channel_id=1, source_target_pairs={{0,1},{1,0},{2,3},{3,2},{4,5},{5,4},{6,7},{7,6},{8,9},{9,8},{10,11... | collective-permute-start | bytes 147464 | tf_op jit(solution)/shard_map/ppermute | solution.py:472
  12.9 1.6 %collective-permute-start.3 = (bf16[4,32,768]{2,1,0:T(8,128)(2,1)S(1)}, bf16[4,32,768]{2,1,0:T(8,128)(2,1)S(1)}, u32[]{:S(2)}, u32[]{:S(2)}) collective-permute-start(bf16[4,32,768]{2,1,0:T(8,128)(2,1)S(1)} %pad_maximum_fusion.rows_ref), channel_id=1, source_target_pairs={{0,4},{4,0},{1,5},{5,1},{2,6},{6,2},{3,7},{7,3},{8,12},{12,8},{9,1... | collective-permute-start | bytes 589832 | tf_op jit(solution)/shard_map/ppermute | solution.py:472
  16.1 14.4 %collective-permute-start.4 = (bf16[64,4096]{1,0:T(8,128)(2,1)S(1)}, bf16[64,4096]{1,0:T(8,128)(2,1)S(1)}, u32[]{:S(2)}, u32[]{:S(2)}) collective-permute-start(bf16[64,4096]{1,0:T(8,128)(2,1)S(1)} %get-tuple-element.54), channel_id=1, source_target_pairs={{0,1},{1,0},{2,3},{3,2},{4,5},{5,4},{6,7},{7,6},{8,9},{9,8},{10,11... | collective-permute-start | bytes 1572872 | tf_op jit(solution)/shard_map/ppermute | solution.py:472
  16.8 19.9 %collective-permute-start.5 = (bf16[64,4096]{1,0:T(8,128)(2,1)S(1)}, bf16[64,4096]{1,0:T(8,128)(2,1)S(1)}, u32[]{:S(2)}, u32[]{:S(2)}) collective-permute-start(bf16[64,4096]{1,0:T(8,128)(2,1)S(1)} %get-tuple-element.64), channel_id=1, source_target_pairs={{1,2},{2,1},{5,6},{6,5},{9,10},{10,9},{13,14},{14,13},{17,18},{18,... | collective-permute-start | bytes 1572872 | tf_op jit(solution)/shard_map/ppermute | solution.py:519
  31.1 25.7 %collective-permute-start.6 = (bf16[64,4096]{1,0:T(8,128)(2,1)S(1)}, bf16[64,4096]{1,0:T(8,128)(2,1)S(1)}, u32[]{:S(2)}, u32[]{:S(2)}) collective-permute-start(bf16[64,4096]{1,0:T(8,128)(2,1)S(1)} %add_near.1), channel_id=1, source_target_pairs={{0,2},{1,3},{2,0},{3,1},{4,6},{5,7},{6,4},{7,5},{8,10},{9,11},{10,... | collective-permute-start | bytes 1572872 | tf_op jit(solution)/shard_map/ppermute | solution.py:472
  33.4 24.8 %copy-start = (bf16[1,1,64,4096]{3,2,1,0:T(8,128)(2,1)S(1)}, bf16[1,1,64,4096]{3,2,1,0:T(8,128)(2,1)}, u32[]{:S(2)}) copy-start(bf16[1,1,64,4096]{3,2,1,0:T(8,128)(2,1)} %param.16) | copy-start | bytes 1572868
  33.4 4.7 %collective-permute-start.8 = (bf16[4,16,768]{2,1,0:T(8,128)(2,1)S(1)}, bf16[4,16,768]{2,1,0:T(8,128)(2,1)S(1)}, u32[]{:S(2)}, u32[]{:S(2)}) collective-permute-start(bf16[4,16,768]{2,1,0:T(8,128)(2,1)S(1)} %get-tuple-element.88), channel_id=1, source_target_pairs={{0,8},{4,12},{8,0},{12,4},{16,24},{20,28},{24,16},{28,20},{1,9},{5... | collective-permute-start | bytes 294920 | tf_op jit(solution)/shard_map/ppermute | solution.py:477
  35.0 6.0 %collective-permute-start.14 = (bf16[4,16,768]{2,1,0:T(8,128)(2,1)S(1)}, bf16[4,16,768]{2,1,0:T(8,128)(2,1)S(1)}, u32[]{:S(2)}, u32[]{:S(2)}) collective-permute-start(bf16[4,16,768]{2,1,0:T(8,128)(2,1)S(1)} %get-tuple-element.89), channel_id=1, source_target_pairs={{0,28},{4,24},{8,20},{12,16},{16,12},{20,8},{24,4},{28,0},{1,29},{... | collective-permute-start | bytes 294920 | tf_op jit(solution)/shard_map/ppermute | solution.py:477
  35.2 7.3 %collective-permute-start.13 = (bf16[4,16,768]{2,1,0:T(8,128)(2,1)S(1)}, bf16[4,16,768]{2,1,0:T(8,128)(2,1)S(1)}, u32[]{:S(2)}, u32[]{:S(2)}) collective-permute-start(bf16[4,16,768]{2,1,0:T(8,128)(2,1)S(1)} %get-tuple-element.90), channel_id=1, source_target_pairs={{0,20},{4,16},{8,28},{12,24},{16,4},{20,0},{24,12},{28,8},{1,21},{... | collective-permute-start | bytes 294920 | tf_op jit(solution)/shard_map/ppermute | solution.py:477
  36.7 6.7 %collective-permute-start.12 = (bf16[4,16,768]{2,1,0:T(8,128)(2,1)S(1)}, bf16[4,16,768]{2,1,0:T(8,128)(2,1)S(1)}, u32[]{:S(2)}, u32[]{:S(2)}) collective-permute-start(bf16[4,16,768]{2,1,0:T(8,128)(2,1)S(1)} %get-tuple-element.91), channel_id=1, source_target_pairs={{0,12},{4,8},{8,4},{12,0},{16,28},{20,24},{24,20},{28,16},{1,13},{... | collective-permute-start | bytes 294920 | tf_op jit(solution)/shard_map/ppermute | solution.py:477
  38.1 5.5 %collective-permute-start.11 = (bf16[4,16,768]{2,1,0:T(8,128)(2,1)S(1)}, bf16[4,16,768]{2,1,0:T(8,128)(2,1)S(1)}, u32[]{:S(2)}, u32[]{:S(2)}) collective-permute-start(bf16[4,16,768]{2,1,0:T(8,128)(2,1)S(1)} %get-tuple-element.92), channel_id=1, source_target_pairs={{0,4},{4,0},{8,12},{12,8},{16,20},{20,16},{24,28},{28,24},{1,5},{5... | collective-permute-start | bytes 294920 | tf_op jit(solution)/shard_map/ppermute | solution.py:477
  41.0 5.9 %collective-permute-start.10 = (bf16[4,16,768]{2,1,0:T(8,128)(2,1)S(1)}, bf16[4,16,768]{2,1,0:T(8,128)(2,1)S(1)}, u32[]{:S(2)}, u32[]{:S(2)}) collective-permute-start(bf16[4,16,768]{2,1,0:T(8,128)(2,1)S(1)} %get-tuple-element.93), channel_id=1, source_target_pairs={{0,24},{4,28},{8,16},{12,20},{16,8},{20,12},{24,0},{28,4},{1,25},{... | collective-permute-start | bytes 294920 | tf_op jit(solution)/shard_map/ppermute | solution.py:477
  42.5 6.4 %collective-permute-start.9 = (bf16[4,16,768]{2,1,0:T(8,128)(2,1)S(1)}, bf16[4,16,768]{2,1,0:T(8,128)(2,1)S(1)}, u32[]{:S(2)}, u32[]{:S(2)}) collective-permute-start(bf16[4,16,768]{2,1,0:T(8,128)(2,1)S(1)} %get-tuple-element.94), channel_id=1, source_target_pairs={{0,16},{4,20},{8,24},{12,28},{16,0},{20,4},{24,8},{28,12},{1,17},{... | collective-permute-start | bytes 294920 | tf_op jit(solution)/shard_map/ppermute | solution.py:477
  43.4 14.4 %collective-permute-start.15 = (bf16[32,3328]{1,0:T(8,128)(2,1)S(1)}, bf16[32,3328]{1,0:T(8,128)(2,1)S(1)}, u32[]{:S(2)}, u32[]{:S(2)}) collective-permute-start(bf16[32,3328]{1,0:T(8,128)(2,1)S(1)} %get-tuple-element.68.picked_ref), channel_id=1, source_target_pairs={{0,4},{4,0},{1,5},{5,1},{2,6},{6,2},{3,7},{7,3},{8,12},{12,8},{9,1... | collective-permute-start | bytes 638984 | tf_op jit(solution)/shard_map/ppermute | solution.py:472
  43.6 14.6 %collective-permute-start.7 = (bf16[64,4096]{1,0:T(8,128)(2,1)S(1)}, bf16[64,4096]{1,0:T(8,128)(2,1)S(1)}, u32[]{:S(2)}, u32[]{:S(2)}) collective-permute-start(bf16[64,4096]{1,0:T(8,128)(2,1)S(1)} %get-tuple-element.64), channel_id=1, source_target_pairs={{0,1},{3,2},{4,5},{7,6},{8,9},{11,10},{12,13},{15,14},{16,17},{19,... | collective-permute-start | bytes 1572872 | tf_op jit(solution)/shard_map/ppermute | solution.py:528
  56.9 17.6 %copy-start.1 = (bf16[8,3072]{1,0:T(8,128)(2,1)S(1)}, bf16[8,3072]{1,0:T(8,128)(2,1)}, u32[]{:S(2)}) copy-start(bf16[8,3072]{1,0:T(8,128)(2,1)} %router_ref.3) | copy-start | bytes 147460
  59.7 5.0 %collective-permute-start.16 = (bf16[2,24,896]{2,1,0:T(8,128)(2,1)S(1)}, bf16[2,24,896]{2,1,0:T(8,128)(2,1)S(1)}, u32[]{:S(2)}, u32[]{:S(2)}) collective-permute-start(bf16[2,24,896]{2,1,0:T(8,128)(2,1)S(1)} %slice.168), channel_id=1, source_target_pairs={{0,1},{1,0},{2,3},{3,2},{4,5},{5,4},{6,7},{7,6},{8,9},{9,8},{10,11... | collective-permute-start | bytes 258056 | tf_op jit(solution)/shard_map/ppermute | solution.py:472
  64.7 5.0 %collective-permute-start.17 = (bf16[24,896]{1,0:T(8,128)(2,1)S(1)}, bf16[24,896]{1,0:T(8,128)(2,1)S(1)}, u32[]{:S(2)}, u32[]{:S(2)}) collective-permute-start(bf16[24,896]{1,0:T(8,128)(2,1)S(1)} %fusion), channel_id=1, source_target_pairs={{0,2},{1,3},{2,0},{3,1},{4,6},{5,7},{6,4},{7,5},{8,10},{9,11},{10,... | collective-permute-start | bytes 129032 | tf_op jit(solution)/shard_map/ppermute | solution.py:472
  69.8 6.0 %collective-permute-start.20 = (bf16[24,896]{1,0:T(8,128)(2,1)S(1)}, bf16[24,896]{1,0:T(8,128)(2,1)S(1)}, u32[]{:S(2)}, u32[]{:S(2)}) collective-permute-start(bf16[24,896]{1,0:T(8,128)(2,1)S(1)} %pad_maximum_fusion.1), channel_id=1, source_target_pairs={{0,24},{8,16},{16,8},{24,0},{1,25},{9,17},{17,9},{25,1},{2,26},{10... | collective-permute-start | bytes 129032 | tf_op jit(solution)/shard_map/ppermute | solution.py:472
  71.9 4.0 %collective-permute-start.19 = (bf16[24,896]{1,0:T(8,128)(2,1)S(1)}, bf16[24,896]{1,0:T(8,128)(2,1)S(1)}, u32[]{:S(2)}, u32[]{:S(2)}) collective-permute-start(bf16[24,896]{1,0:T(8,128)(2,1)S(1)} %pad_maximum_fusion.1), channel_id=1, source_target_pairs={{0,16},{8,24},{16,0},{24,8},{1,17},{9,25},{17,1},{25,9},{2,18},{10... | collective-permute-start | bytes 129032 | tf_op jit(solution)/shard_map/ppermute | solution.py:472
  72.8 4.0 %collective-permute-start.18 = (bf16[24,896]{1,0:T(8,128)(2,1)S(1)}, bf16[24,896]{1,0:T(8,128)(2,1)S(1)}, u32[]{:S(2)}, u32[]{:S(2)}) collective-permute-start(bf16[24,896]{1,0:T(8,128)(2,1)S(1)} %pad_maximum_fusion.1), channel_id=1, source_target_pairs={{0,8},{8,0},{16,24},{24,16},{1,9},{9,1},{17,25},{25,17},{2,10},{10... | collective-permute-start | bytes 129032 | tf_op jit(solution)/shard_map/ppermute | solution.py:472
  73.3 1.2 %collective-permute-start.21 = (f32[32,128]{1,0:T(8,128)S(1)}, f32[32,128]{1,0:T(8,128)S(1)}, u32[]{:S(2)}, u32[]{:S(2)}) collective-permute-start(f32[32,128]{1,0:T(8,128)S(1)} %get-tuple-element.78), channel_id=1, source_target_pairs={{0,4},{4,0},{1,5},{5,1},{2,6},{6,2},{3,7},{7,3},{8,12},{12,8},{9,1... | collective-permute-start | bytes 49160 | tf_op jit(solution)/shard_map/ppermute | solution.py:472
  76.9 1.4 %collective-permute-start.22 = (bf16[72,896]{1,0:T(8,128)(2,1)S(1)}, bf16[72,896]{1,0:T(8,128)(2,1)S(1)}, u32[]{:S(2)}, u32[]{:S(2)}) collective-permute-start(bf16[72,896]{1,0:T(8,128)(2,1)S(1)} %get-tuple-element.99), channel_id=1, source_target_pairs={{0,4},{4,0},{1,5},{5,1},{2,6},{6,2},{3,7},{7,3},{8,12},{12,8},{9,1... | collective-permute-start | bytes 387080 | tf_op jit(solution)/shard_map/ppermute | solution.py:472
